TPU v7x, 32 devices: a whole 2x2x4 slice. The times are simulated.
32 devices in a mesh: group: 4 (over y, x), dev: 8 (over z, core).
Axes of the slice: x: 2, y: 2, z: 4, core: 2. Of those that a mesh axis runs over, the one named last changes fastest.
Arguments:
- right_side: float32 [16, 131072], P(None, ('group', 'dev')), may hold values from -6 to 6
- nugget: float32 [131072], P(('group', 'dev')), may hold values from 3 to 6
- near_blocks: bfloat16 [1024, 4, 128, 128], P(('group', 'dev')), as said below
- near_list: int32 [1024, 4], P(('group', 'dev')), may hold values from 0 to 1023, as said below
- basis: bfloat16 [1024, 64, 128], P(('group', 'dev')), may hold values from -0.5 to 0.5
- transfer: bfloat16 [1024, 4096], P(('group', 'dev')), may hold values from -0.25 to 0.25
- coupling: bfloat16 [128, 16, 4096], P(('group', 'dev')), as said below
- top_list: int32 [128, 16], P(('group', 'dev')), may hold values from 0 to 127, as said below
Outputs:
- solution_field: float32 [16, 131072], P(None, ('group', 'dev'))
- residual: float32 [16, 131072], P(None, ('group', 'dev'))
Inputs may be any that keep to these rules, and one draw needn't show every extreme that they name: If near_list[i, k] = j then near_list[j, k] = i. Each entry names a leaf of the same subtree (256 leaves a subtree) at most 4 leaves away, or the leaf itself; column 0 names a leaf exactly 4 away wherever that leaf lies in the subtree. If near_list[i, k] = j then near_blocks[j, k] is near_blocks[i, k] transposed; a block of a leaf that names itself is symmetric. If top_list[c, k] = d then top_list[d, k] = c, and d differs from c. If top_list[c, k] = d then coupling[d, k] is coupling[c, k] transposed as a 64 x 64 matrix.
All inputs are finite; a program needn't handle non-finite values.
Results may differ from a plain program's by a relative error of at most 0.008.
Values may be sent and summed in bfloat16 or wider, within the bound.
No kernel may reach another device: no remote copies, remote signals or barrier semaphores. Data moves between devices by JAX's collectives and lax.ppermute only.
A program may use at most 64 MiB of HBM per device.

v0:
```python
import jax
import jax.numpy as jnp
from jax import lax
from jax.sharding import PartitionSpec as P

LEAF_CL = 8
TOPK = 16
HALO = 4
ITERS = 2


def padded(cells, sides, width):
    for axis, dim in sides:
        count = lax.axis_size(axis)
        ends = count - 1
        head = lax.slice_in_dim(cells, 0, width, axis=dim)
        tail = lax.slice_in_dim(cells, cells.shape[dim] - width, cells.shape[dim], axis=dim)
        cells = jnp.concatenate(
            [
                lax.ppermute(tail, axis, [(i, (i + 1) % count) for i in range(ends)]),
                cells,
                lax.ppermute(head, axis, [((i + 1) % count, i) for i in range(ends)]),
            ],
            axis=dim,
        )
    return cells


def operate(field, nugget, near_blocks, near_list, basis, transfer, coupling, top_list):
    rhs_count, width = field.shape
    leaf_dev = near_list.shape[0]
    leaf_size = basis.shape[2]
    rank_size = basis.shape[1]
    cl_dev = coupling.shape[0]
    vb = field.astype(jnp.bfloat16).reshape(rhs_count, leaf_dev, leaf_size)
    extended = padded(vb, (("dev", 1),), HALO)
    first_leaf = (lax.axis_index("group") * lax.axis_size("dev") + lax.axis_index("dev")) * leaf_dev
    local_ids = near_list - first_leaf + HALO
    values = jnp.take(extended, local_ids, axis=1)
    near = jnp.einsum("lkpq,rlkq->rlp", near_blocks, values, preferred_element_type=jnp.float32)
    coef = jnp.einsum("lap,rlp->lar", basis, vb, preferred_element_type=jnp.float32).astype(
        jnp.bfloat16
    )
    emat = transfer.reshape(leaf_dev, rank_size, rank_size)
    upward = jnp.einsum("lab,lar->lbr", emat, coef, preferred_element_type=jnp.float32)
    upward = upward.reshape(cl_dev, LEAF_CL, rank_size, rhs_count).sum(axis=1).astype(jnp.bfloat16)
    upward = upward.reshape(cl_dev, rank_size * rhs_count)
    gathered = lax.all_gather(upward, ("group", "dev"), axis=0, tiled=True)
    picked = jnp.take(gathered, top_list, axis=0).reshape(cl_dev, TOPK, rank_size, rhs_count)
    smat = coupling.reshape(cl_dev, TOPK, rank_size, rank_size)
    down = jnp.einsum("ckab,ckbr->car", smat, picked, preferred_element_type=jnp.float32).astype(
        jnp.bfloat16
    )
    spread = jnp.repeat(down, LEAF_CL, axis=0)
    local_coef = jnp.einsum(
        "lab,lbr->lar", emat, spread, preferred_element_type=jnp.float32
    ).astype(jnp.bfloat16)
    far = jnp.einsum("lap,lar->rlp", basis, local_coef, preferred_element_type=jnp.float32)
    return nugget[None, :] * field + (near + far).reshape(rhs_count, width)


def squares(residual):
    return lax.psum(jnp.sum(residual * residual, axis=1), ("group", "dev"))


def per_device(right_side, nugget, near_blocks, near_list, basis, transfer, coupling, top_list):
    solution_field = jnp.zeros_like(right_side)
    residual = right_side
    direction = right_side
    norm_now = squares(residual)
    for step in range(ITERS):
        image = operate(
            direction, nugget, near_blocks, near_list, basis, transfer, coupling, top_list
        )
        curve = lax.psum(jnp.sum(direction * image, axis=1), ("group", "dev"))
        alpha = norm_now / curve
        solution_field = solution_field + alpha[:, None] * direction
        residual = residual - alpha[:, None] * image
        norm_next = squares(residual)
        direction = residual + (norm_next / norm_now)[:, None] * direction
        norm_now = norm_next
    return (solution_field, residual)


def solution(mesh):
    placed = (
        P(None, ("group", "dev")),
        P(("group", "dev")),
        P(("group", "dev"), None, None, None),
        P(("group", "dev"), None),
        P(("group", "dev"), None, None),
        P(("group", "dev"), None),
        P(("group", "dev"), None, None),
        P(("group", "dev"), None),
    )
    return jax.shard_map(
        per_device,
        mesh=mesh,
        in_specs=placed,
        out_specs=(P(None, ("group", "dev")), P(None, ("group", "dev"))),
        check_vma=False,
    )
```

profile of v0, /device:TPU:0, one launch (start us, length us, event | category | flops | bytes accessed | tf_op | source)
XLA Modules:
  0.0 246.2 jit_solution(16975253267556010789)
XLA Ops:
  0.6 1.0 copy_bitcast_fusion.1
  1.7 0.6 fusion.19
  2.3 2.9 %collective-permute-start = (bf16[16,4,128]{2,0,1:T(8,128)(2,1)}, bf16[16,4,128]{2,0,1:T(8,128)(2,1)}, u32[]{:S(2)}, u32[]{:S(2)}) collective-permute-start(bf16[16,4,128]{2,0,1:T(8,128)(2,1)} %get-tuple-element.14), channel_id=1, source_target_pairs={{0,1},{1,2},{2,3},{3,4},{4,5},{5,6},{6,7},{8,9},{9,10},{10,11},{11... | collective-permute-start | bytes 49160 | tf_op jit(solution)/shard_map/ppermute | solution.py:20
  5.2 1.3 collective-permute-start.1
  6.5 0.7 compare_select_fusion
  7.2 0.7 compare_and_fusion
  7.9 1.2 compare_and_fusion.1
  9.1 0.1 copy.48
  9.2 0.6 reshape.120
  9.8 1.5 reshape.63
  11.3 1.5 bitcast_reduce_fusion.1
  12.8 0.1 copy.50
  12.9 0.1 reshape.114
  13.0 45.6 %all-gather = bf16[32,4,1024]{2,1,0:T(4,128)(2,1)S(1)} all-gather(bf16[1,4,1024]{2,1,0:T(4,128)(2,1)S(1)} %reshape.114), channel_id=1, replica_groups=mesh['group'=4,'dev'=8] {'group','dev'}, dimensions={0}, use_global_device_ids=true | all-gather | bytes 270336 | tf_op jit(solution)/shard_map/all_gather | solution.py:48
  58.7 0.1 reshape.124
  58.8 0.7 gather_fusion.1
  59.5 0.1 broadcast_select_fusion.1
  59.6 0.8 reshape.65
  60.4 2.1 reshape.66
  62.5 1.1 fusion.7
  63.6 0.6 pad_clamp_fusion.1
  64.3 0.7 copy.44
  65.0 0.8 pad_maximum_fusion
  65.8 0.7 gather_fusion
  66.5 3.4 %convolution_bitcast_fusion.1 = f32[32,16,128]{2,1,0:T(8,128)S(1)} fusion(bf16[32,4,128,128]{3,2,1,0:T(8,128)(2,1)} %param.14, bf16[32,4,16,128]{3,2,1,0:T(8,128)(2,1)S(1)} %bitcast.117, pred[32,4]{1,0:T(8,128)(4,1)S(1)} %copy.44), kind=kOutput, calls=%fused_computation.9 | convolution fusion | flops 67371008 | bytes 4980864 | tf_op jit(solution)/shard_map/lkpq,rlkq->rlp/dot_general | solution.py:40
  70.0 0.5 fusion.1
  70.5 0.2 multiply_reduce_fusion.2
  70.7 36.9 %all-reduce = (f32[16]{0:T(128)S(1)}, f32[16]{0:T(128)S(1)}) all-reduce(f32[16]{0:T(128)S(1)} %get-tuple-element.5, f32[16]{0:T(128)S(1)} %get-tuple-element.4), channel_id=1, replica_groups=mesh['group'=4,'dev'=8] {'group','dev'}, use_global_device_ids=true, to_apply=%region_1.0 | all-reduce | flops 32 | bytes 256 | tf_op jit(solution)/shard_map/psum | solution.py:63
  107.6 0.2 multiply_reduce_fusion.1
  107.8 41.4 %psum.30 = f32[16]{0:T(128)S(1)} all-reduce(f32[16]{0:T(128)S(1)} %multiply_reduce_fusion.1), channel_id=1, replica_groups=mesh['group'=4,'dev'=8] {'group','dev'}, use_global_device_ids=true, to_apply=%region_6.9 | all-reduce | flops 16 | bytes 128 | tf_op jit(solution)/shard_map/psum | solution.py:63
  149.2 0.5 copy-done.12
  149.7 0.6 bitcast_reduce_fusion
  150.3 0.1 copy_bitcast_fusion
  150.4 0.1 copy.59
  150.5 0.1 reshape.116
  150.7 41.6 %all-gather.1 = bf16[32,4,1024]{2,1,0:T(4,128)(2,1)S(1)} all-gather(bf16[1,4,1024]{2,1,0:T(4,128)(2,1)S(1)} %reshape.116), channel_id=1, replica_groups=mesh['group'=4,'dev'=8] {'group','dev'}, dimensions={0}, use_global_device_ids=true | all-gather | bytes 270336 | tf_op jit(solution)/shard_map/all_gather | solution.py:48
  192.3 0.7 gather_fusion.3
  193.0 0.1 broadcast_select_fusion
  193.1 1.8 reshape.71
  194.9 2.2 collective-permute-start.2
  197.2 1.3 collective-permute-start.3
  198.5 1.7 fusion.6
  200.3 0.7 gather_fusion.2
  201.0 3.4 %convolution_bitcast_fusion = f32[32,16,128]{2,1,0:T(8,128)S(1)} fusion(bf16[32,4,128,128]{3,2,1,0:T(8,128)(2,1)} %param.14, bf16[32,4,16,128]{3,2,1,0:T(8,128)(2,1)S(1)} %bitcast.116, pred[32,4]{1,0:T(8,128)(4,1)S(1)} %copy-done.7), kind=kOutput, calls=%fused_computation.6 | convolution fusion | flops 67371008 | bytes 4980864 | tf_op jit(solution)/shard_map/lkpq,rlkq->rlp/dot_general | solution.py:40
  204.5 0.5 fusion
  205.0 0.3 multiply_reduce_fusion
  205.3 40.0 %psum.31 = f32[16]{0:T(128)S(1)} all-reduce(f32[16]{0:T(128)S(1)} %multiply_reduce_fusion), channel_id=1, replica_groups=mesh['group'=4,'dev'=8] {'group','dev'}, use_global_device_ids=true, to_apply=%region_9.12 | all-reduce | flops 16 | bytes 128 | tf_op jit(solution)/shard_map/psum | solution.py:75
  245.2 1.0 multiply_subtract_fusion
  (41 shorter events, 0.3 us)
Async XLA Ops:
  0.6 10.7 %copy-start = (bf16[32,64,128]{2,1,0:T(8,128)(2,1)S(1)}, bf16[32,64,128]{2,1,0:T(8,128)(2,1)}, u32[]{:S(2)}) copy-start(bf16[32,64,128]{2,1,0:T(8,128)(2,1)} %param.16) | copy-start | bytes 1572868
  2.3 62.7 %collective-permute-start = (bf16[16,4,128]{2,0,1:T(8,128)(2,1)}, bf16[16,4,128]{2,0,1:T(8,128)(2,1)}, u32[]{:S(2)}, u32[]{:S(2)}) collective-permute-start(bf16[16,4,128]{2,0,1:T(8,128)(2,1)} %get-tuple-element.14), channel_id=1, source_target_pairs={{0,1},{1,2},{2,3},{3,4},{4,5},{5,6},{6,7},{8,9},{9,10},{10,11},{11... | collective-permute-start | bytes 49160 | tf_op jit(solution)/shard_map/ppermute | solution.py:20
  5.2 59.8 %collective-permute-start.1 = (bf16[16,4,128]{2,0,1:T(8,128)(2,1)}, bf16[16,4,128]{2,0,1:T(8,128)(2,1)}, u32[]{:S(2)}, u32[]{:S(2)}) collective-permute-start(bf16[16,4,128]{2,0,1:T(8,128)(2,1)} %get-tuple-element.15), channel_id=1, source_target_pairs={{1,0},{2,1},{3,2},{4,3},{5,4},{6,5},{7,6},{9,8},{10,9},{11,10},{12... | collective-permute-start | bytes 49160 | tf_op jit(solution)/shard_map/ppermute | solution.py:22
  7.9 54.6 %copy-start.10 = (pred[4,16]{1,0:T(4,128)(4,1)}, pred[4,16]{1,0:T(4,128)(4,1)S(1)}, u32[]{:S(2)}) copy-start(pred[4,16]{1,0:T(4,128)(4,1)S(1)} %compare_and_fusion) | copy-start | bytes 196
  58.8 3.7 %copy-start.8 = (s32[1024]{0:T(1024)}, s32[1024]{0:T(1024)S(1)}, u32[]{:S(2)}) copy-start(s32[1024]{0:T(1024)S(1)} %pad_clamp_fusion) | copy-start | bytes 12292
  63.6 6.3 %copy-start.5 = (bf16[4,64,16]{1,2,0:T(8,128)(2,1)S(1)}, bf16[4,64,16]{1,2,0:T(8,128)(2,1)}, u32[]{:S(2)}) copy-start(bf16[4,64,16]{1,2,0:T(8,128)(2,1)} %fusion.7) | copy-start | bytes 24580
  63.6 6.9 %copy-start.1 = (f32[16,4096]{1,0:T(8,128)S(1)}, f32[16,4096]{1,0:T(8,128)}, u32[]{:S(2)}) copy-start(f32[16,4096]{1,0:T(8,128)} %param.12) | copy-start | bytes 786436
  63.6 6.9 %copy-start.2 = (f32[4096]{0:T(1024)S(1)}, f32[4096]{0:T(1024)}, u32[]{:S(2)}) copy-start(f32[4096]{0:T(1024)} %param.13) | copy-start | bytes 49156
  64.3 5.7 %copy-start.3 = (s32[1024]{0:T(1024)}, s32[1024]{0:T(1024)S(1)}, u32[]{:S(2)}) copy-start(s32[1024]{0:T(1024)S(1)} %pad_clamp_fusion.1) | copy-start | bytes 12292
  65.0 5.0 %copy-start.6 = (pred[32,4]{1,0:T(8,128)(4,1)}, pred[32,4]{1,0:T(8,128)(4,1)S(1)}, u32[]{:S(2)}) copy-start(pred[32,4]{1,0:T(8,128)(4,1)S(1)} %copy.44) | copy-start | bytes 388
  69.9 122.4 %copy-start.9 = (s32[1024]{0:T(1024)S(1)}, s32[1024]{0:T(1024)}, u32[]{:S(2)}) copy-start(s32[1024]{0:T(1024)} %copy-done.8) | copy-start | bytes 12292
  69.9 123.1 %copy-start.11 = (pred[4,16]{1,0:T(4,128)(4,1)S(1)}, pred[4,16]{1,0:T(4,128)(4,1)}, u32[]{:S(2)}) copy-start(pred[4,16]{1,0:T(4,128)(4,1)} %copy-done.10) | copy-start | bytes 196
  107.8 92.5 %copy-start.4 = (s32[1024]{0:T(1024)S(1)}, s32[1024]{0:T(1024)}, u32[]{:S(2)}) copy-start(s32[1024]{0:T(1024)} %copy-done.3) | copy-start | bytes 12292
  149.2 0.5 copy-start.12
  150.3 50.7 %copy-start.7 = (pred[32,4]{1,0:T(8,128)(4,1)S(1)}, pred[32,4]{1,0:T(8,128)(4,1)}, u32[]{:S(2)}) copy-start(pred[32,4]{1,0:T(8,128)(4,1)} %copy-done.6) | copy-start | bytes 388
  194.9 5.3 %collective-permute-start.2 = (bf16[16,4,128]{2,0,1:T(8,128)(2,1)S(1)}, bf16[16,4,128]{2,0,1:T(8,128)(2,1)S(1)}, u32[]{:S(2)}, u32[]{:S(2)}) collective-permute-start(bf16[16,4,128]{2,0,1:T(8,128)(2,1)S(1)} %get-tuple-element.12), channel_id=1, source_target_pairs={{0,1},{1,2},{2,3},{3,4},{4,5},{5,6},{6,7},{8,9},{9,10},{10,11},{11... | collective-permute-start | bytes 49160 | tf_op jit(solution)/shard_map/ppermute | solution.py:20
  197.2 3.1 %collective-permute-start.3 = (bf16[16,4,128]{2,0,1:T(8,128)(2,1)S(1)}, bf16[16,4,128]{2,0,1:T(8,128)(2,1)S(1)}, u32[]{:S(2)}, u32[]{:S(2)}) collective-permute-start(bf16[16,4,128]{2,0,1:T(8,128)(2,1)S(1)} %get-tuple-element.13), channel_id=1, source_target_pairs={{1,0},{2,1},{3,2},{4,3},{5,4},{6,5},{7,6},{9,8},{10,9},{11,10},{12... | collective-permute-start | bytes 49160 | tf_op jit(solution)/shard_map/ppermute | solution.py:22
  200.3 44.9 %copy-start.13 = (f32[16]{0:T(128)S(1)}, f32[16]{0:T(128)}, u32[]{:S(2)}) copy-start(f32[16]{0:T(128)} %copy-done.12) | copy-start | bytes 196
where the time goes:
time: 247 us; the launch traced here: 246 us
  blocking collectives  205 us (83%)
  matrix products  12.7 us (5%)
  local copies, waits for them, and re-layouts  12.3 us (5%)
  starting transfers between devices  7.75 us (3%)
  other arithmetic  7 us (3%)
    all_gather x2, blocking collectives, operate(): gathered = lax.all_gather(upward, ('group', 'dev'), axis=0, tiled=True)  87.2 us
    psum x2, blocking collectives, squares(): return lax.psum(jnp.sum(residual * residual, axis=1), ('group', 'dev'))  78.3 us
    psum x1, blocking collectives, per_device(): curve = lax.psum(jnp.sum(direction * image, axis=1), ('group', 'dev'))  40 us
    dot_general x2, matrix products, operate(): jnp.einsum('lkpq,rlkq->rlp', near_blocks, values, preferred_element_type=...  6.84 us
    ppermute x2, starting transfers between devices, padded(): lax.ppermute(tail, axis, [(i, (i + 1) % count) for i in range(ends)])  5.18 us
  transfers between devices with their start and end apart: 4, of which 1 were waited for; matrix products, arithmetic and copies ran while one was open for 6% of the time, Pallas kernels for 0%

commit v1 on v0

v1 whole, which is shorter than its diff:
```python
import jax
import jax.numpy as jnp
from jax import lax
from jax.sharding import PartitionSpec as P

LEAF_CL = 8
TOPK = 16
HALO = 4
AXES = ("group", "dev")


def gather_all(part):
    count = lax.axis_size("group") * lax.axis_size("dev")
    return lax.all_to_all(jnp.broadcast_to(part[None], (count,) + part.shape), AXES, 0, 0)


def halo(cells):
    ends = lax.axis_size("dev") - 1
    head = cells[:, :HALO]
    tail = cells[:, cells.shape[1] - HALO :]
    before = lax.ppermute(tail, "dev", [(i, i + 1) for i in range(ends)])
    after = lax.ppermute(head, "dev", [(i + 1, i) for i in range(ends)])
    return jnp.concatenate([before, cells, after], axis=1)


def operate(field, nugget, near_blocks, local_ids, basis, emat, smat, top_list):
    rhs_count, width = field.shape
    leaf_dev = basis.shape[0]
    leaf_size = basis.shape[2]
    rank_size = basis.shape[1]
    cl_dev = smat.shape[0]
    vb = field.astype(jnp.bfloat16).reshape(rhs_count, leaf_dev, leaf_size)
    coef = jnp.einsum("lap,rlp->lar", basis, vb, preferred_element_type=jnp.float32).astype(
        jnp.bfloat16
    )
    upward = jnp.einsum("lab,lar->lbr", emat, coef, preferred_element_type=jnp.float32)
    upward = upward.reshape(cl_dev, LEAF_CL, rank_size, rhs_count).sum(axis=1).astype(jnp.bfloat16)
    gathered = gather_all(upward.reshape(cl_dev, rank_size * rhs_count))
    gathered = gathered.reshape(-1, rank_size * rhs_count)
    values = jnp.take(halo(vb), local_ids, axis=1)
    near = jnp.einsum("lkpq,rlkq->rlp", near_blocks, values, preferred_element_type=jnp.float32)
    picked = jnp.take(gathered, top_list, axis=0).reshape(cl_dev, TOPK, rank_size, rhs_count)
    down = jnp.einsum("ckab,ckbr->car", smat, picked, preferred_element_type=jnp.float32).astype(
        jnp.bfloat16
    )
    spread = jnp.repeat(down, LEAF_CL, axis=0)
    local_coef = jnp.einsum(
        "lab,lbr->lar", emat, spread, preferred_element_type=jnp.float32
    ).astype(jnp.bfloat16)
    far = jnp.einsum("lap,lar->rlp", basis, local_coef, preferred_element_type=jnp.float32)
    return nugget[None, :] * field + (near + far).reshape(rhs_count, width)


def per_device(right_side, nugget, near_blocks, near_list, basis, transfer, coupling, top_list):
    leaf_dev = near_list.shape[0]
    rank_size = basis.shape[1]
    cl_dev = coupling.shape[0]
    first_leaf = (lax.axis_index("group") * lax.axis_size("dev") + lax.axis_index("dev")) * leaf_dev
    local_ids = near_list - first_leaf + HALO
    emat = transfer.reshape(leaf_dev, rank_size, rank_size)
    smat = coupling.reshape(cl_dev, TOPK, rank_size, rank_size)
    fixed = (nugget, near_blocks, local_ids, basis, emat, smat, top_list)
    field = right_side
    image = operate(field, *fixed)
    twice = operate(image, *fixed)

    def dot(left, right):
        return jnp.sum(left * right, axis=1)

    size = dot(image, image)
    own = dot(field, image) / jnp.where(size > 0, size, 1.0)
    rest = field - own[:, None] * image
    bent = image - own[:, None] * twice
    sums = jnp.stack(
        [
            own,
            dot(field, field),
            dot(field, image),
            dot(rest, rest),
            dot(rest, image),
            size,
            dot(rest, bent),
            dot(image, bent) + dot(rest, twice),
            dot(image, twice),
            dot(field, bent),
            dot(field, twice),
        ]
    )
    sums = gather_all(sums)
    norm = jnp.sum(sums[:, 1], axis=0)
    curve = jnp.sum(sums[:, 2], axis=0)
    alpha = norm / curve
    delta = sums[:, 0] - alpha
    norm_next = jnp.sum(sums[:, 3] + delta * (2 * sums[:, 4] + delta * sums[:, 5]), axis=0)
    beta = norm_next / norm
    rest_bent = jnp.sum(sums[:, 6] + delta * (sums[:, 7] + delta * sums[:, 8]), axis=0)
    rest_image = jnp.sum(sums[:, 4] + delta * sums[:, 5], axis=0)
    field_bent = jnp.sum(sums[:, 9] + delta * sums[:, 10], axis=0)
    curve_next = rest_bent + beta * (rest_image + field_bent + beta * curve)
    alpha_next = norm_next / curve_next
    residual = field - alpha[:, None] * image
    direction = residual + beta[:, None] * field
    solution_field = alpha[:, None] * field + alpha_next[:, None] * direction
    image_next = image - alpha[:, None] * twice + beta[:, None] * image
    return (solution_field, residual - alpha_next[:, None] * image_next)


def solution(mesh):
    placed = (
        P(None, AXES),
        P(AXES),
        P(AXES, None, None, None),
        P(AXES, None),
        P(AXES, None, None),
        P(AXES, None),
        P(AXES, None, None),
        P(AXES, None),
    )
    return jax.shard_map(
        per_device,
        mesh=mesh,
        in_specs=placed,
        out_specs=(P(None, AXES), P(None, AXES)),
        check_vma=False,
    )
```

time: 247 us -> 75.4 us (0.31)
  blocking collectives: 205 us -> 9.57 us
  starting transfers between devices: 7.75 us -> 23.4 us
  waiting for transfers between devices: 0.07 us -> 5.12 us
    psum x3 -> x0, blocking collectives: 118 us -> none  [the longest x2 78.3 us: squares(): return lax.psum(jnp.sum(residual * residual, axis=1), ('group', 'dev'))]
    all_gather x2 -> x0, blocking collectives: 87.2 us -> none  [operate(): gathered = lax.all_gather(upward, ('group', 'dev'), axis=0, tiled=True)]
    all_to_all x0 -> x2, starting transfers between devices: none -> 16.2 us  [gather_all(): lax.all_to_all(jnp.broadcast_to(part[None], (count,) + part.shape), AXES,...]
    all_to_all x0 -> x1, blocking collectives: none -> 9.57 us  [gather_all(): lax.all_to_all(jnp.broadcast_to(part[None], (count,) + part.shape), AXES,...]
    all_to_all x0 -> x2, waiting for transfers between devices: none -> 5.11 us  [gather_all(): lax.all_to_all(jnp.broadcast_to(part[None], (count,) + part.shape), AXES,...]
  transfers between devices with their start and end apart: 4 -> 6, of which waited for: 1 -> 2; matrix products, arithmetic and copies ran while one was open for 6% -> 27% of each run, Pallas kernels for 0% -> 0%
where the time goes in v1:
time: 75.4 us; the launch traced here: 74.6 us
  starting transfers between devices  23.4 us (31%)
  matrix products  14.2 us (19%)
  local copies, waits for them, and re-layouts  12.5 us (17%)
  blocking collectives  9.57 us (13%)
  other arithmetic  8.7 us (12%)
  waiting for transfers between devices  5.12 us (7%)
  between operations  1.05 us (1%)
    all_to_all x2, starting transfers between devices, gather_all(): lax.all_to_all(jnp.broadcast_to(part[None], (count,) + part.shape), AXES,...  16.2 us
    all_to_all x1, blocking collectives, gather_all(): lax.all_to_all(jnp.broadcast_to(part[None], (count,) + part.shape), AXES,...  9.57 us
    dot_general x2, matrix products, operate(): jnp.einsum('lkpq,rlkq->rlp', near_blocks, values, preferred_element_type=...  8.28 us
    all_to_all x2, waiting for transfers between devices, gather_all(): lax.all_to_all(jnp.broadcast_to(part[None], (count,) + part.shape), AXES,...  5.11 us
    ppermute x2, starting transfers between devices, halo(): before = lax.ppermute(tail, 'dev', [(i, i + 1) for i in range(ends)])  4.65 us
    dot_general x2, matrix products, operate(): jnp.einsum('lap,lar->rlp', basis, local_coef, preferred_element_type=jnp....  2.96 us
    ppermute x2, starting transfers between devices, halo(): after = lax.ppermute(head, 'dev', [(i + 1, i) for i in range(ends)])  2.58 us
    reshape x1, local copies, waits for them, and re-layouts, per_device(): smat = coupling.reshape(cl_dev, TOPK, rank_size, rank_size)  2.05 us
  transfers between devices with their start and end apart: 6, of which 2 were waited for; matrix products, arithmetic and copies ran while one was open for 27% of the time, Pallas kernels for 0%

profile of v1, /device:TPU:0, one launch (start us, length us, event | category | flops | bytes accessed | tf_op | source)
XLA Modules:
  0.0 74.6 jit_solution(13729326350610731806)
XLA Ops:
  0.6 1.0 %copy_bitcast_fusion.1 = bf16[16,32,128]{2,0,1:T(8,128)(2,1)S(1)} fusion(f32[16,4096]{1,0:T(8,128)} %param.12), kind=kLoop, calls=%fused_computation.53 | loop fusion | flops 65536 | bytes 393216 | tf_op jit(solution)/shard_map/reshape | solution.py:32
  1.7 2.4 %collective-permute-start = (bf16[16,4,128]{2,0,1:T(8,128)(2,1)S(1)}, bf16[16,4,128]{2,0,1:T(8,128)(2,1)S(1)}, u32[]{:S(2)}, u32[]{:S(2)}) collective-permute-start(bf16[16,4,128]{2,0,1:T(8,128)(2,1)S(1)} %get-tuple-element.46), channel_id=1, source_target_pairs={{0,1},{1,2},{2,3},{3,4},{4,5},{5,6},{6,7},{8,9},{9,10},{10,11},{11... | collective-permute-start | bytes 49160 | tf_op jit(solution)/shard_map/ppermute | solution.py:21
  4.1 1.3 %collective-permute-start.1 = (bf16[16,4,128]{2,0,1:T(8,128)(2,1)S(1)}, bf16[16,4,128]{2,0,1:T(8,128)(2,1)S(1)}, u32[]{:S(2)}, u32[]{:S(2)}) collective-permute-start(bf16[16,4,128]{2,0,1:T(8,128)(2,1)S(1)} %get-tuple-element.47), channel_id=1, source_target_pairs={{1,0},{2,1},{3,2},{4,3},{5,4},{6,5},{7,6},{9,8},{10,9},{11,10},{12... | collective-permute-start | bytes 49160 | tf_op jit(solution)/shard_map/ppermute | solution.py:22
  5.4 1.5 %reshape.140 = bf16[32,64,64]{2,1,0:T(8,128)(2,1)S(1)} reshape(bf16[32,4096]{1,0:T(8,128)(2,1)} %param.17) | data formatting | bytes 524288 | tf_op jit(solution)/shard_map/reshape | solution.py:60
  6.8 1.5 %bitcast_reduce_fusion.1 = bf16[4,64,16]{1,2,0:T(8,128)(2,1)S(1)} fusion(bf16[32,64,64]{2,1,0:T(8,128)(2,1)S(1)} %reshape.140, bf16[32,64,128]{2,1,0:T(8,128)(2,1)S(1)} %copy-done, f32[16,4096]{1,0:T(8,128)} %param.12), kind=kOutput, calls=%fused_computation.31 | convolution fusion | flops 12709888 | bytes 1056768 | tf_op jit(solution)/shard_map/lab,lar->lbr/dot_general | solution.py:36
  8.3 0.1 copy.118
  8.4 0.1 convert_element_type.56
  8.5 0.8 %broadcast_in_dim.34 = bf16[32,4,1024]{2,1,0:T(4,128)(2,1)} broadcast(bf16[4,1024]{1,0:T(4,128)(2,1)S(1)} %convert_element_type.56), dimensions={1,2} | broadcast | bytes 270336 | tf_op jit(solution)/shard_map/broadcast_in_dim | solution.py:14
  9.3 9.2 %all-to-all-start = ((bf16[32,4,1024]{2,1,0:T(4,128)(2,1)}), bf16[32,4,1024]{2,1,0:T(4,128)(2,1)S(1)}, u32[]{:S(2)}, u32[]{:S(2)}) async-start(bf16[32,4,1024]{2,1,0:T(4,128)(2,1)} %broadcast_in_dim.34), calls=%async_computation | async-start | bytes 524288 | tf_op jit(solution)/shard_map/all_to_all | solution.py:14
  18.5 0.7 compare_select_fusion
  19.2 0.7 compare_and_fusion
  19.9 0.7 compare_and_fusion.1
  20.9 0.1 copy.112
  21.0 2.1 %reshape.144 = bf16[4,16,64,64]{3,2,1,0:T(8,128)(2,1)S(1)} reshape(bf16[4,16,4096]{2,1,0:T(8,128)(2,1)} %param.18) | data formatting | bytes 1048576 | tf_op jit(solution)/shard_map/reshape | solution.py:61
  23.1 0.7 gather_fusion
  23.8 4.1 %convolution_bitcast_fusion.1 = f32[32,16,128]{2,1,0:T(8,128)} fusion(bf16[32,4,128,128]{3,2,1,0:T(8,128)(2,1)} %param.14, bf16[32,4,16,128]{3,2,1,0:T(8,128)(2,1)S(1)} %bitcast.145, pred[32,4]{1,0:T(8,128)(4,1)S(1)} %copy.112), kind=kOutput, calls=%fused_computation.9 | convolution fusion | flops 67371008 | bytes 4980864 | tf_op jit(solution)/shard_map/lkpq,rlkq->rlp/dot_general | solution.py:41
  28.0 0.9 %all-to-all-done = bf16[32,4,1024]{2,1,0:T(4,128)(2,1)S(1)} async-done(((bf16[32,4,1024]{2,1,0:T(4,128)(2,1)}), bf16[32,4,1024]{2,1,0:T(4,128)(2,1)S(1)}, u32[]{:S(2)}, u32[]{:S(2)}) %all-to-all-start) | async-done | bytes 262176 | tf_op jit(solution)/shard_map/all_to_all | solution.py:14
  29.0 0.7 gather_fusion.1
  29.8 0.8 %reshape.143 = bf16[4,16,64,16]{3,2,1,0:T(8,128)(2,1)S(1)} reshape(bf16[4,16,1024]{2,1,0:T(8,128)(2,1)S(1)} %broadcast_select_fusion.1) | data formatting | bytes 262144 | tf_op jit(solution)/shard_map/reshape | solution.py:42
  30.6 0.5 fusion.7
  31.2 1.5 %fusion.1 = f32[32,2,8,128]{3,2,1,0:T(8,128)S(1)} fusion(f32[32,16,128]{2,1,0:T(8,128)} %convolution_bitcast_fusion.1, bf16[32,64,128]{2,1,0:T(8,128)(2,1)S(1)} %copy-done, bf16[32,64,16]{1,2,0:T(8,128)(2,1)S(1)} %bitcast.151, bf16[32,64,64]{2,1,0:T(8,128)(2,1)S(1)} %reshape.140), kind=kOutput, calls=%fused_computation.8 | convolution fusion | flops 12681216 | bytes 1376256 | tf_op jit(solution)/shard_map/lap,lar->rlp/dot_general | solution.py:50
  32.7 0.8 %convert_bitcast_fusion = (bf16[2,32,8,128]{3,2,1,0:T(8,128)(2,1)S(1)}, f32[16,4096]{1,0:T(8,128)S(1)}) fusion(f32[32,2,8,128]{3,2,1,0:T(8,128)S(1)} %fusion.1, f32[16,4096]{1,0:T(8,128)S(1)} %copy-done.1, f32[4096]{0:T(1024)} %param.13), kind=kLoop, calls=%fused_computation.54 | loop fusion | flops 196608 | bytes 933888
  33.5 0.5 bitcast_reduce_fusion
  34.0 2.3 %collective-permute-start.2 = (bf16[16,4,128]{2,0,1:T(8,128)(2,1)S(1)}, bf16[16,4,128]{2,0,1:T(8,128)(2,1)S(1)}, u32[]{:S(2)}, u32[]{:S(2)}) collective-permute-start(bf16[16,4,128]{2,0,1:T(8,128)(2,1)S(1)} %get-tuple-element.44), channel_id=1, source_target_pairs={{0,1},{1,2},{2,3},{3,4},{4,5},{5,6},{6,7},{8,9},{9,10},{10,11},{11... | collective-permute-start | bytes 49160 | tf_op jit(solution)/shard_map/ppermute | solution.py:21
  36.3 1.3 %collective-permute-start.3 = (bf16[16,4,128]{2,0,1:T(8,128)(2,1)S(1)}, bf16[16,4,128]{2,0,1:T(8,128)(2,1)S(1)}, u32[]{:S(2)}, u32[]{:S(2)}) collective-permute-start(bf16[16,4,128]{2,0,1:T(8,128)(2,1)S(1)} %get-tuple-element.45), channel_id=1, source_target_pairs={{1,0},{2,1},{3,2},{4,3},{5,4},{6,5},{7,6},{9,8},{10,9},{11,10},{12... | collective-permute-start | bytes 49160 | tf_op jit(solution)/shard_map/ppermute | solution.py:22
  37.6 0.1 copy.127
  37.7 0.1 convert_element_type.63
  37.8 0.8 %broadcast_in_dim.62 = bf16[32,4,1024]{2,1,0:T(4,128)(2,1)} broadcast(bf16[4,1024]{1,0:T(4,128)(2,1)S(1)} %convert_element_type.63), dimensions={1,2} | broadcast | bytes 270336 | tf_op jit(solution)/shard_map/broadcast_in_dim | solution.py:14
  38.6 7.0 %all-to-all-start.1 = ((bf16[32,4,1024]{2,1,0:T(4,128)(2,1)}), bf16[32,4,1024]{2,1,0:T(4,128)(2,1)}, u32[]{:S(2)}, u32[]{:S(2)}) async-start(bf16[32,4,1024]{2,1,0:T(4,128)(2,1)} %broadcast_in_dim.62), calls=%async_computation.1 | async-start | bytes 524288 | tf_op jit(solution)/shard_map/all_to_all | solution.py:14
  45.6 0.2 multiply_reduce_fusion.10
  45.8 0.6 fusion.17
  46.4 0.5 fusion.16
  47.0 0.7 gather_fusion.2
  47.7 4.1 %convolution_bitcast_fusion = f32[32,16,128]{2,1,0:T(8,128)} fusion(bf16[32,4,128,128]{3,2,1,0:T(8,128)(2,1)} %param.14, bf16[32,4,16,128]{3,2,1,0:T(8,128)(2,1)S(1)} %bitcast.144, pred[32,4]{1,0:T(8,128)(4,1)S(1)} %copy.112), kind=kOutput, calls=%fused_computation.6 | convolution fusion | flops 67371008 | bytes 4980864 | tf_op jit(solution)/shard_map/lkpq,rlkq->rlp/dot_general | solution.py:41
  51.8 4.2 %all-to-all-done.1 = bf16[32,4,1024]{2,1,0:T(4,128)(2,1)} async-done(((bf16[32,4,1024]{2,1,0:T(4,128)(2,1)}), bf16[32,4,1024]{2,1,0:T(4,128)(2,1)}, u32[]{:S(2)}, u32[]{:S(2)}) %all-to-all-start.1) | async-done | bytes 262176 | tf_op jit(solution)/shard_map/all_to_all | solution.py:14
  56.0 1.0 %reshape.149 = bf16[128,1024]{1,0:T(8,128)(2,1)S(1)} reshape(bf16[32,4,1024]{2,1,0:T(4,128)(2,1)} %all-to-all-done.1) | data formatting | bytes 524288 | tf_op jit(solution)/shard_map/reshape | solution.py:39
  57.0 0.7 gather_fusion.3
  57.8 0.8 %reshape.150 = bf16[4,16,64,16]{3,2,1,0:T(8,128)(2,1)S(1)} reshape(bf16[4,16,1024]{2,1,0:T(8,128)(2,1)S(1)} %broadcast_select_fusion) | data formatting | bytes 262144 | tf_op jit(solution)/shard_map/reshape | solution.py:42
  58.7 0.5 fusion.6
  59.2 1.5 %fusion = f32[32,2,8,128]{3,2,1,0:T(8,128)S(1)} fusion(f32[32,16,128]{2,1,0:T(8,128)} %convolution_bitcast_fusion, bf16[32,64,128]{2,1,0:T(8,128)(2,1)S(1)} %copy-done, bf16[32,64,16]{1,2,0:T(8,128)(2,1)S(1)} %bitcast.150, bf16[32,64,64]{2,1,0:T(8,128)(2,1)S(1)} %reshape.140), kind=kOutput, calls=%fused_computation.5 | convolution fusion | flops 12681216 | bytes 1376256 | tf_op jit(solution)/shard_map/lap,lar->rlp/dot_general | solution.py:50
  60.7 1.4 %multiply_reduce_fusion.3 = (f32[16]{0:T(128)S(1)}, f32[16]{0:T(128)S(1)}, f32[16]{0:T(128)S(1)}, f32[16]{0:T(128)S(1)}, f32[16]{0:T(128)S(1)}, /*index=5*/f32[1...) fusion(f32[32,2,8,128]{3,2,1,0:T(8,128)S(1)} %fusion, f32[16,4096]{1,0:T(8,128)} %copy-done.2, ...), kind=kLoop, calls=%fused_computation.40 | loop fusion | flops 1572720 | bytes 803456 | tf_op jit(solution)/shard_map/reduce_sum | solution.py:68
  62.3 0.1 reshape.213
  62.5 9.6 %all_to_all.15 = f32[32,1,176]{2,1,0:T(1,128)S(1)} all-to-all(f32[32,1,176]{2,1,0:T(1,128)S(1)} %reshape.213), channel_id=1, replica_groups=mesh['group'=4,'dev'=8] {'group','dev'}, dimensions={0} | all-to-all | bytes 45056 | tf_op jit(solution)/shard_map/all_to_all | solution.py:14
  72.0 0.5 broadcast.81
  72.5 0.7 reduce.2
  73.3 0.1 reshape.214
  73.4 0.1 fusion.20
  73.6 1.0 %multiply_subtract_fusion = (f32[16,4096]{1,0:T(8,128)}, f32[16,4096]{1,0:T(8,128)}) fusion(f32[16,4096]{1,0:T(8,128)S(1)} %copy-done.3, f32[16,4096]{1,0:T(8,128)S(1)} %copy-done.1, f32[16]{0:T(128)S(1)} %get-tuple-element.26, f32[16]{0:T(128)S(1)} %get-tuple-element.25, f32[16]{0:T(128)S(1)} %div.46, f32[32,2,8,128]{3,2,1,0:T(8,128)S(1)} %fusion, ...), kind=kLoop, calls=%fused_computation.34 | loop fusion | flops 983040 | bytes 1327296 | tf_op jit(solution)/shard_map/sub | solution.py:105
  (53 shorter events, 0.9 us)
Async XLA Ops:
  0.6 6.2 %copy-start = (bf16[32,64,128]{2,1,0:T(8,128)(2,1)S(1)}, bf16[32,64,128]{2,1,0:T(8,128)(2,1)}, u32[]{:S(2)}) copy-start(bf16[32,64,128]{2,1,0:T(8,128)(2,1)} %param.16) | copy-start | bytes 1572868
  1.7 21.4 %collective-permute-start = (bf16[16,4,128]{2,0,1:T(8,128)(2,1)S(1)}, bf16[16,4,128]{2,0,1:T(8,128)(2,1)S(1)}, u32[]{:S(2)}, u32[]{:S(2)}) collective-permute-start(bf16[16,4,128]{2,0,1:T(8,128)(2,1)S(1)} %get-tuple-element.46), channel_id=1, source_target_pairs={{0,1},{1,2},{2,3},{3,4},{4,5},{5,6},{6,7},{8,9},{9,10},{10,11},{11... | collective-permute-start | bytes 49160 | tf_op jit(solution)/shard_map/ppermute | solution.py:21
  4.1 19.0 %collective-permute-start.1 = (bf16[16,4,128]{2,0,1:T(8,128)(2,1)S(1)}, bf16[16,4,128]{2,0,1:T(8,128)(2,1)S(1)}, u32[]{:S(2)}, u32[]{:S(2)}) collective-permute-start(bf16[16,4,128]{2,0,1:T(8,128)(2,1)S(1)} %get-tuple-element.47), channel_id=1, source_target_pairs={{1,0},{2,1},{3,2},{4,3},{5,4},{6,5},{7,6},{9,8},{10,9},{11,10},{12... | collective-permute-start | bytes 49160 | tf_op jit(solution)/shard_map/ppermute | solution.py:22
  9.3 19.6 %all-to-all-start = ((bf16[32,4,1024]{2,1,0:T(4,128)(2,1)}), bf16[32,4,1024]{2,1,0:T(4,128)(2,1)S(1)}, u32[]{:S(2)}, u32[]{:S(2)}) async-start(bf16[32,4,1024]{2,1,0:T(4,128)(2,1)} %broadcast_in_dim.34), calls=%async_computation | async-start | bytes 524288 | tf_op jit(solution)/shard_map/all_to_all | solution.py:14
  19.9 9.8 %copy-start.7 = (pred[4,16]{1,0:T(4,128)(4,1)}, pred[4,16]{1,0:T(4,128)(4,1)S(1)}, u32[]{:S(2)}) copy-start(pred[4,16]{1,0:T(4,128)(4,1)S(1)} %compare_and_fusion) | copy-start | bytes 196
  20.9 8.1 %copy-start.5 = (s32[1024]{0:T(1024)}, s32[1024]{0:T(1024)S(1)}, u32[]{:S(2)}) copy-start(s32[1024]{0:T(1024)S(1)} %pad_clamp_fusion) | copy-start | bytes 12292
  28.0 4.7 %copy-start.1 = (f32[16,4096]{1,0:T(8,128)S(1)}, f32[16,4096]{1,0:T(8,128)}, u32[]{:S(2)}) copy-start(f32[16,4096]{1,0:T(8,128)} %param.12) | copy-start | bytes 786436
  33.4 18.4 %copy-start.2 = (f32[16,4096]{1,0:T(8,128)}, f32[16,4096]{1,0:T(8,128)S(1)}, u32[]{:S(2)}) copy-start(f32[16,4096]{1,0:T(8,128)S(1)} %get-tuple-element.28) | copy-start | bytes 786436
  34.0 12.9 %collective-permute-start.2 = (bf16[16,4,128]{2,0,1:T(8,128)(2,1)S(1)}, bf16[16,4,128]{2,0,1:T(8,128)(2,1)S(1)}, u32[]{:S(2)}, u32[]{:S(2)}) collective-permute-start(bf16[16,4,128]{2,0,1:T(8,128)(2,1)S(1)} %get-tuple-element.44), channel_id=1, source_target_pairs={{0,1},{1,2},{2,3},{3,4},{4,5},{5,6},{6,7},{8,9},{9,10},{10,11},{11... | collective-permute-start | bytes 49160 | tf_op jit(solution)/shard_map/ppermute | solution.py:21
  36.3 20.7 %copy-start.6 = (s32[1024]{0:T(1024)S(1)}, s32[1024]{0:T(1024)}, u32[]{:S(2)}) copy-start(s32[1024]{0:T(1024)} %copy-done.5) | copy-start | bytes 12292
  36.3 10.6 %collective-permute-start.3 = (bf16[16,4,128]{2,0,1:T(8,128)(2,1)S(1)}, bf16[16,4,128]{2,0,1:T(8,128)(2,1)S(1)}, u32[]{:S(2)}, u32[]{:S(2)}) collective-permute-start(bf16[16,4,128]{2,0,1:T(8,128)(2,1)S(1)} %get-tuple-element.45), channel_id=1, source_target_pairs={{1,0},{2,1},{3,2},{4,3},{5,4},{6,5},{7,6},{9,8},{10,9},{11,10},{12... | collective-permute-start | bytes 49160 | tf_op jit(solution)/shard_map/ppermute | solution.py:22
  38.6 17.4 %all-to-all-start.1 = ((bf16[32,4,1024]{2,1,0:T(4,128)(2,1)}), bf16[32,4,1024]{2,1,0:T(4,128)(2,1)}, u32[]{:S(2)}, u32[]{:S(2)}) async-start(bf16[32,4,1024]{2,1,0:T(4,128)(2,1)} %broadcast_in_dim.62), calls=%async_computation.1 | async-start | bytes 524288 | tf_op jit(solution)/shard_map/all_to_all | solution.py:14
  45.6 12.1 %copy-start.8 = (pred[4,16]{1,0:T(4,128)(4,1)S(1)}, pred[4,16]{1,0:T(4,128)(4,1)}, u32[]{:S(2)}) copy-start(pred[4,16]{1,0:T(4,128)(4,1)} %copy-done.7) | copy-start | bytes 196
  45.8 1.1 %copy-start.9 = (f32[16]{0:T(128)}, f32[16]{0:T(128)S(1)}, u32[]{:S(2)}) copy-start(f32[16]{0:T(128)S(1)} %get-tuple-element.17) | copy-start | bytes 196
  45.8 1.1 %copy-start.11 = (f32[16]{0:T(128)}, f32[16]{0:T(128)S(1)}, u32[]{:S(2)}) copy-start(f32[16]{0:T(128)S(1)} %get-tuple-element.18) | copy-start | bytes 196
  51.8 8.9 %copy-start.4 = (f32[4096]{0:T(1024)S(1)}, f32[4096]{0:T(1024)}, u32[]{:S(2)}) copy-start(f32[4096]{0:T(1024)} %param.13) | copy-start | bytes 49156
  58.7 3.5 %copy-start.10 = (f32[16]{0:T(128)S(1)}, f32[16]{0:T(128)}, u32[]{:S(2)}) copy-start(f32[16]{0:T(128)} %copy-done.9) | copy-start | bytes 196
  58.7 3.5 %copy-start.12 = (f32[16]{0:T(128)S(1)}, f32[16]{0:T(128)}, u32[]{:S(2)}) copy-start(f32[16]{0:T(128)} %copy-done.11) | copy-start | bytes 196
  58.7 3.5 %copy-start.13 = (f32[1,16]{1,0:T(1,128)S(1)}, f32[1,16]{1,0:T(1,128)}, u32[]{:S(2)}) copy-start(f32[1,16]{1,0:T(1,128)} %fusion.16) | copy-start | bytes 196
  59.2 14.4 %copy-start.3 = (f32[16,4096]{1,0:T(8,128)S(1)}, f32[16,4096]{1,0:T(8,128)}, u32[]{:S(2)}) copy-start(f32[16,4096]{1,0:T(8,128)} %copy-done.2) | copy-start | bytes 786436

commit v2 on v1

v2 whole, which is shorter than its diff:
```python
import jax
import jax.numpy as jnp
from jax import lax
from jax.experimental import pallas as pl
from jax.experimental.pallas import tpu as pltpu
from jax.sharding import PartitionSpec as P

LEAF_CL = 8
TOPK = 16
HALO = 4
AXES = ("group", "dev")
VMEM = pl.BlockSpec(memory_space=pltpu.VMEM)
SMEM = pl.BlockSpec(memory_space=pltpu.SMEM)
HBM = pl.BlockSpec(memory_space=pltpu.HBM)
PARAMS = pltpu.CompilerParams(vmem_limit_bytes=16 * 1024 * 1024)


def struct(shape, dtype):
    return jax.ShapeDtypeStruct(shape, dtype)


def in_hbm(*values):
    return [pltpu.with_memory_space_constraint(value, pltpu.HBM) for value in values]


def load_blocks(blocks_hbm, blocks_ref, sem):
    parts = sem.shape[0]
    each = blocks_ref.shape[0] // parts
    spans = [pl.ds(p * each, each) for p in range(parts)]
    copies = load_all([(blocks_hbm.at[at], blocks_ref.at[at]) for at in spans], sem)

    def ready(leaf):
        if leaf % each == 0:
            copies[leaf // each].wait()

    return ready


def load_all(pairs, sem):
    copies = [pltpu.make_async_copy(src, dst, sem.at[at]) for at, (src, dst) in enumerate(pairs)]
    for copy in copies:
        copy.start()
    return copies


def dot_tt(left, right):
    return lax.dot_general(
        left, right, (((1,), (1,)), ((), ())), preferred_element_type=jnp.float32
    )


def dot_nn(left, right):
    return lax.dot_general(
        left, right, (((1,), (0,)), ((), ())), preferred_element_type=jnp.float32
    )


def split(value):
    high = value.astype(jnp.bfloat16)
    low = (value - high.astype(jnp.float32)).astype(jnp.bfloat16)
    return jnp.concatenate([high, low], axis=0)


def put_chunk(chunk_ref, parts):
    for at in range(len(parts) // 2):
        pair = jnp.concatenate(parts[2 * at : 2 * at + 2], axis=1).astype(jnp.bfloat16)
        chunk_ref[:, at] = jnp.broadcast_to(pair[None], (chunk_ref.shape[0],) + pair.shape)


def put_halo(parity, cells, inner_ref, outer_ref):
    span = inner_ref.shape[1]
    head, tail = cells[:, :span], cells[:, cells.shape[1] - span :]

    @pl.when(parity == 0)
    def _():
        inner_ref[...] = tail
        outer_ref[...] = head

    @pl.when(parity != 0)
    def _():
        inner_ref[...] = head
        outer_ref[...] = tail


def first_kernel(
    parity_ref, field_hbm, basis_hbm, transfer_hbm,
    chunk_ref, fold_ref, cells_ref, inner_ref, outer_ref,
    field_ref, basis_ref, transfer_ref, rows_ref, emat_ref, sem,
):
    copies = load_all(
        [(transfer_hbm, transfer_ref), (basis_hbm, basis_ref), (field_hbm, field_ref)], sem
    )
    clusters, rank, span = fold_ref.shape
    leaves, _, leaf = basis_ref.shape
    rhs = field_ref.shape[0]
    lanes = 2 * rank
    copies[0].wait()
    for j in range(rank // 2):
        rows_ref[j * leaves : (j + 1) * leaves] = transfer_ref[:, j * lanes : (j + 1) * lanes].astype(jnp.float32)
    for i in range(leaves):
        rows = rows_ref[pl.ds(i, rank // 2, stride=leaves), :]
        emat_ref[i, pl.ds(0, rank // 2, stride=2), :] = rows
        emat_ref[i, pl.ds(1, rank // 2, stride=2), :] = pltpu.roll(rows, rank, 1)
    copies[1].wait()
    copies[2].wait()
    cells = split(field_ref[...])
    cells_ref[...] = cells
    put_halo(parity_ref[0], cells, inner_ref, outer_ref)
    parts = []
    for c in range(clusters):
        for i in range(LEAF_CL):
            at = c * LEAF_CL + i
            emat = emat_ref[at][:, :rank].astype(jnp.bfloat16)
            fold = lax.dot_general(
                emat, basis_ref[at], (((0,), (0,)), ((), ())), preferred_element_type=jnp.float32
            )
            fold_ref[c, :, i * leaf : (i + 1) * leaf] = fold.astype(jnp.bfloat16)
        up = dot_tt(cells[:, c * span : (c + 1) * span], fold_ref[c])
        parts.append(up[:rhs] + up[rhs:])
    put_chunk(chunk_ref, parts)


def near_sum(ids_ref, cells_ref, inner_ref, outer_ref, blocks_ref, near_ref, table, ready):
    leaves, nears, leaf, _ = blocks_ref.shape
    for i in range(leaves):
        table[i] = cells_ref[:, i * leaf : (i + 1) * leaf]
    for i in range(HALO):
        table[leaves + i] = inner_ref[:, i * leaf : (i + 1) * leaf]
        table[leaves + HALO + i] = outer_ref[:, i * leaf : (i + 1) * leaf]
    rhs = near_ref.shape[0]
    for i in range(leaves):
        ready(i)
        total = None
        for k in range(0, nears, 2):
            values = jnp.concatenate([table[ids_ref[i, k]], table[ids_ref[i, k + 1]]], axis=1)
            part = dot_tt(values, jnp.concatenate([blocks_ref[i, k], blocks_ref[i, k + 1]], axis=1))
            total = part if total is None else total + part
        near_ref[:, i * leaf : (i + 1) * leaf] = total[:rhs] + total[rhs:]


def prepare_kernel(
    ids_ref, cells_ref, inner_ref, outer_ref, fold_ref, coupling_hbm, blocks_hbm,
    near_ref, smat_ref, turned_ref, table, coupling_ref, rows_ref, blocks_ref, coupling_sem, sem,
):
    copies = load_all([(coupling_hbm, coupling_ref)], coupling_sem)
    ready = load_blocks(blocks_hbm, blocks_ref, sem)
    clusters, rank, span = fold_ref.shape
    half = rank // 2
    row = lax.broadcasted_iota(jnp.int32, (rank, rank), 0)
    column = lax.broadcasted_iota(jnp.int32, (rank, rank), 1)
    order = (column == 2 * (row % half) + row // half).astype(jnp.bfloat16)
    for c in range(clusters):
        turned_ref[c] = dot_nn(order, fold_ref[c]).astype(jnp.bfloat16)
    copies[0].wait()
    lower = lax.broadcasted_iota(jnp.int32, (half, 2 * rank), 1) < rank
    for c in range(clusters):
        for j in range(half):
            rows_ref[j * TOPK : (j + 1) * TOPK] = coupling_ref[c, :, j * 2 * rank : (j + 1) * 2 * rank].astype(jnp.float32)
        for k in range(0, TOPK, 2):
            one = rows_ref[pl.ds(k, half, stride=TOPK), :]
            two = rows_ref[pl.ds(k + 1, half, stride=TOPK), :]
            even = jnp.where(lower, one, pltpu.roll(two, rank, 1))
            odd = jnp.where(lower, pltpu.roll(one, rank, 1), two)
            smat_ref[c, :, k * rank : (k + 2) * rank] = jnp.concatenate([even, odd], axis=0).astype(jnp.bfloat16)

    near_sum(ids_ref, cells_ref, inner_ref, outer_ref, blocks_ref, near_ref, table, ready)


def near_kernel(ids_ref, cells_ref, inner_ref, outer_ref, blocks_hbm, near_ref, table, blocks_ref, sem):
    ready = load_blocks(blocks_hbm, blocks_ref, sem)
    near_sum(ids_ref, cells_ref, inner_ref, outer_ref, blocks_ref, near_ref, table, ready)


def far_part(c, top_ref, table_ref, smat_ref, turned_ref):
    rhs, lanes = table_ref.shape[2], table_ref.shape[3]
    rank = lanes // 2
    pairs = table_ref.shape[1]
    lower = lax.broadcasted_iota(jnp.int32, (rhs, lanes), 1) < rank
    pieces = []
    for k in range(0, TOPK, 2):
        halves = []
        for side in (0, 1):
            top = top_ref[c, k + side]
            pair = top // 2
            tile = table_ref[pair // pairs, pair % pairs].astype(jnp.float32)
            turned = pltpu.roll(tile, rank, 1)
            swap = jnp.broadcast_to(top % 2 != side, (rhs, lanes))
            halves.append(jnp.where(swap, turned, tile))
        pieces.append(jnp.where(lower, halves[0], halves[1]).astype(jnp.bfloat16))
    down = dot_tt(jnp.concatenate(pieces, axis=1), smat_ref[c]).astype(jnp.bfloat16)
    return dot_nn(down, turned_ref[c])


def second_kernel(
    parity_ref, top_ref, table_ref, smat_ref, turned_ref, fold_ref, nugget_ref, field_ref, near_ref,
    chunk_ref, image_ref, cells_ref, inner_ref, outer_ref,
):
    clusters, _, span = fold_ref.shape
    rhs = field_ref.shape[0]
    parts = []
    for c in range(clusters):
        at = slice(c * span, (c + 1) * span)
        far = far_part(c, top_ref, table_ref, smat_ref, turned_ref)
        image = nugget_ref[:, at] * field_ref[:, at] + near_ref[:, at] + far
        image_ref[:, at] = image
        both = split(image)
        cells_ref[:, at] = both
        up = dot_tt(both, fold_ref[c])
        parts.append(up[:rhs] + up[rhs:])
    put_chunk(chunk_ref, parts)
    put_halo(parity_ref[0], cells_ref[...], inner_ref, outer_ref)


def third_kernel(
    top_ref, table_ref, smat_ref, turned_ref, nugget_ref, field_ref, image_ref, near_ref,
    twice_ref, sums_ref,
):
    clusters, _, span = turned_ref.shape
    rhs = field_ref.shape[0]
    for c in range(clusters):
        at = slice(c * span, (c + 1) * span)
        far = far_part(c, top_ref, table_ref, smat_ref, turned_ref)
        twice_ref[:, at] = nugget_ref[:, at] * image_ref[:, at] + near_ref[:, at] + far

    def dot(left, right):
        return jnp.sum(left * right, axis=1, keepdims=True)

    field, image, twice = field_ref[...], image_ref[...], twice_ref[...]
    size = dot(image, image)
    cross = dot(field, image)
    own = cross / jnp.where(size > 0, size, 1.0)
    rest = field - own * image
    bent = image - own * twice
    sums = [
        own,
        dot(field, field),
        cross,
        dot(rest, rest),
        dot(rest, image),
        size,
        dot(rest, bent),
        dot(image, bent) + dot(rest, twice),
        dot(image, twice),
        dot(field, bent),
        dot(field, twice),
    ]
    width = sums_ref.shape[2]
    lane = lax.broadcasted_iota(jnp.int32, (rhs, width), 1)
    row = lax.broadcasted_iota(jnp.int32, (rhs, width), 0)
    packed = jnp.zeros((rhs, width), jnp.float32)
    for at, value in enumerate(sums):
        packed = jnp.where(lane == row + at * rhs, value, packed)
    flat = jnp.sum(packed, axis=0, keepdims=True)
    sums_ref[...] = jnp.broadcast_to(flat[None], sums_ref.shape)


def last_kernel(sums_ref, field_ref, image_ref, twice_ref, solution_ref, residual_ref):
    rhs = field_ref.shape[0]
    sums = sums_ref[...].reshape(sums_ref.shape[0], sums_ref.shape[2])

    def part(at):
        return sums[:, at * rhs : (at + 1) * rhs]

    def total(value):
        return jnp.sum(value, axis=0, keepdims=True)

    norm = total(part(1))
    curve = total(part(2))
    alpha = norm / curve
    delta = part(0) - alpha
    norm_next = total(part(3) + delta * (2 * part(4) + delta * part(5)))
    beta = norm_next / norm
    rest_bent = total(part(6) + delta * (part(7) + delta * part(8)))
    rest_image = total(part(4) + delta * part(5))
    field_bent = total(part(9) + delta * part(10))
    curve_next = rest_bent + beta * (rest_image + field_bent + beta * curve)
    alpha_next = norm_next / curve_next
    eye = lax.broadcasted_iota(jnp.int32, (rhs, rhs), 0) == lax.broadcasted_iota(jnp.int32, (rhs, rhs), 1)

    def column(value):
        return jnp.sum(jnp.where(eye, value, 0.0), axis=1, keepdims=True)

    alpha, beta, alpha_next = column(alpha), column(beta), column(alpha_next)
    field, image = field_ref[...], image_ref[...]
    residual = field - alpha * image
    direction = residual + beta * field
    solution_ref[...] = alpha * field + alpha_next * direction
    image_next = image - alpha * twice_ref[...] + beta * image
    residual_ref[...] = residual - alpha_next * image_next


def exchange(chunk):
    return lax.all_to_all(chunk, AXES, 0, 0)


def swap_ends(inner, outer):
    count = lax.axis_size("dev")
    inner = lax.ppermute(inner, "dev", [(i, i ^ 1) for i in range(count)])
    pairs = [(i, i + 1) for i in range(1, count - 1, 2)]
    outer = lax.ppermute(outer, "dev", pairs + [(b, a) for a, b in pairs])
    return inner, outer


def per_device(right_side, nugget, near_blocks, near_list, basis, transfer, coupling, top_list):
    rhs, width = right_side.shape
    leaves, rank, leaf = basis.shape
    clusters = coupling.shape[0]
    span = leaf * LEAF_CL
    devices = lax.axis_size("group") * lax.axis_size("dev")
    place = lax.axis_index("dev")
    parity = place % 2
    first = (lax.axis_index("group") * lax.axis_size("dev") + place) * leaves
    rel = near_list - first
    before = jnp.where(parity == 0, leaves + HALO, leaves)
    after = jnp.where(parity == 0, leaves, leaves + HALO)
    ids = jnp.where(rel < 0, rel + HALO + before, jnp.where(rel >= leaves, rel - leaves + after, rel))
    parity = parity.reshape(1).astype(jnp.int32)
    nugget = nugget[None]
    chunk_shape = struct((devices, clusters // 2, rhs, 2 * rank), jnp.bfloat16)
    end = HALO * leaf
    field_shape = pltpu.VMEM((rhs, width), jnp.float32)
    cells_shape = pltpu.VMEM((2 * rhs, width), jnp.bfloat16)
    fold_shape = pltpu.VMEM((clusters, rank, span), jnp.bfloat16)
    end_shape = struct((2 * rhs, end), jnp.bfloat16)
    table_shape = pltpu.VMEM((leaves + 2 * HALO, 2 * rhs, leaf), jnp.bfloat16)
    parts = 4

    chunk, fold, cells, inner, outer = pl.pallas_call(
        first_kernel,
        in_specs=[SMEM] + [HBM] * 3,
        out_specs=[VMEM] * 5,
        out_shape=[chunk_shape, fold_shape, cells_shape, end_shape, end_shape],
        scratch_shapes=[
            pltpu.VMEM(right_side.shape, right_side.dtype),
            pltpu.VMEM(basis.shape, basis.dtype),
            pltpu.VMEM(transfer.shape, transfer.dtype),
            pltpu.VMEM((leaves * rank // 2, 2 * rank), jnp.float32),
            pltpu.VMEM((leaves, rank, 2 * rank), jnp.float32),
            pltpu.SemaphoreType.DMA((3,)),
        ],
        compiler_params=PARAMS,
        name="first",
    )(parity, *in_hbm(right_side, basis, transfer))
    table = exchange(chunk)
    blocks = in_hbm(near_blocks)
    near, smat, turned = pl.pallas_call(
        prepare_kernel,
        in_specs=[SMEM] + [VMEM] * 4 + [HBM] * 2,
        out_specs=[VMEM] * 3,
        out_shape=[
            field_shape,
            pltpu.VMEM((clusters, rank, TOPK * rank), jnp.bfloat16),
            fold_shape,
        ],
        scratch_shapes=[
            table_shape,
            pltpu.VMEM(coupling.shape, coupling.dtype),
            pltpu.VMEM((rank // 2 * TOPK, 2 * rank), jnp.float32),
            pltpu.VMEM(near_blocks.shape, near_blocks.dtype),
            pltpu.SemaphoreType.DMA((1,)),
            pltpu.SemaphoreType.DMA((parts,)),
        ],
        compiler_params=PARAMS,
        name="prepare",
    )(ids, cells, *swap_ends(inner, outer), fold, *in_hbm(coupling), *blocks)

    chunk, image, cells, inner, outer = pl.pallas_call(
        second_kernel,
        in_specs=[SMEM] * 2 + [VMEM] * 7,
        out_specs=[VMEM] * 5,
        out_shape=[chunk_shape, field_shape, cells_shape, end_shape, end_shape],
        compiler_params=PARAMS,
        name="second",
    )(parity, top_list, table, smat, turned, fold, nugget, right_side, near)
    table = exchange(chunk)
    near = pl.pallas_call(
        near_kernel,
        in_specs=[SMEM] + [VMEM] * 3 + [HBM],
        out_specs=VMEM,
        out_shape=field_shape,
        scratch_shapes=[
            table_shape,
            pltpu.VMEM(near_blocks.shape, near_blocks.dtype),
            pltpu.SemaphoreType.DMA((parts,)),
        ],
        compiler_params=PARAMS,
        name="near",
    )(ids, cells, *swap_ends(inner, outer), *blocks)

    twice, sums = pl.pallas_call(
        third_kernel,
        in_specs=[SMEM] + [VMEM] * 7,
        out_specs=[VMEM] * 2,
        out_shape=[field_shape, struct((devices, 1, 256), jnp.float32)],
        compiler_params=PARAMS,
        name="third",
    )(top_list, table, smat, turned, nugget, right_side, image, near)
    sums = exchange(sums)

    return pl.pallas_call(
        last_kernel,
        in_specs=[VMEM] * 4,
        out_specs=[VMEM] * 2,
        out_shape=[struct((rhs, width), jnp.float32)] * 2,
        compiler_params=PARAMS,
        name="last",
    )(sums, right_side, image, twice)


def solution(mesh):
    placed = (
        P(None, AXES),
        P(AXES),
        P(AXES, None, None, None),
        P(AXES, None),
        P(AXES, None, None),
        P(AXES, None),
        P(AXES, None, None),
        P(AXES, None),
    )
    return jax.shard_map(
        per_device,
        mesh=mesh,
        in_specs=placed,
        out_specs=(P(None, AXES), P(None, AXES)),
        check_vma=False,
    )
```

time: 75.4 us -> 58.5 us (0.78)
  Pallas kernels: 0 us -> 18.2 us
  matrix products: 14.2 us -> 0 us
  local copies, waits for them, and re-layouts: 12.5 us -> 0.78 us
  other arithmetic: 8.7 us -> 0.01 us
  starting transfers between devices: 23.4 us -> 16.5 us
  waiting for transfers between devices: 5.12 us -> 8.96 us
  blocking collectives: 9.57 us -> 13 us
    pallas_call x0 -> x6, Pallas kernels: none -> 18.2 us  [the longest x1 5.18 us: per_device(): pl.pallas_call(prepare_kernel, in_specs=[SMEM] + [VMEM] * 4 + [HBM] * 2,...]
    dot_general x8 -> x0, matrix products: 14.2 us -> none  [the longest x2 8.28 us: operate(): jnp.einsum('lkpq,rlkq->rlp', near_blocks, values, preferred_element_type=...]
    reshape x7 -> x0, local copies, waits for them, and re-layouts: 6.28 us -> none  [the longest x1 2.05 us: per_device(): smat = coupling.reshape(cl_dev, TOPK, rank_size, rank_size)]
    ppermute x4, starting transfers between devices: 7.23 us -> 1.93 us  [the longest x2 1.3 us: swap_ends(): outer = lax.ppermute(outer, 'dev', pairs + [(b, a) for a, b in pairs])]
    all_to_all x2, waiting for transfers between devices: 5.11 us -> 8.66 us  [exchange(): return lax.all_to_all(chunk, AXES, 0, 0)]
    all_to_all x1, blocking collectives: 9.57 us -> 13 us  [exchange(): return lax.all_to_all(chunk, AXES, 0, 0)]
    gather x4 -> x0, local copies, waits for them, and re-layouts: 2.83 us -> none  [the longest x2 1.42 us: operate(): jnp.take(gathered, top_list, axis=0)]
    broadcast_in_dim x7 -> x0, local copies, waits for them, and re-layouts: 1.83 us -> none  [the longest x3 1.57 us: gather_all(): jnp.broadcast_to(part[None], (count,) + part.shape)]
  transfers between devices with their start and end apart: 6 -> 6, of which waited for: 2 -> 3; matrix products, arithmetic and copies ran while one was open for 27% -> 1% of each run, Pallas kernels for 0% -> 16%
where the time goes in v2:
time: 58.5 us; the launch traced here: 58.2 us
  Pallas kernels  18.2 us (31%)
  starting transfers between devices  16.5 us (28%)
  blocking collectives  13 us (22%)
  waiting for transfers between devices  8.96 us (15%)
  local copies, waits for them, and re-layouts  0.78 us (1%)
  between operations  0.77 us (1%)
    all_to_all x2, starting transfers between devices, exchange(): return lax.all_to_all(chunk, AXES, 0, 0)  14.6 us
    all_to_all x1, blocking collectives, exchange(): return lax.all_to_all(chunk, AXES, 0, 0)  13 us
    all_to_all x2, waiting for transfers between devices, exchange(): return lax.all_to_all(chunk, AXES, 0, 0)  8.66 us
    pallas_call x1, Pallas kernels, per_device(): pl.pallas_call(prepare_kernel, in_specs=[SMEM] + [VMEM] * 4 + [HBM] * 2,...  5.18 us
    pallas_call x1, Pallas kernels, per_device(): pl.pallas_call(near_kernel, in_specs=[SMEM] + [VMEM] * 3 + [HBM], out_spe...  3.84 us
    pallas_call x1, Pallas kernels, per_device(): pl.pallas_call(first_kernel, in_specs=[SMEM] + [HBM] * 3, out_specs=[VMEM...  3.04 us
    pallas_call x1, Pallas kernels, per_device(): pl.pallas_call(second_kernel, in_specs=[SMEM] * 2 + [VMEM] * 7, out_specs...  2.76 us
    pallas_call x1, Pallas kernels, per_device(): pl.pallas_call(third_kernel, in_specs=[SMEM] + [VMEM] * 7, out_specs=[VME...  2.15 us
  transfers between devices with their start and end apart: 6, of which 3 were waited for; matrix products, arithmetic and copies ran while one was open for 1% of the time, Pallas kernels for 16%

profile of v2, /device:TPU:0, one launch (start us, length us, event | category | flops | bytes accessed | tf_op | source)
XLA Modules:
  0.0 58.2 jit_solution(15272382703316586426)
XLA Ops:
  0.6 0.0 copy-start
  0.6 0.0 copy-start.2
  0.7 0.0 copy-start.1
  0.7 3.0 %first.1 = (bf16[32,2,16,128]{3,2,1,0:T(8,128)(2,1)}, bf16[4,64,1024]{2,1,0:T(8,128)(2,1)S(1)}, bf16[32,4096]{1,0:T(8,128)(2,1)S(1)}, bf16[32,512]{1,0:T(8,128)(2,1)S(1)}, bf16[32,512]{1,0:T(8,128)(2,1)S(1)}) custom-call(s32[1]{0:T(128)} %bitcast.parity_ref, f32[16,4096]{1,0:T(8,128)} %field_ref.5, bf16[32,64,128]{2,1,0:T(8,128)(2,1)} %basis_hbm.1, ...), custom_call_target="tpu_custom_call" | custom-call | tf_op jit(solution)/shard_map/first/pallas_call | solution.py:328
  3.7 7.3 %all-to-all-start = ((bf16[32,2,16,128]{3,2,1,0:T(8,128)(2,1)}), bf16[32,2,16,128]{3,2,1,0:T(8,128)(2,1)S(1)}, u32[]{:S(2)}, u32[]{:S(2)}) async-start(bf16[32,2,16,128]{3,2,1,0:T(8,128)(2,1)} %get-tuple-element.17), calls=%async_computation | async-start | bytes 524288 | tf_op jit(solution)/shard_map/all_to_all | solution.py:293
  11.0 0.3 collective-permute-start
  11.3 0.7 %collective-permute-start.1 = (bf16[32,512]{1,0:T(8,128)(2,1)S(1)}, bf16[32,512]{1,0:T(8,128)(2,1)S(1)}, u32[]{:S(2)}, u32[]{:S(2)}) collective-permute-start(bf16[32,512]{1,0:T(8,128)(2,1)S(1)} %get-tuple-element.20), channel_id=1, source_target_pairs={{1,2},{3,4},{5,6},{2,1},{4,3},{6,5},{9,10},{11,12},{13,14},{10,9},... | collective-permute-start | bytes 98312 | tf_op jit(solution)/shard_map/ppermute | solution.py:300
  12.0 0.8 %copy.10 = s32[32,4]{1,0:T(8,128)S(1)} copy(s32[32,4]{0,1:T(4,128)} %param.11) | data formatting | bytes 1024 | tf_op args[3]
  12.8 0.0 collective-permute-done.inner_ref
  12.8 0.0 collective-permute-done.1.outer_ref
  12.8 5.2 %prepare.1 = (f32[16,4096]{1,0:T(8,128)S(1)}, bf16[4,64,1024]{2,1,0:T(8,128)(2,1)S(1)}, bf16[4,64,1024]{2,1,0:T(8,128)(2,1)S(1)}) custom-call(s32[32,4]{1,0:T(8,128)S(1)} %fusion.ids_ref, bf16[32,4096]{1,0:T(8,128)(2,1)S(1)} %get-tuple-element.18.cells_ref, bf16[32,512]{1,0:T(8,128)(2,1)S(1)} %collective-permute-done.inner_ref, ...), custom_call_target="tpu_custom_call" | custom-call | tf_op jit(solution)/shard_map/prepare/pallas_call | solution.py:346
  18.0 3.4 %all-to-all-done.table_ref = bf16[32,2,16,128]{3,2,1,0:T(8,128)(2,1)S(1)} async-done(((bf16[32,2,16,128]{3,2,1,0:T(8,128)(2,1)}), bf16[32,2,16,128]{3,2,1,0:T(8,128)(2,1)S(1)}, u32[]{:S(2)}, u32[]{:S(2)}) %all-to-all-start) | async-done | bytes 262176 | tf_op jit(solution)/shard_map/all_to_all | solution.py:293
  21.4 0.0 copy-done
  21.4 0.0 copy-done.2
  21.4 0.0 copy-done.1
  21.4 2.8 %second.1 = (bf16[32,2,16,128]{3,2,1,0:T(8,128)(2,1)}, f32[16,4096]{1,0:T(8,128)S(1)}, bf16[32,4096]{1,0:T(8,128)(2,1)S(1)}, bf16[32,512]{1,0:T(8,128)(2,1)S(1)}, bf16[32,512]{1,0:T(8,128)(2,1)S(1)}) custom-call(s32[1]{0:T(128)} %bitcast.parity_ref, s32[4,16]{1,0:T(4,128)S(1)} %copy-done.2, bf16[32,2,16,128]{3,2,1,0:T(8,128)(2,1)S(1)} %all-to-all-done.table_ref, ...), custom_call_target="tpu_custom_call" | custom-call | tf_op jit(solution)/shard_map/second/pallas_call | solution.py:367
  24.2 7.3 %all-to-all-start.1 = ((bf16[32,2,16,128]{3,2,1,0:T(8,128)(2,1)}), bf16[32,2,16,128]{3,2,1,0:T(8,128)(2,1)S(1)}, u32[]{:S(2)}, u32[]{:S(2)}) async-start(bf16[32,2,16,128]{3,2,1,0:T(8,128)(2,1)} %get-tuple-element.25), calls=%async_computation.1 | async-start | bytes 524288 | tf_op jit(solution)/shard_map/all_to_all | solution.py:293
  31.5 0.3 collective-permute-start.2
  31.8 0.7 %collective-permute-start.3 = (bf16[32,512]{1,0:T(8,128)(2,1)S(1)}, bf16[32,512]{1,0:T(8,128)(2,1)S(1)}, u32[]{:S(2)}, u32[]{:S(2)}) collective-permute-start(bf16[32,512]{1,0:T(8,128)(2,1)S(1)} %get-tuple-element.29), channel_id=1, source_target_pairs={{1,2},{3,4},{5,6},{2,1},{4,3},{6,5},{9,10},{11,12},{13,14},{10,9},... | collective-permute-start | bytes 98312 | tf_op jit(solution)/shard_map/ppermute | solution.py:300
  32.5 0.3 collective-permute-done.2.inner_ref
  32.8 0.0 collective-permute-done.3.outer_ref
  32.8 3.8 %near.1.near_ref = f32[16,4096]{1,0:T(8,128)S(1)} custom-call(s32[32,4]{1,0:T(8,128)S(1)} %fusion.ids_ref, bf16[32,4096]{1,0:T(8,128)(2,1)S(1)} %get-tuple-element.27.cells_ref, bf16[32,512]{1,0:T(8,128)(2,1)S(1)} %collective-permute-done.2.inner_ref, bf16[32,512]{1,0:T(8,128)(2,1)S(1)} %collective-permute-done.3.outer_ref, bf16[32,4,128,128]{3,2,1,0:T(8,128)(2,1)} %blocks_hbm.3), custom_call_target="tpu_custom_call" | custom-call | tf_op jit(solution)/shard_map/near/pallas_call | solution.py:376
  36.6 5.3 %all-to-all-done.1.table_ref = bf16[32,2,16,128]{3,2,1,0:T(8,128)(2,1)S(1)} async-done(((bf16[32,2,16,128]{3,2,1,0:T(8,128)(2,1)}), bf16[32,2,16,128]{3,2,1,0:T(8,128)(2,1)S(1)}, u32[]{:S(2)}, u32[]{:S(2)}) %all-to-all-start.1) | async-done | bytes 262176 | tf_op jit(solution)/shard_map/all_to_all | solution.py:293
  41.9 2.1 %third.1 = (f32[16,4096]{1,0:T(8,128)S(1)}, f32[32,1,256]{2,1,0:T(1,128)S(1)}) custom-call(s32[4,16]{1,0:T(4,128)S(1)} %copy-done.2, bf16[32,2,16,128]{3,2,1,0:T(8,128)(2,1)S(1)} %all-to-all-done.1.table_ref, bf16[4,64,1024]{2,1,0:T(8,128)(2,1)S(1)} %get-tuple-element.22.smat_ref, bf16[4,64,1024]{2,1,0:T(8,128)(2,1)S(1)} %get-tuple-element.23.turned_ref, ...), custom_call_target="tpu_custom_call" | custom-call | tf_op jit(solution)/shard_map/third/pallas_call | solution.py:390
  44.0 13.0 %all_to_all.15.sums_ref = f32[32,1,256]{2,1,0:T(1,128)S(1)} all-to-all(f32[32,1,256]{2,1,0:T(1,128)S(1)} %get-tuple-element.30), channel_id=1, replica_groups=mesh['group'=4,'dev'=8] {'group','dev'}, dimensions={0} | all-to-all | bytes 65536 | tf_op jit(solution)/shard_map/all_to_all | solution.py:293
  57.0 1.2 %last.1 = (f32[16,4096]{1,0:T(8,128)}, f32[16,4096]{1,0:T(8,128)}) custom-call(f32[32,1,256]{2,1,0:T(1,128)S(1)} %all_to_all.15.sums_ref, f32[16,4096]{1,0:T(8,128)S(1)} %copy-done, f32[16,4096]{1,0:T(8,128)S(1)} %get-tuple-element.26.image_ref, f32[16,4096]{1,0:T(8,128)S(1)} %get-tuple-element.31.twice_ref), custom_call_target="tpu_custom_call" | custom-call | tf_op jit(solution)/shard_map/last/pallas_call | solution.py:400
  (1 shorter events, 0.0 us)
Async XLA Ops:
  0.6 20.8 %copy-start = (f32[16,4096]{1,0:T(8,128)S(1)}, f32[16,4096]{1,0:T(8,128)}, u32[]{:S(2)}) copy-start(f32[16,4096]{1,0:T(8,128)} %field_ref.5) | copy-start | bytes 786436
  0.6 20.8 %copy-start.2 = (s32[4,16]{1,0:T(4,128)S(1)}, s32[4,16]{1,0:T(4,128)}, u32[]{:S(2)}) copy-start(s32[4,16]{1,0:T(4,128)} %top_ref.3) | copy-start | bytes 772
  0.7 20.8 %copy-start.1 = (f32[4096]{0:T(1024)S(1)}, f32[4096]{0:T(1024)}, u32[]{:S(2)}) copy-start(f32[4096]{0:T(1024)} %param.9) | copy-start | bytes 49156
  3.7 17.7 %all-to-all-start = ((bf16[32,2,16,128]{3,2,1,0:T(8,128)(2,1)}), bf16[32,2,16,128]{3,2,1,0:T(8,128)(2,1)S(1)}, u32[]{:S(2)}, u32[]{:S(2)}) async-start(bf16[32,2,16,128]{3,2,1,0:T(8,128)(2,1)} %get-tuple-element.17), calls=%async_computation | async-start | bytes 524288 | tf_op jit(solution)/shard_map/all_to_all | solution.py:293
  11.0 1.8 %collective-permute-start = (bf16[32,512]{1,0:T(8,128)(2,1)S(1)}, bf16[32,512]{1,0:T(8,128)(2,1)S(1)}, u32[]{:S(2)}, u32[]{:S(2)}) collective-permute-start(bf16[32,512]{1,0:T(8,128)(2,1)S(1)} %get-tuple-element.19), channel_id=1, source_target_pairs={{0,1},{1,0},{2,3},{3,2},{4,5},{5,4},{6,7},{7,6},{8,9},{9,8},{10,11... | collective-permute-start | bytes 98312 | tf_op jit(solution)/shard_map/ppermute | solution.py:298
  11.3 1.5 %collective-permute-start.1 = (bf16[32,512]{1,0:T(8,128)(2,1)S(1)}, bf16[32,512]{1,0:T(8,128)(2,1)S(1)}, u32[]{:S(2)}, u32[]{:S(2)}) collective-permute-start(bf16[32,512]{1,0:T(8,128)(2,1)S(1)} %get-tuple-element.20), channel_id=1, source_target_pairs={{1,2},{3,4},{5,6},{2,1},{4,3},{6,5},{9,10},{11,12},{13,14},{10,9},... | collective-permute-start | bytes 98312 | tf_op jit(solution)/shard_map/ppermute | solution.py:300
  24.2 17.7 %all-to-all-start.1 = ((bf16[32,2,16,128]{3,2,1,0:T(8,128)(2,1)}), bf16[32,2,16,128]{3,2,1,0:T(8,128)(2,1)S(1)}, u32[]{:S(2)}, u32[]{:S(2)}) async-start(bf16[32,2,16,128]{3,2,1,0:T(8,128)(2,1)} %get-tuple-element.25), calls=%async_computation.1 | async-start | bytes 524288 | tf_op jit(solution)/shard_map/all_to_all | solution.py:293
  31.5 1.3 %collective-permute-start.2 = (bf16[32,512]{1,0:T(8,128)(2,1)S(1)}, bf16[32,512]{1,0:T(8,128)(2,1)S(1)}, u32[]{:S(2)}, u32[]{:S(2)}) collective-permute-start(bf16[32,512]{1,0:T(8,128)(2,1)S(1)} %get-tuple-element.28), channel_id=1, source_target_pairs={{0,1},{1,0},{2,3},{3,2},{4,5},{5,4},{6,7},{7,6},{8,9},{9,8},{10,11... | collective-permute-start | bytes 98312 | tf_op jit(solution)/shard_map/ppermute | solution.py:298
  31.8 1.0 %collective-permute-start.3 = (bf16[32,512]{1,0:T(8,128)(2,1)S(1)}, bf16[32,512]{1,0:T(8,128)(2,1)S(1)}, u32[]{:S(2)}, u32[]{:S(2)}) collective-permute-start(bf16[32,512]{1,0:T(8,128)(2,1)S(1)} %get-tuple-element.29), channel_id=1, source_target_pairs={{1,2},{3,4},{5,6},{2,1},{4,3},{6,5},{9,10},{11,12},{13,14},{10,9},... | collective-permute-start | bytes 98312 | tf_op jit(solution)/shard_map/ppermute | solution.py:300

commit v3 on v2

--- a/solution.py
+++ b/solution.py
@@ -1,3 +1,5 @@
+import functools
+
 import jax
 import jax.numpy as jnp
 from jax import lax
@@ -7,6 +9,7 @@
 
 LEAF_CL = 8
 TOPK = 16
+NEAR = 4
 HALO = 4
 AXES = ("group", "dev")
 VMEM = pl.BlockSpec(memory_space=pltpu.VMEM)
@@ -21,19 +24,6 @@
 
 def in_hbm(*values):
     return [pltpu.with_memory_space_constraint(value, pltpu.HBM) for value in values]
-
-
-def load_blocks(blocks_hbm, blocks_ref, sem):
-    parts = sem.shape[0]
-    each = blocks_ref.shape[0] // parts
-    spans = [pl.ds(p * each, each) for p in range(parts)]
-    copies = load_all([(blocks_hbm.at[at], blocks_ref.at[at]) for at in spans], sem)
-
-    def ready(leaf):
-        if leaf % each == 0:
-            copies[leaf // each].wait()
-
-    return ready
 
 
 def load_all(pairs, sem):
@@ -120,30 +110,18 @@
     put_chunk(chunk_ref, parts)
 
 
-def near_sum(ids_ref, cells_ref, inner_ref, outer_ref, blocks_ref, near_ref, table, ready):
-    leaves, nears, leaf, _ = blocks_ref.shape
-    for i in range(leaves):
-        table[i] = cells_ref[:, i * leaf : (i + 1) * leaf]
-    for i in range(HALO):
-        table[leaves + i] = inner_ref[:, i * leaf : (i + 1) * leaf]
-        table[leaves + HALO + i] = outer_ref[:, i * leaf : (i + 1) * leaf]
-    rhs = near_ref.shape[0]
-    for i in range(leaves):
-        ready(i)
-        total = None
-        for k in range(0, nears, 2):
-            values = jnp.concatenate([table[ids_ref[i, k]], table[ids_ref[i, k + 1]]], axis=1)
-            part = dot_tt(values, jnp.concatenate([blocks_ref[i, k], blocks_ref[i, k + 1]], axis=1))
-            total = part if total is None else total + part
-        near_ref[:, i * leaf : (i + 1) * leaf] = total[:rhs] + total[rhs:]
-
-
 def prepare_kernel(
-    ids_ref, cells_ref, inner_ref, outer_ref, fold_ref, coupling_hbm, blocks_hbm,
-    near_ref, smat_ref, turned_ref, table, coupling_ref, rows_ref, blocks_ref, coupling_sem, sem,
+    place_ref, cells_ref, fold_ref, list_hbm, coupling_hbm, blocks_hbm,
+    near_ref, ends_ref, smat_ref, turned_ref, list_out, table, blocks_ref, coupling_ref, rows_ref, list_ref, sem
 ):
-    copies = load_all([(coupling_hbm, coupling_ref)], coupling_sem)
-    ready = load_blocks(blocks_hbm, blocks_ref, sem)
+    leaves = blocks_ref.shape[0]
+    starts = [0, leaves // 2]
+    spans = [pl.ds(at, leaves // 2) for at in starts]
+    copies = load_all(
+        [(coupling_hbm, coupling_ref), (list_hbm, list_ref), (list_hbm, list_out)]
+        + [(blocks_hbm.at[at], blocks_ref.at[at]) for at in spans],
+        sem,
+    )
     clusters, rank, span = fold_ref.shape
     half = rank // 2
     row = lax.broadcasted_iota(jnp.int32, (rank, rank), 0)
@@ -162,13 +140,93 @@
             even = jnp.where(lower, one, pltpu.roll(two, rank, 1))
             odd = jnp.where(lower, pltpu.roll(one, rank, 1), two)
             smat_ref[c, :, k * rank : (k + 2) * rank] = jnp.concatenate([even, odd], axis=0).astype(jnp.bfloat16)
-
-    near_sum(ids_ref, cells_ref, inner_ref, outer_ref, blocks_ref, near_ref, table, ready)
-
-
-def near_kernel(ids_ref, cells_ref, inner_ref, outer_ref, blocks_hbm, near_ref, table, blocks_ref, sem):
-    ready = load_blocks(blocks_hbm, blocks_ref, sem)
-    near_sum(ids_ref, cells_ref, inner_ref, outer_ref, blocks_ref, near_ref, table, ready)
+    copies[1].wait()
+    copies[2].wait()
+
+    def ready(leaf):
+        if leaf in starts:
+            copies[3 + starts.index(leaf)].wait()
+
+    near_sum(place_ref, list_ref, cells_ref, blocks_ref, near_ref, ends_ref, table, ready)
+
+
+def near_rows(pick, block):
+    total = None
+    for k in range(0, NEAR, 2):
+        values = jnp.concatenate([pick(k), pick(k + 1)], axis=1)
+        part = dot_tt(values, jnp.concatenate([block(k), block(k + 1)], axis=1))
+        total = part if total is None else total + part
+    rhs = total.shape[0] // 2
+    return total[:rhs] + total[rhs:]
+
+
+def near_sum(place_ref, list_ref, cells_ref, blocks_ref, near_ref, ends_ref, table, ready):
+    leaves, _, leaf, _ = blocks_ref.shape
+    for i in range(leaves):
+        table[i] = cells_ref[:, i * leaf : (i + 1) * leaf]
+    table[leaves] = jnp.zeros(table.shape[1:], table.dtype)
+    first = place_ref[0]
+    for i in range(leaves):
+        ready(i)
+
+        def pick(k):
+            at = list_ref[k, i] - first
+            return table[jnp.where((at < 0) | (at >= leaves), leaves, at)]
+
+        near_ref[:, i * leaf : (i + 1) * leaf] = near_rows(pick, lambda k: blocks_ref[i, k])
+    ends_ref[:HALO] = blocks_ref[:HALO]
+    ends_ref[HALO:] = blocks_ref[leaves - HALO :]
+
+
+def near_kernel(
+    place_ref, list_ref, cells_ref, blocks_hbm, near_ref, ends_ref, table, blocks_ref, sem
+):
+    leaves = blocks_ref.shape[0]
+    starts = [0, leaves // 2, leaves * 13 // 16]
+    spans = [pl.ds(a, b - a) for a, b in zip(starts, starts[1:] + [leaves])]
+    copies = [pltpu.make_async_copy(blocks_hbm.at[at], blocks_ref.at[at], sem.at[p]) for p, at in enumerate(spans)]
+    copies[0].start()
+    copies[1].start()
+
+    def ready(leaf):
+        if leaf in starts:
+            at = starts.index(leaf)
+            copies[at].wait()
+            if at == 0:
+                copies[2].start()
+
+    near_sum(place_ref, list_ref, cells_ref, blocks_ref, near_ref, ends_ref, table, ready)
+
+
+def edge_kernel(leaves, place_ref, list_ref, inner_ref, outer_ref, ends_ref, edge_ref, table):
+    leaf = ends_ref.shape[2]
+    zero = 2 * HALO
+    table[zero] = jnp.zeros(table.shape[1:], table.dtype)
+    even = jnp.where(place_ref[1] == 0, HALO, 0)
+    for i in range(HALO):
+        table[even + i] = inner_ref[:, i * leaf : (i + 1) * leaf]
+        table[HALO - even + i] = outer_ref[:, i * leaf : (i + 1) * leaf]
+    first = place_ref[0]
+    for i in range(2 * HALO):
+        own = i if i < HALO else leaves - 2 * HALO + i
+
+        def pick(k):
+            at = list_ref[k, own] - first
+            return table[jnp.where(at < 0, at + HALO, jnp.where(at >= leaves, at - leaves + HALO, zero))]
+
+        edge_ref[:, i * leaf : (i + 1) * leaf] = near_rows(pick, lambda k: ends_ref[i, k])
+
+
+def near_part(c, clusters, near_ref, edge_ref):
+    span = near_ref.shape[1] // clusters
+    near = near_ref[:, c * span : (c + 1) * span]
+    half = edge_ref.shape[1] // 2
+    rest = jnp.zeros((near.shape[0], span - half), jnp.float32)
+    if c == 0:
+        near += jnp.concatenate([edge_ref[:, :half], rest], axis=1)
+    if c == clusters - 1:
+        near += jnp.concatenate([rest, edge_ref[:, half:]], axis=1)
+    return near
 
 
 def far_part(c, top_ref, table_ref, smat_ref, turned_ref):
@@ -192,7 +250,7 @@
 
 
 def second_kernel(
-    parity_ref, top_ref, table_ref, smat_ref, turned_ref, fold_ref, nugget_ref, field_ref, near_ref,
+    parity_ref, top_ref, table_ref, smat_ref, turned_ref, fold_ref, nugget_ref, field_ref, near_ref, edge_ref,
     chunk_ref, image_ref, cells_ref, inner_ref, outer_ref,
 ):
     clusters, _, span = fold_ref.shape
@@ -201,7 +259,7 @@
     for c in range(clusters):
         at = slice(c * span, (c + 1) * span)
         far = far_part(c, top_ref, table_ref, smat_ref, turned_ref)
-        image = nugget_ref[:, at] * field_ref[:, at] + near_ref[:, at] + far
+        image = nugget_ref[:, at] * field_ref[:, at] + near_part(c, clusters, near_ref, edge_ref) + far
         image_ref[:, at] = image
         both = split(image)
         cells_ref[:, at] = both
@@ -212,7 +270,7 @@
 
 
 def third_kernel(
-    top_ref, table_ref, smat_ref, turned_ref, nugget_ref, field_ref, image_ref, near_ref,
+    top_ref, table_ref, smat_ref, turned_ref, nugget_ref, field_ref, image_ref, near_ref, edge_ref,
     twice_ref, sums_ref,
 ):
     clusters, _, span = turned_ref.shape
@@ -220,7 +278,8 @@
     for c in range(clusters):
         at = slice(c * span, (c + 1) * span)
         far = far_part(c, top_ref, table_ref, smat_ref, turned_ref)
-        twice_ref[:, at] = nugget_ref[:, at] * image_ref[:, at] + near_ref[:, at] + far
+        near = near_part(c, clusters, near_ref, edge_ref)
+        twice_ref[:, at] = nugget_ref[:, at] * image_ref[:, at] + near + far
 
     def dot(left, right):
         return jnp.sum(left * right, axis=1, keepdims=True)
@@ -293,9 +352,13 @@
     return lax.all_to_all(chunk, AXES, 0, 0)
 
 
+def swap_cores(value):
+    return lax.ppermute(value, "dev", [(i, i ^ 1) for i in range(lax.axis_size("dev"))])
+
+
 def swap_ends(inner, outer):
     count = lax.axis_size("dev")
-    inner = lax.ppermute(inner, "dev", [(i, i ^ 1) for i in range(count)])
+    inner = swap_cores(inner)
     pairs = [(i, i + 1) for i in range(1, count - 1, 2)]
     outer = lax.ppermute(outer, "dev", pairs + [(b, a) for a, b in pairs])
     return inner, outer
@@ -310,11 +373,9 @@
     place = lax.axis_index("dev")
     parity = place % 2
     first = (lax.axis_index("group") * lax.axis_size("dev") + place) * leaves
-    rel = near_list - first
-    before = jnp.where(parity == 0, leaves + HALO, leaves)
-    after = jnp.where(parity == 0, leaves, leaves + HALO)
-    ids = jnp.where(rel < 0, rel + HALO + before, jnp.where(rel >= leaves, rel - leaves + after, rel))
     parity = parity.reshape(1).astype(jnp.int32)
+    place = jnp.stack([first, parity[0]]).astype(jnp.int32)
+    near_list = near_list.T
     nugget = nugget[None]
     chunk_shape = struct((devices, clusters // 2, rhs, 2 * rank), jnp.bfloat16)
     end = HALO * leaf
@@ -322,8 +383,6 @@
     cells_shape = pltpu.VMEM((2 * rhs, width), jnp.bfloat16)
     fold_shape = pltpu.VMEM((clusters, rank, span), jnp.bfloat16)
     end_shape = struct((2 * rhs, end), jnp.bfloat16)
-    table_shape = pltpu.VMEM((leaves + 2 * HALO, 2 * rhs, leaf), jnp.bfloat16)
-    parts = 4
 
     chunk, fold, cells, inner, outer = pl.pallas_call(
         first_kernel,
@@ -342,59 +401,74 @@
         name="first",
     )(parity, *in_hbm(right_side, basis, transfer))
     table = exchange(chunk)
-    blocks = in_hbm(near_blocks)
-    near, smat, turned = pl.pallas_call(
+    ends_shape = pltpu.VMEM((2 * HALO,) + near_blocks.shape[1:], near_blocks.dtype)
+    near_scratch = [
+        pltpu.VMEM((leaves + 1, 2 * rhs, leaf), jnp.bfloat16),
+        pltpu.VMEM(near_blocks.shape, near_blocks.dtype),
+    ]
+
+    def edge_product(near_list, inner, outer, ends):
+        return pl.pallas_call(
+            functools.partial(edge_kernel, leaves),
+            in_specs=[SMEM] * 2 + [VMEM] * 3,
+            out_specs=VMEM,
+            out_shape=pltpu.VMEM((rhs, 2 * end), jnp.float32),
+            scratch_shapes=[pltpu.VMEM((2 * HALO + 1, 2 * rhs, leaf), jnp.bfloat16)],
+            compiler_params=PARAMS,
+            name="edge",
+        )(place, near_list, *swap_ends(inner, outer), ends)
+
+    near, ends, smat, turned, near_list = pl.pallas_call(
         prepare_kernel,
-        in_specs=[SMEM] + [VMEM] * 4 + [HBM] * 2,
-        out_specs=[VMEM] * 3,
+        in_specs=[SMEM] + [VMEM] * 2 + [HBM] * 3,
+        out_specs=[VMEM] * 5,
         out_shape=[
             field_shape,
+            ends_shape,
             pltpu.VMEM((clusters, rank, TOPK * rank), jnp.bfloat16),
             fold_shape,
+            pltpu.VMEM(near_list.shape, near_list.dtype),
         ],
-        scratch_shapes=[
-            table_shape,
+        scratch_shapes=near_scratch
+        + [
             pltpu.VMEM(coupling.shape, coupling.dtype),
             pltpu.VMEM((rank // 2 * TOPK, 2 * rank), jnp.float32),
-            pltpu.VMEM(near_blocks.shape, near_blocks.dtype),
-            pltpu.SemaphoreType.DMA((1,)),
-            pltpu.SemaphoreType.DMA((parts,)),
+            pltpu.SMEM(near_list.shape, near_list.dtype),
+            pltpu.SemaphoreType.DMA((5,)),
         ],
         compiler_params=PARAMS,
         name="prepare",
-    )(ids, cells, *swap_ends(inner, outer), fold, *in_hbm(coupling), *blocks)
+    )(place, cells, fold, *in_hbm(near_list, coupling, near_blocks))
+    edge = edge_product(near_list, inner, outer, ends)
 
     chunk, image, cells, inner, outer = pl.pallas_call(
         second_kernel,
-        in_specs=[SMEM] * 2 + [VMEM] * 7,
+        in_specs=[SMEM] * 2 + [VMEM] * 8,
         out_specs=[VMEM] * 5,
         out_shape=[chunk_shape, field_shape, cells_shape, end_shape, end_shape],
         compiler_params=PARAMS,
         name="second",
-    )(parity, top_list, table, smat, turned, fold, nugget, right_side, near)
+    )(parity, top_list, table, smat, turned, fold, nugget, right_side, near, edge)
     table = exchange(chunk)
-    near = pl.pallas_call(
+    near, ends = pl.pallas_call(
         near_kernel,
-        in_specs=[SMEM] + [VMEM] * 3 + [HBM],
-        out_specs=VMEM,
-        out_shape=field_shape,
-        scratch_shapes=[
-            table_shape,
-            pltpu.VMEM(near_blocks.shape, near_blocks.dtype),
-            pltpu.SemaphoreType.DMA((parts,)),
-        ],
+        in_specs=[SMEM] * 2 + [VMEM, HBM],
+        out_specs=[VMEM] * 2,
+        out_shape=[field_shape, ends_shape],
+        scratch_shapes=near_scratch + [pltpu.SemaphoreType.DMA((3,))],
         compiler_params=PARAMS,
         name="near",
-    )(ids, cells, *swap_ends(inner, outer), *blocks)
+    )(place, near_list, cells, *in_hbm(near_blocks))
+    edge = edge_product(near_list, inner, outer, ends)
 
     twice, sums = pl.pallas_call(
         third_kernel,
-        in_specs=[SMEM] + [VMEM] * 7,
+        in_specs=[SMEM] + [VMEM] * 8,
         out_specs=[VMEM] * 2,
         out_shape=[field_shape, struct((devices, 1, 256), jnp.float32)],
         compiler_params=PARAMS,
         name="third",
-    )(top_list, table, smat, turned, nugget, right_side, image, near)
+    )(top_list, table, smat, turned, nugget, right_side, image, near, edge)
     sums = exchange(sums)
 
     return pl.pallas_call(

time: 58.5 us -> 51.6 us (0.88)
  starting transfers between devices: 16.5 us -> 12.4 us
  blocking collectives: 13 us -> 10.1 us
  Pallas kernels: 18.2 us -> 19 us
  local copies, waits for them, and re-layouts: 0.78 us -> 0.01 us
    all_to_all x2, starting transfers between devices: 14.6 us -> 10.4 us  [exchange(): return lax.all_to_all(chunk, AXES, 0, 0)]
    all_to_all x1, blocking collectives: 13 us -> 10.1 us  [exchange(): return lax.all_to_all(chunk, AXES, 0, 0)]
    pallas_call x4 -> x6, Pallas kernels: 13.9 us -> 14.8 us  [the longest x1 3.97 us: per_device(): pl.pallas_call(prepare_kernel, in_specs=[SMEM] + [VMEM] * 2 + [HBM] * 3,...]
    unnamed x7 -> x6, local copies, waits for them, and re-layouts: 0.78 us -> 0.01 us
  transfers between devices with their start and end apart: 6 -> 6, of which waited for: 3 -> 2; matrix products, arithmetic and copies ran while one was open for 1% -> 0% of each run, Pallas kernels for 16% -> 19%
where the time goes in v3:
time: 51.6 us; the launch traced here: 51.2 us
  Pallas kernels  19 us (37%)
  starting transfers between devices  12.4 us (24%)
  blocking collectives  10.1 us (20%)
  waiting for transfers between devices  8.82 us (17%)
  between operations  0.78 us (2%)
    all_to_all x2, starting transfers between devices, exchange(): return lax.all_to_all(chunk, AXES, 0, 0)  10.4 us
    all_to_all x1, blocking collectives, exchange(): return lax.all_to_all(chunk, AXES, 0, 0)  10.1 us
    all_to_all x2, waiting for transfers between devices, exchange(): return lax.all_to_all(chunk, AXES, 0, 0)  8.81 us
    pallas_call x1, Pallas kernels, per_device(): pl.pallas_call(prepare_kernel, in_specs=[SMEM] + [VMEM] * 2 + [HBM] * 3,...  3.97 us
    pallas_call x1, Pallas kernels, per_device(): pl.pallas_call(near_kernel, in_specs=[SMEM] * 2 + [VMEM, HBM], out_specs=...  3.91 us
    pallas_call x1, Pallas kernels, per_device(): pl.pallas_call(first_kernel, in_specs=[SMEM] + [HBM] * 3, out_specs=[VMEM...  3.04 us
    pallas_call x1, Pallas kernels, per_device(): pl.pallas_call(second_kernel, in_specs=[SMEM] * 2 + [VMEM] * 8, out_specs...  2.76 us
    pallas_call x1, Pallas kernels, per_device(): pl.pallas_call(third_kernel, in_specs=[SMEM] + [VMEM] * 8, out_specs=[VME...  2.15 us
  transfers between devices with their start and end apart: 6, of which 2 were waited for; matrix products, arithmetic and copies ran while one was open for 0% of the time, Pallas kernels for 19%

profile of v3, /device:TPU:0, one launch (start us, length us, event | category | flops | bytes accessed | tf_op | source)
XLA Modules:
  0.0 51.2 jit_solution(1736025518633138921)
XLA Ops:
  0.6 0.0 copy-start
  0.6 0.0 copy-start.2
  0.7 0.0 copy-start.1
  0.7 3.0 %first.1 = (bf16[32,2,16,128]{3,2,1,0:T(8,128)(2,1)}, bf16[4,64,1024]{2,1,0:T(8,128)(2,1)S(1)}, bf16[32,4096]{1,0:T(8,128)(2,1)S(1)}, bf16[32,512]{1,0:T(8,128)(2,1)S(1)}, bf16[32,512]{1,0:T(8,128)(2,1)S(1)}) custom-call(s32[1]{0:T(128)} %bitcast.parity_ref, f32[16,4096]{1,0:T(8,128)} %field_ref.5, bf16[32,64,128]{2,1,0:T(8,128)(2,1)} %basis_hbm.1, ...), custom_call_target="tpu_custom_call" | custom-call | tf_op jit(solution)/shard_map/first/pallas_call | solution.py:387
  3.7 7.3 %all-to-all-start = ((bf16[32,2,16,128]{3,2,1,0:T(8,128)(2,1)}), bf16[32,2,16,128]{3,2,1,0:T(8,128)(2,1)S(1)}, u32[]{:S(2)}, u32[]{:S(2)}) async-start(bf16[32,2,16,128]{3,2,1,0:T(8,128)(2,1)} %get-tuple-element.21), calls=%async_computation | async-start | bytes 524288 | tf_op jit(solution)/shard_map/all_to_all | solution.py:352
  11.0 0.3 collective-permute-start
  11.3 0.7 %collective-permute-start.1 = (bf16[32,512]{1,0:T(8,128)(2,1)S(1)}, bf16[32,512]{1,0:T(8,128)(2,1)S(1)}, u32[]{:S(2)}, u32[]{:S(2)}) collective-permute-start(bf16[32,512]{1,0:T(8,128)(2,1)S(1)} %get-tuple-element.29), channel_id=1, source_target_pairs={{1,2},{3,4},{5,6},{2,1},{4,3},{6,5},{9,10},{11,12},{13,14},{10,9},... | collective-permute-start | bytes 98312 | tf_op jit(solution)/shard_map/ppermute | solution.py:363
  12.0 0.1 pad_add_fusion.place_ref
  12.1 4.0 %prepare.1 = (f32[16,4096]{1,0:T(8,128)S(1)}, bf16[8,4,128,128]{3,2,1,0:T(8,128)(2,1)S(1)}, bf16[4,64,1024]{2,1,0:T(8,128)(2,1)S(1)}, bf16[4,64,1024]{2,1,0:T(8,128)(2,1)S(1)}, s32[4,32]{1,0:T(4,128)S(1)}) custom-call(s32[2]{0:T(128)S(1)} %pad_add_fusion.place_ref, bf16[32,4096]{1,0:T(8,128)(2,1)S(1)} %get-tuple-element.22.cells_ref, ...), custom_call_target="tpu_custom_call" | custom-call | tf_op jit(solution)/shard_map/prepare/pallas_call | solution.py:421
  16.1 0.0 collective-permute-done.inner_ref
  16.1 0.0 collective-permute-done.1.outer_ref
  16.1 1.0 %edge.2.edge_ref = f32[16,1024]{1,0:T(8,128)S(1)} custom-call(s32[2]{0:T(128)S(1)} %pad_add_fusion.place_ref, s32[4,32]{1,0:T(4,128)S(1)} %get-tuple-element.27.list_ref, bf16[32,512]{1,0:T(8,128)(2,1)S(1)} %collective-permute-done.inner_ref, bf16[32,512]{1,0:T(8,128)(2,1)S(1)} %collective-permute-done.1.outer_ref, ...), custom_call_target="tpu_custom_call" | custom-call | tf_op jit(solution)/shard_map/edge/pallas_call | solution.py:411
  17.1 4.3 %all-to-all-done.table_ref = bf16[32,2,16,128]{3,2,1,0:T(8,128)(2,1)S(1)} async-done(((bf16[32,2,16,128]{3,2,1,0:T(8,128)(2,1)}), bf16[32,2,16,128]{3,2,1,0:T(8,128)(2,1)S(1)}, u32[]{:S(2)}, u32[]{:S(2)}) %all-to-all-start) | async-done | bytes 262176 | tf_op jit(solution)/shard_map/all_to_all | solution.py:352
  21.4 0.0 copy-done
  21.4 0.0 copy-done.2
  21.4 0.0 copy-done.1
  21.4 2.8 %second.1 = (bf16[32,2,16,128]{3,2,1,0:T(8,128)(2,1)}, f32[16,4096]{1,0:T(8,128)S(1)}, bf16[32,4096]{1,0:T(8,128)(2,1)S(1)}, bf16[32,512]{1,0:T(8,128)(2,1)S(1)}, bf16[32,512]{1,0:T(8,128)(2,1)S(1)}) custom-call(s32[1]{0:T(128)} %bitcast.parity_ref, s32[4,16]{1,0:T(4,128)S(1)} %copy-done.2, bf16[32,2,16,128]{3,2,1,0:T(8,128)(2,1)S(1)} %all-to-all-done.table_ref, ...), custom_call_target="tpu_custom_call" | custom-call | tf_op jit(solution)/shard_map/second/pallas_call | solution.py:444
  24.2 3.1 %all-to-all-start.1 = ((bf16[32,2,16,128]{3,2,1,0:T(8,128)(2,1)}), bf16[32,2,16,128]{3,2,1,0:T(8,128)(2,1)S(1)}, u32[]{:S(2)}, u32[]{:S(2)}) async-start(bf16[32,2,16,128]{3,2,1,0:T(8,128)(2,1)} %get-tuple-element.31), calls=%async_computation.1 | async-start | bytes 524288 | tf_op jit(solution)/shard_map/all_to_all | solution.py:352
  27.3 0.3 collective-permute-start.2
  27.7 0.7 %collective-permute-start.3 = (bf16[32,512]{1,0:T(8,128)(2,1)S(1)}, bf16[32,512]{1,0:T(8,128)(2,1)S(1)}, u32[]{:S(2)}, u32[]{:S(2)}) collective-permute-start(bf16[32,512]{1,0:T(8,128)(2,1)S(1)} %get-tuple-element.36), channel_id=1, source_target_pairs={{1,2},{3,4},{5,6},{2,1},{4,3},{6,5},{9,10},{11,12},{13,14},{10,9},... | collective-permute-start | bytes 98312 | tf_op jit(solution)/shard_map/ppermute | solution.py:363
  28.3 3.9 %near.1 = (f32[16,4096]{1,0:T(8,128)S(1)}, bf16[8,4,128,128]{3,2,1,0:T(8,128)(2,1)S(1)}) custom-call(s32[2]{0:T(128)S(1)} %pad_add_fusion.place_ref, s32[4,32]{1,0:T(4,128)S(1)} %get-tuple-element.27.list_ref, bf16[32,4096]{1,0:T(8,128)(2,1)S(1)} %get-tuple-element.33.cells_ref, bf16[32,4,128,128]{3,2,1,0:T(8,128)(2,1)} %blocks_hbm.3), custom_call_target="tpu_custom_call" | custom-call | tf_op jit(solution)/shard_map/near/pallas_call | solution.py:453
  32.2 0.0 collective-permute-done.2.inner_ref
  32.2 0.0 collective-permute-done.3.outer_ref
  32.2 1.0 %edge.3.edge_ref = f32[16,1024]{1,0:T(8,128)S(1)} custom-call(s32[2]{0:T(128)S(1)} %pad_add_fusion.place_ref, s32[4,32]{1,0:T(4,128)S(1)} %get-tuple-element.27.list_ref, bf16[32,512]{1,0:T(8,128)(2,1)S(1)} %collective-permute-done.2.inner_ref, bf16[32,512]{1,0:T(8,128)(2,1)S(1)} %collective-permute-done.3.outer_ref, ...), custom_call_target="tpu_custom_call" | custom-call | tf_op jit(solution)/shard_map/edge/pallas_call | solution.py:411
  33.2 4.5 %all-to-all-done.1.table_ref = bf16[32,2,16,128]{3,2,1,0:T(8,128)(2,1)S(1)} async-done(((bf16[32,2,16,128]{3,2,1,0:T(8,128)(2,1)}), bf16[32,2,16,128]{3,2,1,0:T(8,128)(2,1)S(1)}, u32[]{:S(2)}, u32[]{:S(2)}) %all-to-all-start.1) | async-done | bytes 262176 | tf_op jit(solution)/shard_map/all_to_all | solution.py:352
  37.7 2.1 %third.1 = (f32[16,4096]{1,0:T(8,128)S(1)}, f32[32,1,256]{2,1,0:T(1,128)S(1)}) custom-call(s32[4,16]{1,0:T(4,128)S(1)} %copy-done.2, bf16[32,2,16,128]{3,2,1,0:T(8,128)(2,1)S(1)} %all-to-all-done.1.table_ref, bf16[4,64,1024]{2,1,0:T(8,128)(2,1)S(1)} %get-tuple-element.24.smat_ref, bf16[4,64,1024]{2,1,0:T(8,128)(2,1)S(1)} %get-tuple-element.25.turned_ref, ...), custom_call_target="tpu_custom_call" | custom-call | tf_op jit(solution)/shard_map/third/pallas_call | solution.py:464
  39.9 10.1 %all_to_all.15.sums_ref = f32[32,1,256]{2,1,0:T(1,128)S(1)} all-to-all(f32[32,1,256]{2,1,0:T(1,128)S(1)} %get-tuple-element.38), channel_id=1, replica_groups=mesh['group'=4,'dev'=8] {'group','dev'}, dimensions={0} | all-to-all | bytes 65536 | tf_op jit(solution)/shard_map/all_to_all | solution.py:352
  50.0 1.2 %last.1 = (f32[16,4096]{1,0:T(8,128)}, f32[16,4096]{1,0:T(8,128)}) custom-call(f32[32,1,256]{2,1,0:T(1,128)S(1)} %all_to_all.15.sums_ref, f32[16,4096]{1,0:T(8,128)S(1)} %copy-done, f32[16,4096]{1,0:T(8,128)S(1)} %get-tuple-element.32.image_ref, f32[16,4096]{1,0:T(8,128)S(1)} %get-tuple-element.39.twice_ref), custom_call_target="tpu_custom_call" | custom-call | tf_op jit(solution)/shard_map/last/pallas_call | solution.py:474
Async XLA Ops:
  0.6 20.8 %copy-start = (f32[16,4096]{1,0:T(8,128)S(1)}, f32[16,4096]{1,0:T(8,128)}, u32[]{:S(2)}) copy-start(f32[16,4096]{1,0:T(8,128)} %field_ref.5) | copy-start | bytes 786436
  0.6 20.8 %copy-start.2 = (s32[4,16]{1,0:T(4,128)S(1)}, s32[4,16]{1,0:T(4,128)}, u32[]{:S(2)}) copy-start(s32[4,16]{1,0:T(4,128)} %top_ref.3) | copy-start | bytes 772
  0.7 20.8 %copy-start.1 = (f32[4096]{0:T(1024)S(1)}, f32[4096]{0:T(1024)}, u32[]{:S(2)}) copy-start(f32[4096]{0:T(1024)} %param.9) | copy-start | bytes 49156
  3.7 17.7 %all-to-all-start = ((bf16[32,2,16,128]{3,2,1,0:T(8,128)(2,1)}), bf16[32,2,16,128]{3,2,1,0:T(8,128)(2,1)S(1)}, u32[]{:S(2)}, u32[]{:S(2)}) async-start(bf16[32,2,16,128]{3,2,1,0:T(8,128)(2,1)} %get-tuple-element.21), calls=%async_computation | async-start | bytes 524288 | tf_op jit(solution)/shard_map/all_to_all | solution.py:352
  11.0 5.0 %collective-permute-start = (bf16[32,512]{1,0:T(8,128)(2,1)S(1)}, bf16[32,512]{1,0:T(8,128)(2,1)S(1)}, u32[]{:S(2)}, u32[]{:S(2)}) collective-permute-start(bf16[32,512]{1,0:T(8,128)(2,1)S(1)} %get-tuple-element.28), channel_id=1, source_target_pairs={{0,1},{1,0},{2,3},{3,2},{4,5},{5,4},{6,7},{7,6},{8,9},{9,8},{10,11... | collective-permute-start | bytes 98312 | tf_op jit(solution)/shard_map/ppermute | solution.py:356
  11.3 4.7 %collective-permute-start.1 = (bf16[32,512]{1,0:T(8,128)(2,1)S(1)}, bf16[32,512]{1,0:T(8,128)(2,1)S(1)}, u32[]{:S(2)}, u32[]{:S(2)}) collective-permute-start(bf16[32,512]{1,0:T(8,128)(2,1)S(1)} %get-tuple-element.29), channel_id=1, source_target_pairs={{1,2},{3,4},{5,6},{2,1},{4,3},{6,5},{9,10},{11,12},{13,14},{10,9},... | collective-permute-start | bytes 98312 | tf_op jit(solution)/shard_map/ppermute | solution.py:363
  24.2 13.5 %all-to-all-start.1 = ((bf16[32,2,16,128]{3,2,1,0:T(8,128)(2,1)}), bf16[32,2,16,128]{3,2,1,0:T(8,128)(2,1)S(1)}, u32[]{:S(2)}, u32[]{:S(2)}) async-start(bf16[32,2,16,128]{3,2,1,0:T(8,128)(2,1)} %get-tuple-element.31), calls=%async_computation.1 | async-start | bytes 524288 | tf_op jit(solution)/shard_map/all_to_all | solution.py:352
  27.3 4.9 %collective-permute-start.2 = (bf16[32,512]{1,0:T(8,128)(2,1)S(1)}, bf16[32,512]{1,0:T(8,128)(2,1)S(1)}, u32[]{:S(2)}, u32[]{:S(2)}) collective-permute-start(bf16[32,512]{1,0:T(8,128)(2,1)S(1)} %get-tuple-element.35), channel_id=1, source_target_pairs={{0,1},{1,0},{2,3},{3,2},{4,5},{5,4},{6,7},{7,6},{8,9},{9,8},{10,11... | collective-permute-start | bytes 98312 | tf_op jit(solution)/shard_map/ppermute | solution.py:356
  27.7 4.6 %collective-permute-start.3 = (bf16[32,512]{1,0:T(8,128)(2,1)S(1)}, bf16[32,512]{1,0:T(8,128)(2,1)S(1)}, u32[]{:S(2)}, u32[]{:S(2)}) collective-permute-start(bf16[32,512]{1,0:T(8,128)(2,1)S(1)} %get-tuple-element.36), channel_id=1, source_target_pairs={{1,2},{3,4},{5,6},{2,1},{4,3},{6,5},{9,10},{11,12},{13,14},{10,9},... | collective-permute-start | bytes 98312 | tf_op jit(solution)/shard_map/ppermute | solution.py:363

commit v4 on v3

--- a/solution.py
+++ b/solution.py
@@ -96,29 +96,34 @@
     cells = split(field_ref[...])
     cells_ref[...] = cells
     put_halo(parity_ref[0], cells, inner_ref, outer_ref)
-    parts = []
+    folds = []
     for c in range(clusters):
-        for i in range(LEAF_CL):
-            at = c * LEAF_CL + i
+        tiles = []
+        for at in range(c * LEAF_CL, (c + 1) * LEAF_CL):
             emat = emat_ref[at][:, :rank].astype(jnp.bfloat16)
             fold = lax.dot_general(
                 emat, basis_ref[at], (((0,), (0,)), ((), ())), preferred_element_type=jnp.float32
             )
-            fold_ref[c, :, i * leaf : (i + 1) * leaf] = fold.astype(jnp.bfloat16)
-        up = dot_tt(cells[:, c * span : (c + 1) * span], fold_ref[c])
+            tiles.append(fold.astype(jnp.bfloat16))
+        folds.append(jnp.concatenate(tiles, axis=1))
+        fold_ref[c] = folds[c]
+    parts = []
+    for c, fold in enumerate(folds):
+        up = dot_tt(cells[:, c * span : (c + 1) * span], fold)
         parts.append(up[:rhs] + up[rhs:])
     put_chunk(chunk_ref, parts)
 
 
 def prepare_kernel(
-    place_ref, cells_ref, fold_ref, list_hbm, coupling_hbm, blocks_hbm,
-    near_ref, ends_ref, smat_ref, turned_ref, list_out, table, blocks_ref, coupling_ref, rows_ref, list_ref, sem
+    place_ref, cells_ref, fold_ref, top_hbm, list_hbm, coupling_hbm, blocks_hbm,
+    near_ref, ends_ref, smat_ref, turned_ref, list_out,
+    table, blocks_ref, coupling_ref, rows_ref, top_ref, list_ref, sem
 ):
     leaves = blocks_ref.shape[0]
     starts = [0, leaves // 2]
     spans = [pl.ds(at, leaves // 2) for at in starts]
     copies = load_all(
-        [(coupling_hbm, coupling_ref), (list_hbm, list_ref), (list_hbm, list_out)]
+        [(top_hbm, top_ref), (coupling_hbm, coupling_ref), (list_hbm, list_ref), (list_hbm, list_out)]
         + [(blocks_hbm.at[at], blocks_ref.at[at]) for at in spans],
         sem,
     )
@@ -130,22 +135,26 @@
     for c in range(clusters):
         turned_ref[c] = dot_nn(order, fold_ref[c]).astype(jnp.bfloat16)
     copies[0].wait()
+    copies[1].wait()
     lower = lax.broadcasted_iota(jnp.int32, (half, 2 * rank), 1) < rank
     for c in range(clusters):
         for j in range(half):
             rows_ref[j * TOPK : (j + 1) * TOPK] = coupling_ref[c, :, j * 2 * rank : (j + 1) * 2 * rank].astype(jnp.float32)
-        for k in range(0, TOPK, 2):
-            one = rows_ref[pl.ds(k, half, stride=TOPK), :]
-            two = rows_ref[pl.ds(k + 1, half, stride=TOPK), :]
-            even = jnp.where(lower, one, pltpu.roll(two, rank, 1))
-            odd = jnp.where(lower, pltpu.roll(one, rank, 1), two)
-            smat_ref[c, :, k * rank : (k + 2) * rank] = jnp.concatenate([even, odd], axis=0).astype(jnp.bfloat16)
-    copies[1].wait()
+        for k in range(TOPK):
+            rows = rows_ref[pl.ds(k, half, stride=TOPK), :]
+            upper = jnp.broadcast_to(top_ref[c, k] % 2, lower.shape) == 1
+            here = lower != upper
+            turned = pltpu.roll(rows, rank, 1)
+            even = jnp.where(here, jnp.where(upper, turned, rows), 0.0)
+            odd = jnp.where(here, jnp.where(upper, rows, turned), 0.0)
+            at = slice(k * 2 * rank, (k + 1) * 2 * rank)
+            smat_ref[c, :, at] = jnp.concatenate([even, odd], axis=0).astype(jnp.bfloat16)
     copies[2].wait()
+    copies[3].wait()
 
     def ready(leaf):
         if leaf in starts:
-            copies[3 + starts.index(leaf)].wait()
+            copies[4 + starts.index(leaf)].wait()
 
     near_sum(place_ref, list_ref, cells_ref, blocks_ref, near_ref, ends_ref, table, ready)
 
@@ -229,24 +238,12 @@
     return near
 
 
-def far_part(c, top_ref, table_ref, smat_ref, turned_ref):
-    rhs, lanes = table_ref.shape[2], table_ref.shape[3]
-    rank = lanes // 2
-    pairs = table_ref.shape[1]
-    lower = lax.broadcasted_iota(jnp.int32, (rhs, lanes), 1) < rank
-    pieces = []
-    for k in range(0, TOPK, 2):
-        halves = []
-        for side in (0, 1):
-            top = top_ref[c, k + side]
-            pair = top // 2
-            tile = table_ref[pair // pairs, pair % pairs].astype(jnp.float32)
-            turned = pltpu.roll(tile, rank, 1)
-            swap = jnp.broadcast_to(top % 2 != side, (rhs, lanes))
-            halves.append(jnp.where(swap, turned, tile))
-        pieces.append(jnp.where(lower, halves[0], halves[1]).astype(jnp.bfloat16))
-    down = dot_tt(jnp.concatenate(pieces, axis=1), smat_ref[c]).astype(jnp.bfloat16)
-    return dot_nn(down, turned_ref[c])
+def far_parts(top_ref, table_ref, smat_ref, turned_ref):
+    downs = []
+    for c in range(turned_ref.shape[0]):
+        tiles = [table_ref[top_ref[c, k] >> 1] for k in range(TOPK)]
+        downs.append(dot_tt(jnp.concatenate(tiles, axis=1), smat_ref[c]).astype(jnp.bfloat16))
+    return [dot_nn(down, turned_ref[c]) for c, down in enumerate(downs)]
 
 
 def second_kernel(
@@ -256,9 +253,9 @@
     clusters, _, span = fold_ref.shape
     rhs = field_ref.shape[0]
     parts = []
-    for c in range(clusters):
+    fars = far_parts(top_ref, table_ref, smat_ref, turned_ref)
+    for c, far in enumerate(fars):
         at = slice(c * span, (c + 1) * span)
-        far = far_part(c, top_ref, table_ref, smat_ref, turned_ref)
         image = nugget_ref[:, at] * field_ref[:, at] + near_part(c, clusters, near_ref, edge_ref) + far
         image_ref[:, at] = image
         both = split(image)
@@ -275,9 +272,8 @@
 ):
     clusters, _, span = turned_ref.shape
     rhs = field_ref.shape[0]
-    for c in range(clusters):
+    for c, far in enumerate(far_parts(top_ref, table_ref, smat_ref, turned_ref)):
         at = slice(c * span, (c + 1) * span)
-        far = far_part(c, top_ref, table_ref, smat_ref, turned_ref)
         near = near_part(c, clusters, near_ref, edge_ref)
         twice_ref[:, at] = nugget_ref[:, at] * image_ref[:, at] + near + far
 
@@ -382,7 +378,7 @@
     field_shape = pltpu.VMEM((rhs, width), jnp.float32)
     cells_shape = pltpu.VMEM((2 * rhs, width), jnp.bfloat16)
     fold_shape = pltpu.VMEM((clusters, rank, span), jnp.bfloat16)
-    end_shape = struct((2 * rhs, end), jnp.bfloat16)
+    end_shape = pltpu.HBM((2 * rhs, end), jnp.bfloat16)
 
     chunk, fold, cells, inner, outer = pl.pallas_call(
         first_kernel,
@@ -400,7 +396,7 @@
         compiler_params=PARAMS,
         name="first",
     )(parity, *in_hbm(right_side, basis, transfer))
-    table = exchange(chunk)
+    table = exchange(chunk).reshape(-1, rhs, 2 * rank)
     ends_shape = pltpu.VMEM((2 * HALO,) + near_blocks.shape[1:], near_blocks.dtype)
     near_scratch = [
         pltpu.VMEM((leaves + 1, 2 * rhs, leaf), jnp.bfloat16),
@@ -420,12 +416,12 @@
 
     near, ends, smat, turned, near_list = pl.pallas_call(
         prepare_kernel,
-        in_specs=[SMEM] + [VMEM] * 2 + [HBM] * 3,
+        in_specs=[SMEM] + [VMEM] * 2 + [HBM] * 4,
         out_specs=[VMEM] * 5,
         out_shape=[
             field_shape,
             ends_shape,
-            pltpu.VMEM((clusters, rank, TOPK * rank), jnp.bfloat16),
+            pltpu.VMEM((clusters, rank, TOPK * 2 * rank), jnp.bfloat16),
             fold_shape,
             pltpu.VMEM(near_list.shape, near_list.dtype),
         ],
@@ -433,12 +429,13 @@
         + [
             pltpu.VMEM(coupling.shape, coupling.dtype),
             pltpu.VMEM((rank // 2 * TOPK, 2 * rank), jnp.float32),
+            pltpu.SMEM(top_list.shape, top_list.dtype),
             pltpu.SMEM(near_list.shape, near_list.dtype),
-            pltpu.SemaphoreType.DMA((5,)),
+            pltpu.SemaphoreType.DMA((6,)),
         ],
         compiler_params=PARAMS,
         name="prepare",
-    )(place, cells, fold, *in_hbm(near_list, coupling, near_blocks))
+    )(place, cells, fold, *in_hbm(top_list, near_list, coupling, near_blocks))
     edge = edge_product(near_list, inner, outer, ends)
 
     chunk, image, cells, inner, outer = pl.pallas_call(
@@ -449,7 +446,7 @@
         compiler_params=PARAMS,
         name="second",
     )(parity, top_list, table, smat, turned, fold, nugget, right_side, near, edge)
-    table = exchange(chunk)
+    table = exchange(chunk).reshape(-1, rhs, 2 * rank)
     near, ends = pl.pallas_call(
         near_kernel,
         in_specs=[SMEM] * 2 + [VMEM, HBM],

time: 51.6 us -> 49.8 us (0.965)
  Pallas kernels: 19 us -> 17.2 us
    pallas_call x1, Pallas kernels: 2.15 us -> 1.25 us  [per_device(): pl.pallas_call(third_kernel, in_specs=[SMEM] + [VMEM] * 8, out_specs=[VME...]
    pallas_call x1, Pallas kernels: 2.76 us -> 2.09 us  [per_device(): pl.pallas_call(second_kernel, in_specs=[SMEM] * 2 + [VMEM] * 8, out_specs...]
  transfers between devices with their start and end apart: 6 -> 6, of which waited for: 2 -> 2; matrix products, arithmetic and copies ran while one was open for 0% -> 0% of each run, Pallas kernels for 19% -> 20%
where the time goes in v4:
time: 49.8 us; the launch traced here: 49.4 us
  Pallas kernels  17.2 us (35%)
  starting transfers between devices  12.4 us (25%)
  blocking collectives  10.1 us (20%)
  waiting for transfers between devices  8.81 us (18%)
  between operations  0.78 us (2%)
    all_to_all x2, starting transfers between devices, exchange(): return lax.all_to_all(chunk, AXES, 0, 0)  10.4 us
    all_to_all x1, blocking collectives, exchange(): return lax.all_to_all(chunk, AXES, 0, 0)  10.1 us
    all_to_all x2, waiting for transfers between devices, exchange(): return lax.all_to_all(chunk, AXES, 0, 0)  8.8 us
    pallas_call x1, Pallas kernels, per_device(): pl.pallas_call(prepare_kernel, in_specs=[SMEM] + [VMEM] * 2 + [HBM] * 4,...  3.98 us
    pallas_call x1, Pallas kernels, per_device(): pl.pallas_call(near_kernel, in_specs=[SMEM] * 2 + [VMEM, HBM], out_specs=...  3.91 us
    pallas_call x1, Pallas kernels, per_device(): pl.pallas_call(first_kernel, in_specs=[SMEM] + [HBM] * 3, out_specs=[VMEM...  2.81 us
    pallas_call x1, Pallas kernels, per_device(): pl.pallas_call(second_kernel, in_specs=[SMEM] * 2 + [VMEM] * 8, out_specs...  2.09 us
    pallas_call x2, Pallas kernels, edge_product(): pl.pallas_call(functools.partial(edge_kernel, leaves), in_specs=[SMEM] *...  1.98 us
  transfers between devices with their start and end apart: 6, of which 2 were waited for; matrix products, arithmetic and copies ran while one was open for 0% of the time, Pallas kernels for 20%

profile of v4, /device:TPU:0, one launch (start us, length us, event | category | flops | bytes accessed | tf_op | source)
XLA Modules:
  0.0 49.4 jit_solution(10594432099884426768)
XLA Ops:
  0.6 0.0 copy-start
  0.6 0.0 copy-start.2
  0.7 0.0 copy-start.1
  0.7 2.8 %first.1 = (bf16[32,2,16,128]{3,2,1,0:T(8,128)(2,1)}, bf16[4,64,1024]{2,1,0:T(8,128)(2,1)S(1)}, bf16[32,4096]{1,0:T(8,128)(2,1)S(1)}, bf16[32,512]{1,0:T(8,128)(2,1)}, bf16[32,512]{1,0:T(8,128)(2,1)}) custom-call(s32[1]{0:T(128)} %bitcast.parity_ref, f32[16,4096]{1,0:T(8,128)} %field_ref.5, bf16[32,64,128]{2,1,0:T(8,128)(2,1)} %basis_hbm.1, ...), custom_call_target="tpu_custom_call" | custom-call | tf_op jit(solution)/shard_map/first/pallas_call | solution.py:383
  3.5 7.3 %all-to-all-start = ((bf16[32,2,16,128]{3,2,1,0:T(8,128)(2,1)}), bf16[32,2,16,128]{3,2,1,0:T(8,128)(2,1)S(1)}, u32[]{:S(2)}, u32[]{:S(2)}) async-start(bf16[32,2,16,128]{3,2,1,0:T(8,128)(2,1)} %get-tuple-element.21), calls=%async_computation | async-start | bytes 524288 | tf_op jit(solution)/shard_map/all_to_all | solution.py:348
  10.8 0.3 collective-permute-start
  11.1 0.7 %collective-permute-start.1 = (bf16[32,512]{1,0:T(8,128)(2,1)}, bf16[32,512]{1,0:T(8,128)(2,1)S(1)}, u32[]{:S(2)}, u32[]{:S(2)}) collective-permute-start(bf16[32,512]{1,0:T(8,128)(2,1)} %get-tuple-element.29), channel_id=1, source_target_pairs={{1,2},{3,4},{5,6},{2,1},{4,3},{6,5},{9,10},{11,12},{13,14},{10,9},... | collective-permute-start | bytes 98312 | tf_op jit(solution)/shard_map/ppermute | solution.py:359
  11.8 0.1 pad_add_fusion.place_ref
  11.9 4.0 %prepare.1 = (f32[16,4096]{1,0:T(8,128)S(1)}, bf16[8,4,128,128]{3,2,1,0:T(8,128)(2,1)S(1)}, bf16[4,64,2048]{2,1,0:T(8,128)(2,1)S(1)}, bf16[4,64,1024]{2,1,0:T(8,128)(2,1)S(1)}, s32[4,32]{1,0:T(4,128)S(1)}) custom-call(s32[2]{0:T(128)S(1)} %pad_add_fusion.place_ref, bf16[32,4096]{1,0:T(8,128)(2,1)S(1)} %get-tuple-element.22.cells_ref, ...), custom_call_target="tpu_custom_call" | custom-call | tf_op jit(solution)/shard_map/prepare/pallas_call | solution.py:417
  15.8 0.0 collective-permute-done.inner_ref
  15.9 0.0 collective-permute-done.1.outer_ref
  15.9 1.0 %edge.2.edge_ref = f32[16,1024]{1,0:T(8,128)S(1)} custom-call(s32[2]{0:T(128)S(1)} %pad_add_fusion.place_ref, s32[4,32]{1,0:T(4,128)S(1)} %get-tuple-element.27.list_ref, bf16[32,512]{1,0:T(8,128)(2,1)S(1)} %collective-permute-done.inner_ref, bf16[32,512]{1,0:T(8,128)(2,1)S(1)} %collective-permute-done.1.outer_ref, ...), custom_call_target="tpu_custom_call" | custom-call | tf_op jit(solution)/shard_map/edge/pallas_call | solution.py:407
  16.9 4.3 %all-to-all-done = bf16[32,2,16,128]{3,2,1,0:T(8,128)(2,1)S(1)} async-done(((bf16[32,2,16,128]{3,2,1,0:T(8,128)(2,1)}), bf16[32,2,16,128]{3,2,1,0:T(8,128)(2,1)S(1)}, u32[]{:S(2)}, u32[]{:S(2)}) %all-to-all-start) | async-done | bytes 262176 | tf_op jit(solution)/shard_map/all_to_all | solution.py:348
  21.2 0.0 copy-done
  21.2 0.0 copy-done.2
  21.2 0.0 copy-done.1
  21.2 2.1 %second.1 = (bf16[32,2,16,128]{3,2,1,0:T(8,128)(2,1)}, f32[16,4096]{1,0:T(8,128)S(1)}, bf16[32,4096]{1,0:T(8,128)(2,1)S(1)}, bf16[32,512]{1,0:T(8,128)(2,1)}, bf16[32,512]{1,0:T(8,128)(2,1)}) custom-call(s32[1]{0:T(128)} %bitcast.parity_ref, s32[4,16]{1,0:T(4,128)S(1)} %copy-done.2, bf16[64,16,128]{2,1,0:T(8,128)(2,1)S(1)} %bitcast.7, ...), custom_call_target="tpu_custom_call" | custom-call | tf_op jit(solution)/shard_map/second/pallas_call | solution.py:441
  23.3 3.1 %all-to-all-start.1 = ((bf16[32,2,16,128]{3,2,1,0:T(8,128)(2,1)}), bf16[32,2,16,128]{3,2,1,0:T(8,128)(2,1)S(1)}, u32[]{:S(2)}, u32[]{:S(2)}) async-start(bf16[32,2,16,128]{3,2,1,0:T(8,128)(2,1)} %get-tuple-element.31), calls=%async_computation.1 | async-start | bytes 524288 | tf_op jit(solution)/shard_map/all_to_all | solution.py:348
  26.4 0.3 collective-permute-start.2
  26.8 0.7 %collective-permute-start.3 = (bf16[32,512]{1,0:T(8,128)(2,1)}, bf16[32,512]{1,0:T(8,128)(2,1)S(1)}, u32[]{:S(2)}, u32[]{:S(2)}) collective-permute-start(bf16[32,512]{1,0:T(8,128)(2,1)} %get-tuple-element.36), channel_id=1, source_target_pairs={{1,2},{3,4},{5,6},{2,1},{4,3},{6,5},{9,10},{11,12},{13,14},{10,9},... | collective-permute-start | bytes 98312 | tf_op jit(solution)/shard_map/ppermute | solution.py:359
  27.4 3.9 %near.1 = (f32[16,4096]{1,0:T(8,128)S(1)}, bf16[8,4,128,128]{3,2,1,0:T(8,128)(2,1)S(1)}) custom-call(s32[2]{0:T(128)S(1)} %pad_add_fusion.place_ref, s32[4,32]{1,0:T(4,128)S(1)} %get-tuple-element.27.list_ref, bf16[32,4096]{1,0:T(8,128)(2,1)S(1)} %get-tuple-element.33.cells_ref, bf16[32,4,128,128]{3,2,1,0:T(8,128)(2,1)} %blocks_hbm.3), custom_call_target="tpu_custom_call" | custom-call | tf_op jit(solution)/shard_map/near/pallas_call | solution.py:450
  31.3 0.0 collective-permute-done.2.inner_ref
  31.3 0.0 collective-permute-done.3.outer_ref
  31.3 1.0 %edge.3.edge_ref = f32[16,1024]{1,0:T(8,128)S(1)} custom-call(s32[2]{0:T(128)S(1)} %pad_add_fusion.place_ref, s32[4,32]{1,0:T(4,128)S(1)} %get-tuple-element.27.list_ref, bf16[32,512]{1,0:T(8,128)(2,1)S(1)} %collective-permute-done.2.inner_ref, bf16[32,512]{1,0:T(8,128)(2,1)S(1)} %collective-permute-done.3.outer_ref, ...), custom_call_target="tpu_custom_call" | custom-call | tf_op jit(solution)/shard_map/edge/pallas_call | solution.py:407
  32.3 4.5 %all-to-all-done.1 = bf16[32,2,16,128]{3,2,1,0:T(8,128)(2,1)S(1)} async-done(((bf16[32,2,16,128]{3,2,1,0:T(8,128)(2,1)}), bf16[32,2,16,128]{3,2,1,0:T(8,128)(2,1)S(1)}, u32[]{:S(2)}, u32[]{:S(2)}) %all-to-all-start.1) | async-done | bytes 262176 | tf_op jit(solution)/shard_map/all_to_all | solution.py:348
  36.8 1.2 %third.1 = (f32[16,4096]{1,0:T(8,128)S(1)}, f32[32,1,256]{2,1,0:T(1,128)S(1)}) custom-call(s32[4,16]{1,0:T(4,128)S(1)} %copy-done.2, bf16[64,16,128]{2,1,0:T(8,128)(2,1)S(1)} %bitcast.6, bf16[4,64,2048]{2,1,0:T(8,128)(2,1)S(1)} %get-tuple-element.24.smat_ref, bf16[4,64,1024]{2,1,0:T(8,128)(2,1)S(1)} %get-tuple-element.25.turned_ref, f32[1,4096]{1,0:T(1,128)S(1)} %bitcast.9, ...), custom_call_target="tpu_custom_call" | custom-call | tf_op jit(solution)/shard_map/third/pallas_call | solution.py:461
  38.1 10.1 %all_to_all.15.sums_ref = f32[32,1,256]{2,1,0:T(1,128)S(1)} all-to-all(f32[32,1,256]{2,1,0:T(1,128)S(1)} %get-tuple-element.38), channel_id=1, replica_groups=mesh['group'=4,'dev'=8] {'group','dev'}, dimensions={0} | all-to-all | bytes 65536 | tf_op jit(solution)/shard_map/all_to_all | solution.py:348
  48.2 1.2 %last.1 = (f32[16,4096]{1,0:T(8,128)}, f32[16,4096]{1,0:T(8,128)}) custom-call(f32[32,1,256]{2,1,0:T(1,128)S(1)} %all_to_all.15.sums_ref, f32[16,4096]{1,0:T(8,128)S(1)} %copy-done, f32[16,4096]{1,0:T(8,128)S(1)} %get-tuple-element.32.image_ref, f32[16,4096]{1,0:T(8,128)S(1)} %get-tuple-element.39.twice_ref), custom_call_target="tpu_custom_call" | custom-call | tf_op jit(solution)/shard_map/last/pallas_call | solution.py:471
Async XLA Ops:
  0.6 20.6 %copy-start = (f32[16,4096]{1,0:T(8,128)S(1)}, f32[16,4096]{1,0:T(8,128)}, u32[]{:S(2)}) copy-start(f32[16,4096]{1,0:T(8,128)} %field_ref.5) | copy-start | bytes 786436
  0.6 20.5 %copy-start.2 = (s32[4,16]{1,0:T(4,128)S(1)}, s32[4,16]{1,0:T(4,128)}, u32[]{:S(2)}) copy-start(s32[4,16]{1,0:T(4,128)} %top_ref.3) | copy-start | bytes 772
  0.7 20.5 %copy-start.1 = (f32[4096]{0:T(1024)S(1)}, f32[4096]{0:T(1024)}, u32[]{:S(2)}) copy-start(f32[4096]{0:T(1024)} %param.9) | copy-start | bytes 49156
  3.5 17.7 %all-to-all-start = ((bf16[32,2,16,128]{3,2,1,0:T(8,128)(2,1)}), bf16[32,2,16,128]{3,2,1,0:T(8,128)(2,1)S(1)}, u32[]{:S(2)}, u32[]{:S(2)}) async-start(bf16[32,2,16,128]{3,2,1,0:T(8,128)(2,1)} %get-tuple-element.21), calls=%async_computation | async-start | bytes 524288 | tf_op jit(solution)/shard_map/all_to_all | solution.py:348
  10.8 5.1 %collective-permute-start = (bf16[32,512]{1,0:T(8,128)(2,1)}, bf16[32,512]{1,0:T(8,128)(2,1)S(1)}, u32[]{:S(2)}, u32[]{:S(2)}) collective-permute-start(bf16[32,512]{1,0:T(8,128)(2,1)} %get-tuple-element.28), channel_id=1, source_target_pairs={{0,1},{1,0},{2,3},{3,2},{4,5},{5,4},{6,7},{7,6},{8,9},{9,8},{10,11... | collective-permute-start | bytes 98312 | tf_op jit(solution)/shard_map/ppermute | solution.py:352
  11.1 4.7 %collective-permute-start.1 = (bf16[32,512]{1,0:T(8,128)(2,1)}, bf16[32,512]{1,0:T(8,128)(2,1)S(1)}, u32[]{:S(2)}, u32[]{:S(2)}) collective-permute-start(bf16[32,512]{1,0:T(8,128)(2,1)} %get-tuple-element.29), channel_id=1, source_target_pairs={{1,2},{3,4},{5,6},{2,1},{4,3},{6,5},{9,10},{11,12},{13,14},{10,9},... | collective-permute-start | bytes 98312 | tf_op jit(solution)/shard_map/ppermute | solution.py:359
  23.3 13.5 %all-to-all-start.1 = ((bf16[32,2,16,128]{3,2,1,0:T(8,128)(2,1)}), bf16[32,2,16,128]{3,2,1,0:T(8,128)(2,1)S(1)}, u32[]{:S(2)}, u32[]{:S(2)}) async-start(bf16[32,2,16,128]{3,2,1,0:T(8,128)(2,1)} %get-tuple-element.31), calls=%async_computation.1 | async-start | bytes 524288 | tf_op jit(solution)/shard_map/all_to_all | solution.py:348
  26.4 4.9 %collective-permute-start.2 = (bf16[32,512]{1,0:T(8,128)(2,1)}, bf16[32,512]{1,0:T(8,128)(2,1)S(1)}, u32[]{:S(2)}, u32[]{:S(2)}) collective-permute-start(bf16[32,512]{1,0:T(8,128)(2,1)} %get-tuple-element.35), channel_id=1, source_target_pairs={{0,1},{1,0},{2,3},{3,2},{4,5},{5,4},{6,7},{7,6},{8,9},{9,8},{10,11... | collective-permute-start | bytes 98312 | tf_op jit(solution)/shard_map/ppermute | solution.py:352
  26.8 4.6 %collective-permute-start.3 = (bf16[32,512]{1,0:T(8,128)(2,1)}, bf16[32,512]{1,0:T(8,128)(2,1)S(1)}, u32[]{:S(2)}, u32[]{:S(2)}) collective-permute-start(bf16[32,512]{1,0:T(8,128)(2,1)} %get-tuple-element.36), channel_id=1, source_target_pairs={{1,2},{3,4},{5,6},{2,1},{4,3},{6,5},{9,10},{11,12},{13,14},{10,9},... | collective-permute-start | bytes 98312 | tf_op jit(solution)/shard_map/ppermute | solution.py:359

commit v5 on v4

--- a/solution.py
+++ b/solution.py
@@ -10,6 +10,7 @@
 LEAF_CL = 8
 TOPK = 16
 NEAR = 4
+PARTS = 4
 HALO = 4
 AXES = ("group", "dev")
 VMEM = pl.BlockSpec(memory_space=pltpu.VMEM)
@@ -57,9 +58,9 @@
         chunk_ref[:, at] = jnp.broadcast_to(pair[None], (chunk_ref.shape[0],) + pair.shape)
 
 
-def put_halo(parity, cells, inner_ref, outer_ref):
+def put_halo(parity, cells_ref, inner_ref, outer_ref):
     span = inner_ref.shape[1]
-    head, tail = cells[:, :span], cells[:, cells.shape[1] - span :]
+    head, tail = cells_ref[:, :span], cells_ref[:, cells_ref.shape[1] - span :]
 
     @pl.when(parity == 0)
     def _():
@@ -73,17 +74,27 @@
 
 
 def first_kernel(
-    parity_ref, field_hbm, basis_hbm, transfer_hbm,
-    chunk_ref, fold_ref, cells_ref, inner_ref, outer_ref,
+    field_hbm, basis_hbm, transfer_hbm, list_hbm, top_hbm,
+    chunk_ref, fold_ref, cells_ref, inner_ref, outer_ref, place_ref, list_ref, top_ref,
     field_ref, basis_ref, transfer_ref, rows_ref, emat_ref, sem,
 ):
-    copies = load_all(
-        [(transfer_hbm, transfer_ref), (basis_hbm, basis_ref), (field_hbm, field_ref)], sem
-    )
     clusters, rank, span = fold_ref.shape
     leaves, _, leaf = basis_ref.shape
     rhs = field_ref.shape[0]
     lanes = 2 * rank
+    copies = load_all(
+        [
+            (transfer_hbm, transfer_ref),
+            (field_hbm, field_ref),
+            (basis_hbm, basis_ref),
+            (list_hbm, list_ref),
+            (top_hbm, top_ref),
+        ],
+        sem,
+    )
+    device = lax.axis_index("dev")
+    place_ref[0] = (lax.axis_index("group") * lax.axis_size("dev") + device) * leaves
+    place_ref[1] = device % 2
     copies[0].wait()
     for j in range(rank // 2):
         rows_ref[j * leaves : (j + 1) * leaves] = transfer_ref[:, j * lanes : (j + 1) * lanes].astype(jnp.float32)
@@ -95,38 +106,30 @@
     copies[2].wait()
     cells = split(field_ref[...])
     cells_ref[...] = cells
-    put_halo(parity_ref[0], cells, inner_ref, outer_ref)
     folds = []
     for c in range(clusters):
         tiles = []
-        for at in range(c * LEAF_CL, (c + 1) * LEAF_CL):
-            emat = emat_ref[at][:, :rank].astype(jnp.bfloat16)
+        for i in range(c * LEAF_CL, (c + 1) * LEAF_CL):
+            emat = emat_ref[i][:, :rank].astype(jnp.bfloat16)
             fold = lax.dot_general(
-                emat, basis_ref[at], (((0,), (0,)), ((), ())), preferred_element_type=jnp.float32
+                emat, basis_ref[i], (((0,), (0,)), ((), ())), preferred_element_type=jnp.float32
             )
             tiles.append(fold.astype(jnp.bfloat16))
         folds.append(jnp.concatenate(tiles, axis=1))
         fold_ref[c] = folds[c]
-    parts = []
-    for c, fold in enumerate(folds):
-        up = dot_tt(cells[:, c * span : (c + 1) * span], fold)
-        parts.append(up[:rhs] + up[rhs:])
+    parts = [halves_sum(dot_tt(cells[:, c * span : (c + 1) * span], fold)) for c, fold in enumerate(folds)]
     put_chunk(chunk_ref, parts)
+    put_halo(device % 2, cells_ref, inner_ref, outer_ref)
+    copies[3].wait()
+    copies[4].wait()
 
 
 def prepare_kernel(
-    place_ref, cells_ref, fold_ref, top_hbm, list_hbm, coupling_hbm, blocks_hbm,
-    near_ref, ends_ref, smat_ref, turned_ref, list_out,
-    table, blocks_ref, coupling_ref, rows_ref, top_ref, list_ref, sem
+    place_ref, list_ref, top_ref, cells_ref, fold_ref, coupling_hbm, blocks_hbm,
+    near_ref, ends_ref, smat_ref, turned_ref, table, blocks_ref, coupling_ref, rows_ref, sem
 ):
-    leaves = blocks_ref.shape[0]
-    starts = [0, leaves // 2]
-    spans = [pl.ds(at, leaves // 2) for at in starts]
-    copies = load_all(
-        [(top_hbm, top_ref), (coupling_hbm, coupling_ref), (list_hbm, list_ref), (list_hbm, list_out)]
-        + [(blocks_hbm.at[at], blocks_ref.at[at]) for at in spans],
-        sem,
-    )
+    pairs, each = part_copies(blocks_hbm, blocks_ref)
+    copies = load_all([(coupling_hbm, coupling_ref)] + pairs, sem)
     clusters, rank, span = fold_ref.shape
     half = rank // 2
     row = lax.broadcasted_iota(jnp.int32, (rank, rank), 0)
@@ -135,7 +138,6 @@
     for c in range(clusters):
         turned_ref[c] = dot_nn(order, fold_ref[c]).astype(jnp.bfloat16)
     copies[0].wait()
-    copies[1].wait()
     lower = lax.broadcasted_iota(jnp.int32, (half, 2 * rank), 1) < rank
     for c in range(clusters):
         for j in range(half):
@@ -149,22 +151,11 @@
             odd = jnp.where(here, jnp.where(upper, rows, turned), 0.0)
             at = slice(k * 2 * rank, (k + 1) * 2 * rank)
             smat_ref[c, :, at] = jnp.concatenate([even, odd], axis=0).astype(jnp.bfloat16)
-    copies[2].wait()
-    copies[3].wait()
-
-    def ready(leaf):
-        if leaf in starts:
-            copies[4 + starts.index(leaf)].wait()
-
+    ready = wait_parts(copies[1:], each)
     near_sum(place_ref, list_ref, cells_ref, blocks_ref, near_ref, ends_ref, table, ready)
 
 
-def near_rows(pick, block):
-    total = None
-    for k in range(0, NEAR, 2):
-        values = jnp.concatenate([pick(k), pick(k + 1)], axis=1)
-        part = dot_tt(values, jnp.concatenate([block(k), block(k + 1)], axis=1))
-        total = part if total is None else total + part
+def halves_sum(total):
     rhs = total.shape[0] // 2
     return total[:rhs] + total[rhs:]
 
@@ -176,34 +167,41 @@
     table[leaves] = jnp.zeros(table.shape[1:], table.dtype)
     first = place_ref[0]
     for i in range(leaves):
-        ready(i)
-
-        def pick(k):
+        ready(min(i + HALO, leaves - 1))
+        values, blocks = [], []
+        for k in range(NEAR):
             at = list_ref[k, i] - first
-            return table[jnp.where((at < 0) | (at >= leaves), leaves, at)]
-
-        near_ref[:, i * leaf : (i + 1) * leaf] = near_rows(pick, lambda k: blocks_ref[i, k])
+            inside = (at >= 0) & (at < leaves)
+            values.append(table[jnp.where(inside, at, leaves)])
+            blocks.append(blocks_ref[jnp.where(inside, at, i), k])
+        total = dot_nn(jnp.concatenate(values, axis=1), jnp.concatenate(blocks, axis=0))
+        near_ref[:, i * leaf : (i + 1) * leaf] = halves_sum(total)
     ends_ref[:HALO] = blocks_ref[:HALO]
     ends_ref[HALO:] = blocks_ref[leaves - HALO :]
+
+
+def wait_parts(copies, each):
+    done = []
+
+    def ready(leaf):
+        while len(done) <= leaf // each:
+            copies[len(done)].wait()
+            done.append(leaf)
+
+    return ready
+
+
+def part_copies(blocks_hbm, blocks_ref):
+    each = blocks_ref.shape[0] // PARTS
+    spans = [pl.ds(at * each, each) for at in range(PARTS)]
+    return [(blocks_hbm.at[at], blocks_ref.at[at]) for at in spans], each
 
 
 def near_kernel(
     place_ref, list_ref, cells_ref, blocks_hbm, near_ref, ends_ref, table, blocks_ref, sem
 ):
-    leaves = blocks_ref.shape[0]
-    starts = [0, leaves // 2, leaves * 13 // 16]
-    spans = [pl.ds(a, b - a) for a, b in zip(starts, starts[1:] + [leaves])]
-    copies = [pltpu.make_async_copy(blocks_hbm.at[at], blocks_ref.at[at], sem.at[p]) for p, at in enumerate(spans)]
-    copies[0].start()
-    copies[1].start()
-
-    def ready(leaf):
-        if leaf in starts:
-            at = starts.index(leaf)
-            copies[at].wait()
-            if at == 0:
-                copies[2].start()
-
+    pairs, each = part_copies(blocks_hbm, blocks_ref)
+    ready = wait_parts(load_all(pairs, sem), each)
     near_sum(place_ref, list_ref, cells_ref, blocks_ref, near_ref, ends_ref, table, ready)
 
 
@@ -223,7 +221,9 @@
             at = list_ref[k, own] - first
             return table[jnp.where(at < 0, at + HALO, jnp.where(at >= leaves, at - leaves + HALO, zero))]
 
-        edge_ref[:, i * leaf : (i + 1) * leaf] = near_rows(pick, lambda k: ends_ref[i, k])
+        values = jnp.concatenate([pick(k) for k in range(NEAR)], axis=1)
+        blocks = jnp.concatenate([ends_ref[i, k] for k in range(NEAR)], axis=1)
+        edge_ref[:, i * leaf : (i + 1) * leaf] = halves_sum(dot_tt(values, blocks))
 
 
 def near_part(c, clusters, near_ref, edge_ref):
@@ -247,7 +247,7 @@
 
 
 def second_kernel(
-    parity_ref, top_ref, table_ref, smat_ref, turned_ref, fold_ref, nugget_ref, field_ref, near_ref, edge_ref,
+    place_ref, top_ref, table_ref, smat_ref, turned_ref, fold_ref, nugget_ref, field_ref, near_ref, edge_ref,
     chunk_ref, image_ref, cells_ref, inner_ref, outer_ref,
 ):
     clusters, _, span = fold_ref.shape
@@ -260,10 +260,9 @@
         image_ref[:, at] = image
         both = split(image)
         cells_ref[:, at] = both
-        up = dot_tt(both, fold_ref[c])
-        parts.append(up[:rhs] + up[rhs:])
+        parts.append(halves_sum(dot_tt(both, fold_ref[c])))
     put_chunk(chunk_ref, parts)
-    put_halo(parity_ref[0], cells_ref[...], inner_ref, outer_ref)
+    put_halo(place_ref[1], cells_ref, inner_ref, outer_ref)
 
 
 def third_kernel(
@@ -287,17 +286,13 @@
     rest = field - own * image
     bent = image - own * twice
     sums = [
-        own,
         dot(field, field),
         cross,
+        size,
         dot(rest, rest),
-        dot(rest, image),
-        size,
         dot(rest, bent),
         dot(image, bent) + dot(rest, twice),
         dot(image, twice),
-        dot(field, bent),
-        dot(field, twice),
     ]
     width = sums_ref.shape[2]
     lane = lax.broadcasted_iota(jnp.int32, (rhs, width), 1)
@@ -319,16 +314,16 @@
     def total(value):
         return jnp.sum(value, axis=0, keepdims=True)
 
-    norm = total(part(1))
-    curve = total(part(2))
+    norm = total(part(0))
+    curve = total(part(1))
     alpha = norm / curve
-    delta = part(0) - alpha
-    norm_next = total(part(3) + delta * (2 * part(4) + delta * part(5)))
+    size = part(2)
+    delta = part(1) / jnp.where(size > 0, size, 1.0) - alpha
+    norm_next = total(part(3) + delta * delta * size)
     beta = norm_next / norm
-    rest_bent = total(part(6) + delta * (part(7) + delta * part(8)))
-    rest_image = total(part(4) + delta * part(5))
-    field_bent = total(part(9) + delta * part(10))
-    curve_next = rest_bent + beta * (rest_image + field_bent + beta * curve)
+    rest_bent = total(part(4) + delta * (part(5) + delta * part(6)))
+    rest_image = total(delta * size)
+    curve_next = rest_bent + beta * (2.0 * rest_image + beta * curve)
     alpha_next = norm_next / curve_next
     eye = lax.broadcasted_iota(jnp.int32, (rhs, rhs), 0) == lax.broadcasted_iota(jnp.int32, (rhs, rhs), 1)
 
@@ -366,12 +361,6 @@
     clusters = coupling.shape[0]
     span = leaf * LEAF_CL
     devices = lax.axis_size("group") * lax.axis_size("dev")
-    place = lax.axis_index("dev")
-    parity = place % 2
-    first = (lax.axis_index("group") * lax.axis_size("dev") + place) * leaves
-    parity = parity.reshape(1).astype(jnp.int32)
-    place = jnp.stack([first, parity[0]]).astype(jnp.int32)
-    near_list = near_list.T
     nugget = nugget[None]
     chunk_shape = struct((devices, clusters // 2, rhs, 2 * rank), jnp.bfloat16)
     end = HALO * leaf
@@ -380,22 +369,31 @@
     fold_shape = pltpu.VMEM((clusters, rank, span), jnp.bfloat16)
     end_shape = pltpu.HBM((2 * rhs, end), jnp.bfloat16)
 
-    chunk, fold, cells, inner, outer = pl.pallas_call(
+    chunk, fold, cells, inner, outer, place, near_list, top_list = pl.pallas_call(
         first_kernel,
-        in_specs=[SMEM] + [HBM] * 3,
-        out_specs=[VMEM] * 5,
-        out_shape=[chunk_shape, fold_shape, cells_shape, end_shape, end_shape],
+        in_specs=[HBM] * 5,
+        out_specs=[VMEM] * 5 + [SMEM] * 3,
+        out_shape=[
+            chunk_shape,
+            fold_shape,
+            cells_shape,
+            end_shape,
+            end_shape,
+            pltpu.SMEM((2,), jnp.int32),
+            pltpu.SMEM(near_list.T.shape, near_list.dtype),
+            pltpu.SMEM(top_list.shape, top_list.dtype),
+        ],
         scratch_shapes=[
             pltpu.VMEM(right_side.shape, right_side.dtype),
             pltpu.VMEM(basis.shape, basis.dtype),
             pltpu.VMEM(transfer.shape, transfer.dtype),
             pltpu.VMEM((leaves * rank // 2, 2 * rank), jnp.float32),
             pltpu.VMEM((leaves, rank, 2 * rank), jnp.float32),
-            pltpu.SemaphoreType.DMA((3,)),
+            pltpu.SemaphoreType.DMA((5,)),
         ],
         compiler_params=PARAMS,
         name="first",
-    )(parity, *in_hbm(right_side, basis, transfer))
+    )(*in_hbm(right_side, basis, transfer, near_list.T, top_list))
     table = exchange(chunk).reshape(-1, rhs, 2 * rank)
     ends_shape = pltpu.VMEM((2 * HALO,) + near_blocks.shape[1:], near_blocks.dtype)
     near_scratch = [
@@ -403,7 +401,7 @@
         pltpu.VMEM(near_blocks.shape, near_blocks.dtype),
     ]
 
-    def edge_product(near_list, inner, outer, ends):
+    def edge_product(inner, outer, ends):
         return pl.pallas_call(
             functools.partial(edge_kernel, leaves),
             in_specs=[SMEM] * 2 + [VMEM] * 3,
@@ -414,29 +412,26 @@
             name="edge",
         )(place, near_list, *swap_ends(inner, outer), ends)
 
-    near, ends, smat, turned, near_list = pl.pallas_call(
+    near, ends, smat, turned = pl.pallas_call(
         prepare_kernel,
-        in_specs=[SMEM] + [VMEM] * 2 + [HBM] * 4,
-        out_specs=[VMEM] * 5,
+        in_specs=[SMEM] * 3 + [VMEM] * 2 + [HBM] * 2,
+        out_specs=[VMEM] * 4,
         out_shape=[
             field_shape,
             ends_shape,
             pltpu.VMEM((clusters, rank, TOPK * 2 * rank), jnp.bfloat16),
             fold_shape,
-            pltpu.VMEM(near_list.shape, near_list.dtype),
         ],
         scratch_shapes=near_scratch
         + [
             pltpu.VMEM(coupling.shape, coupling.dtype),
             pltpu.VMEM((rank // 2 * TOPK, 2 * rank), jnp.float32),
-            pltpu.SMEM(top_list.shape, top_list.dtype),
-            pltpu.SMEM(near_list.shape, near_list.dtype),
-            pltpu.SemaphoreType.DMA((6,)),
+            pltpu.SemaphoreType.DMA((1 + PARTS,)),
         ],
         compiler_params=PARAMS,
         name="prepare",
-    )(place, cells, fold, *in_hbm(top_list, near_list, coupling, near_blocks))
-    edge = edge_product(near_list, inner, outer, ends)
+    )(place, near_list, top_list, cells, fold, *in_hbm(coupling, near_blocks))
+    edge = edge_product(inner, outer, ends)
 
     chunk, image, cells, inner, outer = pl.pallas_call(
         second_kernel,
@@ -445,24 +440,24 @@
         out_shape=[chunk_shape, field_shape, cells_shape, end_shape, end_shape],
         compiler_params=PARAMS,
         name="second",
-    )(parity, top_list, table, smat, turned, fold, nugget, right_side, near, edge)
+    )(place, top_list, table, smat, turned, fold, nugget, right_side, near, edge)
     table = exchange(chunk).reshape(-1, rhs, 2 * rank)
     near, ends = pl.pallas_call(
         near_kernel,
         in_specs=[SMEM] * 2 + [VMEM, HBM],
         out_specs=[VMEM] * 2,
         out_shape=[field_shape, ends_shape],
-        scratch_shapes=near_scratch + [pltpu.SemaphoreType.DMA((3,))],
+        scratch_shapes=near_scratch + [pltpu.SemaphoreType.DMA((PARTS,))],
         compiler_params=PARAMS,
         name="near",
     )(place, near_list, cells, *in_hbm(near_blocks))
-    edge = edge_product(near_list, inner, outer, ends)
+    edge = edge_product(inner, outer, ends)
 
     twice, sums = pl.pallas_call(
         third_kernel,
         in_specs=[SMEM] + [VMEM] * 8,
         out_specs=[VMEM] * 2,
-        out_shape=[field_shape, struct((devices, 1, 256), jnp.float32)],
+        out_shape=[field_shape, struct((devices, 1, 8 * rhs), jnp.float32)],
         compiler_params=PARAMS,
         name="third",
     )(top_list, table, smat, turned, nugget, right_side, image, near, edge)

time: 49.8 us -> 47.2 us (0.948)
  Pallas kernels: 17.2 us -> 12.6 us
  waiting for transfers between devices: 8.81 us -> 12.4 us
  blocking collectives: 10.1 us -> 9.42 us
  starting transfers between devices: 12.4 us -> 11.8 us
    all_to_all x2, waiting for transfers between devices: 8.8 us -> 12.4 us  [exchange(): return lax.all_to_all(chunk, AXES, 0, 0)]
    pallas_call x1, Pallas kernels: 3.91 us -> 2.64 us  [per_device(): pl.pallas_call(near_kernel, in_specs=[SMEM] * 2 + [VMEM, HBM], out_specs=...]
    pallas_call x2, Pallas kernels: 1.98 us -> 0.85 us  [edge_product(): pl.pallas_call(functools.partial(edge_kernel, leaves), in_specs=[SMEM] *...]
    pallas_call x2, Pallas kernels: 6.79 us -> 5.76 us  [the longest x1 2.96 us: per_device(): pl.pallas_call(prepare_kernel, in_specs=[SMEM] * 3 + [VMEM] * 2 + [HBM] *...]
    all_to_all x1, blocking collectives: 10.1 us -> 9.42 us  [exchange(): return lax.all_to_all(chunk, AXES, 0, 0)]
    pallas_call x1, Pallas kernels: 1.25 us -> 0.66 us  [per_device(): pl.pallas_call(third_kernel, in_specs=[SMEM] + [VMEM] * 8, out_specs=[VME...]
    pallas_call x1, Pallas kernels: 2.09 us -> 1.51 us  [per_device(): pl.pallas_call(second_kernel, in_specs=[SMEM] * 2 + [VMEM] * 8, out_specs...]
    all_to_all x2, starting transfers between devices: 10.4 us -> 9.89 us  [exchange(): return lax.all_to_all(chunk, AXES, 0, 0)]
  transfers between devices with their start and end apart: 6 -> 6, of which waited for: 2 -> 2; matrix products, arithmetic and copies ran while one was open for 0% -> 0% of each run, Pallas kernels for 20% -> 14%
where the time goes in v5:
time: 47.2 us; the launch traced here: 46.9 us
  Pallas kernels  12.6 us (27%)
  waiting for transfers between devices  12.4 us (26%)
  starting transfers between devices  11.8 us (25%)
  blocking collectives  9.42 us (20%)
  between operations  0.75 us (2%)
    all_to_all x2, waiting for transfers between devices, exchange(): return lax.all_to_all(chunk, AXES, 0, 0)  12.4 us
    all_to_all x2, starting transfers between devices, exchange(): return lax.all_to_all(chunk, AXES, 0, 0)  9.89 us
    all_to_all x1, blocking collectives, exchange(): return lax.all_to_all(chunk, AXES, 0, 0)  9.42 us
    pallas_call x1, Pallas kernels, per_device(): pl.pallas_call(prepare_kernel, in_specs=[SMEM] * 3 + [VMEM] * 2 + [HBM] *...  2.96 us
    pallas_call x1, Pallas kernels, per_device(): pl.pallas_call(first_kernel, in_specs=[HBM] * 5, out_specs=[VMEM] * 5 + [...  2.8 us
    pallas_call x1, Pallas kernels, per_device(): pl.pallas_call(near_kernel, in_specs=[SMEM] * 2 + [VMEM, HBM], out_specs=...  2.64 us
    pallas_call x1, Pallas kernels, per_device(): pl.pallas_call(second_kernel, in_specs=[SMEM] * 2 + [VMEM] * 8, out_specs...  1.51 us
    ppermute x2, starting transfers between devices, swap_ends(): outer = lax.ppermute(outer, 'dev', pairs + [(b, a) for a, b in pairs])  1.3 us
  transfers between devices with their start and end apart: 6, of which 2 were waited for; matrix products, arithmetic and copies ran while one was open for 0% of the time, Pallas kernels for 14%

profile of v5, /device:TPU:0, one launch (start us, length us, event | category | flops | bytes accessed | tf_op | source)
XLA Modules:
  0.0 46.9 jit_solution(7061127465076029427)
XLA Ops:
  0.6 0.0 copy-start
  0.6 0.0 copy-start.1
  0.7 2.8 %first.1 = (bf16[32,2,16,128]{3,2,1,0:T(8,128)(2,1)}, bf16[4,64,1024]{2,1,0:T(8,128)(2,1)S(1)}, bf16[32,4096]{1,0:T(8,128)(2,1)S(1)}, bf16[32,512]{1,0:T(8,128)(...) custom-call(f32[16,4096]{1,0:T(8,128)} %field_ref.5, ...), custom_call_target="tpu_custom_call" | custom-call | tf_op jit(solution)/shard_map/first/pallas_call | solution.py:372
  3.5 7.3 %all-to-all-start = ((bf16[32,2,16,128]{3,2,1,0:T(8,128)(2,1)}), bf16[32,2,16,128]{3,2,1,0:T(8,128)(2,1)S(1)}, u32[]{:S(2)}, u32[]{:S(2)}) async-start(bf16[32,2,16,128]{3,2,1,0:T(8,128)(2,1)} %get-tuple-element.25), calls=%async_computation | async-start | bytes 524288 | tf_op jit(solution)/shard_map/all_to_all | solution.py:343
  10.8 0.3 collective-permute-start
  11.1 0.7 %collective-permute-start.1 = (bf16[32,512]{1,0:T(8,128)(2,1)}, bf16[32,512]{1,0:T(8,128)(2,1)S(1)}, u32[]{:S(2)}, u32[]{:S(2)}) collective-permute-start(bf16[32,512]{1,0:T(8,128)(2,1)} %get-tuple-element.33), channel_id=1, source_target_pairs={{1,2},{3,4},{5,6},{2,1},{4,3},{6,5},{9,10},{11,12},{13,14},{10,9},... | collective-permute-start | bytes 98312 | tf_op jit(solution)/shard_map/ppermute | solution.py:354
  11.7 3.0 %prepare.1 = (f32[16,4096]{1,0:T(8,128)S(1)}, bf16[8,4,128,128]{3,2,1,0:T(8,128)(2,1)S(1)}, bf16[4,64,2048]{2,1,0:T(8,128)(2,1)S(1)}, bf16[4,64,1024]{2,1,0:T(8,128)(2,1)S(1)}) custom-call(s32[2]{0:T(128)S(4)} %get-tuple-element.24.place_ref, s32[4,32]{1,0:T(4,128)S(4)} %get-tuple-element.26.list_ref, s32[4,16]{1,0:T(4,128)S(4)} %get-tuple-element.23.top_ref, ...), custom_call_target="tpu_custom_call" | custom-call | tf_op jit(solution)/shard_map/prepare/pallas_call | solution.py:415
  14.7 0.0 collective-permute-done.inner_ref
  14.7 0.0 collective-permute-done.1.outer_ref
  14.7 0.4 edge.2.edge_ref
  15.2 6.0 %all-to-all-done = bf16[32,2,16,128]{3,2,1,0:T(8,128)(2,1)S(1)} async-done(((bf16[32,2,16,128]{3,2,1,0:T(8,128)(2,1)}), bf16[32,2,16,128]{3,2,1,0:T(8,128)(2,1)S(1)}, u32[]{:S(2)}, u32[]{:S(2)}) %all-to-all-start) | async-done | bytes 262176 | tf_op jit(solution)/shard_map/all_to_all | solution.py:343
  21.2 0.0 copy-done
  21.2 0.0 copy-done.1
  21.2 1.5 %second.1 = (bf16[32,2,16,128]{3,2,1,0:T(8,128)(2,1)}, f32[16,4096]{1,0:T(8,128)S(1)}, bf16[32,4096]{1,0:T(8,128)(2,1)S(1)}, bf16[32,512]{1,0:T(8,128)(2,1)}, bf16[32,512]{1,0:T(8,128)(2,1)}) custom-call(s32[2]{0:T(128)S(4)} %get-tuple-element.24.place_ref, s32[4,16]{1,0:T(4,128)S(4)} %get-tuple-element.23.top_ref, bf16[64,16,128]{2,1,0:T(8,128)(2,1)S(1)} %bitcast.5, ...), custom_call_target="tpu_custom_call" | custom-call | tf_op jit(solution)/shard_map/second/pallas_call | solution.py:436
  22.7 2.6 %all-to-all-start.1 = ((bf16[32,2,16,128]{3,2,1,0:T(8,128)(2,1)}), bf16[32,2,16,128]{3,2,1,0:T(8,128)(2,1)S(1)}, u32[]{:S(2)}, u32[]{:S(2)}) async-start(bf16[32,2,16,128]{3,2,1,0:T(8,128)(2,1)} %get-tuple-element.35), calls=%async_computation.1 | async-start | bytes 524288 | tf_op jit(solution)/shard_map/all_to_all | solution.py:343
  25.3 0.3 collective-permute-start.2
  25.5 0.7 %collective-permute-start.3 = (bf16[32,512]{1,0:T(8,128)(2,1)}, bf16[32,512]{1,0:T(8,128)(2,1)S(1)}, u32[]{:S(2)}, u32[]{:S(2)}) collective-permute-start(bf16[32,512]{1,0:T(8,128)(2,1)} %get-tuple-element.40), channel_id=1, source_target_pairs={{1,2},{3,4},{5,6},{2,1},{4,3},{6,5},{9,10},{11,12},{13,14},{10,9},... | collective-permute-start | bytes 98312 | tf_op jit(solution)/shard_map/ppermute | solution.py:354
  26.2 2.6 %near.1 = (f32[16,4096]{1,0:T(8,128)S(1)}, bf16[8,4,128,128]{3,2,1,0:T(8,128)(2,1)S(1)}) custom-call(s32[2]{0:T(128)S(4)} %get-tuple-element.24.place_ref, s32[4,32]{1,0:T(4,128)S(4)} %get-tuple-element.26.list_ref, bf16[32,4096]{1,0:T(8,128)(2,1)S(1)} %get-tuple-element.37.cells_ref, bf16[32,4,128,128]{3,2,1,0:T(8,128)(2,1)} %blocks_hbm.3), custom_call_target="tpu_custom_call" | custom-call | tf_op jit(solution)/shard_map/near/pallas_call | solution.py:445
  28.8 0.0 collective-permute-done.2.inner_ref
  28.8 0.0 collective-permute-done.3.outer_ref
  28.9 0.4 edge.3.edge_ref
  29.3 6.4 %all-to-all-done.1 = bf16[32,2,16,128]{3,2,1,0:T(8,128)(2,1)S(1)} async-done(((bf16[32,2,16,128]{3,2,1,0:T(8,128)(2,1)}), bf16[32,2,16,128]{3,2,1,0:T(8,128)(2,1)S(1)}, u32[]{:S(2)}, u32[]{:S(2)}) %all-to-all-start.1) | async-done | bytes 262176 | tf_op jit(solution)/shard_map/all_to_all | solution.py:343
  35.6 0.7 %third.1 = (f32[16,4096]{1,0:T(8,128)S(1)}, f32[32,1,128]{2,1,0:T(1,128)S(1)}) custom-call(s32[4,16]{1,0:T(4,128)S(4)} %get-tuple-element.23.top_ref, bf16[64,16,128]{2,1,0:T(8,128)(2,1)S(1)} %bitcast.4, bf16[4,64,2048]{2,1,0:T(8,128)(2,1)S(1)} %get-tuple-element.29.smat_ref, bf16[4,64,1024]{2,1,0:T(8,128)(2,1)S(1)} %get-tuple-element.30.turned_ref, ...), custom_call_target="tpu_custom_call" | custom-call | tf_op jit(solution)/shard_map/third/pallas_call | solution.py:456
  36.3 9.4 %all_to_all.15.sums_ref = f32[32,1,128]{2,1,0:T(1,128)S(1)} all-to-all(f32[32,1,128]{2,1,0:T(1,128)S(1)} %get-tuple-element.42), channel_id=1, replica_groups=mesh['group'=4,'dev'=8] {'group','dev'}, dimensions={0} | all-to-all | bytes 32768 | tf_op jit(solution)/shard_map/all_to_all | solution.py:343
  45.7 1.2 %last.1 = (f32[16,4096]{1,0:T(8,128)}, f32[16,4096]{1,0:T(8,128)}) custom-call(f32[32,1,128]{2,1,0:T(1,128)S(1)} %all_to_all.15.sums_ref, f32[16,4096]{1,0:T(8,128)S(1)} %copy-done, f32[16,4096]{1,0:T(8,128)S(1)} %get-tuple-element.36.image_ref, f32[16,4096]{1,0:T(8,128)S(1)} %get-tuple-element.43.twice_ref), custom_call_target="tpu_custom_call" | custom-call | tf_op jit(solution)/shard_map/last/pallas_call | solution.py:466
Async XLA Ops:
  0.6 20.5 %copy-start = (f32[16,4096]{1,0:T(8,128)S(1)}, f32[16,4096]{1,0:T(8,128)}, u32[]{:S(2)}) copy-start(f32[16,4096]{1,0:T(8,128)} %field_ref.5) | copy-start | bytes 786436
  0.6 20.5 %copy-start.1 = (f32[4096]{0:T(1024)S(1)}, f32[4096]{0:T(1024)}, u32[]{:S(2)}) copy-start(f32[4096]{0:T(1024)} %param.9) | copy-start | bytes 49156
  3.5 17.7 %all-to-all-start = ((bf16[32,2,16,128]{3,2,1,0:T(8,128)(2,1)}), bf16[32,2,16,128]{3,2,1,0:T(8,128)(2,1)S(1)}, u32[]{:S(2)}, u32[]{:S(2)}) async-start(bf16[32,2,16,128]{3,2,1,0:T(8,128)(2,1)} %get-tuple-element.25), calls=%async_computation | async-start | bytes 524288 | tf_op jit(solution)/shard_map/all_to_all | solution.py:343
  10.8 3.9 %collective-permute-start = (bf16[32,512]{1,0:T(8,128)(2,1)}, bf16[32,512]{1,0:T(8,128)(2,1)S(1)}, u32[]{:S(2)}, u32[]{:S(2)}) collective-permute-start(bf16[32,512]{1,0:T(8,128)(2,1)} %get-tuple-element.32), channel_id=1, source_target_pairs={{0,1},{1,0},{2,3},{3,2},{4,5},{5,4},{6,7},{7,6},{8,9},{9,8},{10,11... | collective-permute-start | bytes 98312 | tf_op jit(solution)/shard_map/ppermute | solution.py:347
  11.1 3.6 %collective-permute-start.1 = (bf16[32,512]{1,0:T(8,128)(2,1)}, bf16[32,512]{1,0:T(8,128)(2,1)S(1)}, u32[]{:S(2)}, u32[]{:S(2)}) collective-permute-start(bf16[32,512]{1,0:T(8,128)(2,1)} %get-tuple-element.33), channel_id=1, source_target_pairs={{1,2},{3,4},{5,6},{2,1},{4,3},{6,5},{9,10},{11,12},{13,14},{10,9},... | collective-permute-start | bytes 98312 | tf_op jit(solution)/shard_map/ppermute | solution.py:354
  22.7 13.0 %all-to-all-start.1 = ((bf16[32,2,16,128]{3,2,1,0:T(8,128)(2,1)}), bf16[32,2,16,128]{3,2,1,0:T(8,128)(2,1)S(1)}, u32[]{:S(2)}, u32[]{:S(2)}) async-start(bf16[32,2,16,128]{3,2,1,0:T(8,128)(2,1)} %get-tuple-element.35), calls=%async_computation.1 | async-start | bytes 524288 | tf_op jit(solution)/shard_map/all_to_all | solution.py:343
  25.3 3.6 %collective-permute-start.2 = (bf16[32,512]{1,0:T(8,128)(2,1)}, bf16[32,512]{1,0:T(8,128)(2,1)S(1)}, u32[]{:S(2)}, u32[]{:S(2)}) collective-permute-start(bf16[32,512]{1,0:T(8,128)(2,1)} %get-tuple-element.39), channel_id=1, source_target_pairs={{0,1},{1,0},{2,3},{3,2},{4,5},{5,4},{6,7},{7,6},{8,9},{9,8},{10,11... | collective-permute-start | bytes 98312 | tf_op jit(solution)/shard_map/ppermute | solution.py:347
  25.5 3.3 %collective-permute-start.3 = (bf16[32,512]{1,0:T(8,128)(2,1)}, bf16[32,512]{1,0:T(8,128)(2,1)S(1)}, u32[]{:S(2)}, u32[]{:S(2)}) collective-permute-start(bf16[32,512]{1,0:T(8,128)(2,1)} %get-tuple-element.40), channel_id=1, source_target_pairs={{1,2},{3,4},{5,6},{2,1},{4,3},{6,5},{9,10},{11,12},{13,14},{10,9},... | collective-permute-start | bytes 98312 | tf_op jit(solution)/shard_map/ppermute | solution.py:354

commit v6 on v5

--- a/solution.py
+++ b/solution.py
@@ -52,22 +52,25 @@
     return jnp.concatenate([high, low], axis=0)
 
 
-def put_chunk(chunk_ref, parts):
+def send_chunk(chunk_hbm, chunk_ref, sem, parts):
     for at in range(len(parts) // 2):
         pair = jnp.concatenate(parts[2 * at : 2 * at + 2], axis=1).astype(jnp.bfloat16)
         chunk_ref[:, at] = jnp.broadcast_to(pair[None], (chunk_ref.shape[0],) + pair.shape)
-
-
-def put_halo(parity, cells_ref, inner_ref, outer_ref):
+    copy = pltpu.make_async_copy(chunk_ref, chunk_hbm, sem.at[0])
+    copy.start()
+    return copy
+
+
+def put_halo(core, field_ref, inner_ref, outer_ref):
     span = inner_ref.shape[1]
-    head, tail = cells_ref[:, :span], cells_ref[:, cells_ref.shape[1] - span :]
-
-    @pl.when(parity == 0)
+    head, tail = split(field_ref[:, :span]), split(field_ref[:, field_ref.shape[1] - span :])
+
+    @pl.when(core == 0)
     def _():
         inner_ref[...] = tail
         outer_ref[...] = head
 
-    @pl.when(parity != 0)
+    @pl.when(core != 0)
     def _():
         inner_ref[...] = head
         outer_ref[...] = tail
@@ -75,8 +78,8 @@
 
 def first_kernel(
     field_hbm, basis_hbm, transfer_hbm, list_hbm, top_hbm,
-    chunk_ref, fold_ref, cells_ref, inner_ref, outer_ref, place_ref, list_ref, top_ref,
-    field_ref, basis_ref, transfer_ref, rows_ref, emat_ref, sem,
+    chunk_hbm, field_ref, fold_ref, inner_ref, outer_ref, place_ref, list_ref, top_ref,
+    chunk_ref, chunk_sem, basis_ref, transfer_ref, rows_ref, emat_ref, sem,
 ):
     clusters, rank, span = fold_ref.shape
     leaves, _, leaf = basis_ref.shape
@@ -105,7 +108,6 @@
     copies[1].wait()
     copies[2].wait()
     cells = split(field_ref[...])
-    cells_ref[...] = cells
     folds = []
     for c in range(clusters):
         tiles = []
@@ -116,17 +118,19 @@
             )
             tiles.append(fold.astype(jnp.bfloat16))
         folds.append(jnp.concatenate(tiles, axis=1))
-        fold_ref[c] = folds[c]
     parts = [halves_sum(dot_tt(cells[:, c * span : (c + 1) * span], fold)) for c, fold in enumerate(folds)]
-    put_chunk(chunk_ref, parts)
-    put_halo(device % 2, cells_ref, inner_ref, outer_ref)
+    sent = send_chunk(chunk_hbm, chunk_ref, chunk_sem, parts)
+    for c, fold in enumerate(folds):
+        fold_ref[c] = fold
+    put_halo(device % 2, field_ref, inner_ref, outer_ref)
     copies[3].wait()
     copies[4].wait()
+    sent.wait()
 
 
 def prepare_kernel(
-    place_ref, list_ref, top_ref, cells_ref, fold_ref, coupling_hbm, blocks_hbm,
-    near_ref, ends_ref, smat_ref, turned_ref, table, blocks_ref, coupling_ref, rows_ref, sem
+    place_ref, list_ref, top_ref, field_ref, fold_ref, coupling_hbm, blocks_hbm,
+    near_ref, ends_ref, smat_ref, turned_ref, gram_ref, table, blocks_ref, coupling_ref, rows_ref, sem
 ):
     pairs, each = part_copies(blocks_hbm, blocks_ref)
     copies = load_all([(coupling_hbm, coupling_ref)] + pairs, sem)
@@ -136,7 +140,9 @@
     column = lax.broadcasted_iota(jnp.int32, (rank, rank), 1)
     order = (column == 2 * (row % half) + row // half).astype(jnp.bfloat16)
     for c in range(clusters):
-        turned_ref[c] = dot_nn(order, fold_ref[c]).astype(jnp.bfloat16)
+        turned = dot_nn(order, fold_ref[c]).astype(jnp.bfloat16)
+        turned_ref[c] = turned
+        gram_ref[c] = dot_tt(turned, fold_ref[c]).astype(jnp.bfloat16)
     copies[0].wait()
     lower = lax.broadcasted_iota(jnp.int32, (half, 2 * rank), 1) < rank
     for c in range(clusters):
@@ -152,7 +158,7 @@
             at = slice(k * 2 * rank, (k + 1) * 2 * rank)
             smat_ref[c, :, at] = jnp.concatenate([even, odd], axis=0).astype(jnp.bfloat16)
     ready = wait_parts(copies[1:], each)
-    near_sum(place_ref, list_ref, cells_ref, blocks_ref, near_ref, ends_ref, table, ready)
+    near_sum(place_ref, list_ref, field_ref, blocks_ref, near_ref, ends_ref, table, ready)
 
 
 def halves_sum(total):
@@ -160,10 +166,10 @@
     return total[:rhs] + total[rhs:]
 
 
-def near_sum(place_ref, list_ref, cells_ref, blocks_ref, near_ref, ends_ref, table, ready):
+def near_sum(place_ref, list_ref, field_ref, blocks_ref, near_ref, ends_ref, table, ready):
     leaves, _, leaf, _ = blocks_ref.shape
     for i in range(leaves):
-        table[i] = cells_ref[:, i * leaf : (i + 1) * leaf]
+        table[i] = split(field_ref[:, i * leaf : (i + 1) * leaf])
     table[leaves] = jnp.zeros(table.shape[1:], table.dtype)
     first = place_ref[0]
     for i in range(leaves):
@@ -198,11 +204,11 @@
 
 
 def near_kernel(
-    place_ref, list_ref, cells_ref, blocks_hbm, near_ref, ends_ref, table, blocks_ref, sem
+    place_ref, list_ref, field_ref, blocks_hbm, near_ref, ends_ref, table, blocks_ref, sem
 ):
     pairs, each = part_copies(blocks_hbm, blocks_ref)
     ready = wait_parts(load_all(pairs, sem), each)
-    near_sum(place_ref, list_ref, cells_ref, blocks_ref, near_ref, ends_ref, table, ready)
+    near_sum(place_ref, list_ref, field_ref, blocks_ref, near_ref, ends_ref, table, ready)
 
 
 def edge_kernel(leaves, place_ref, list_ref, inner_ref, outer_ref, ends_ref, edge_ref, table):
@@ -238,31 +244,31 @@
     return near
 
 
-def far_parts(top_ref, table_ref, smat_ref, turned_ref):
+def down_parts(top_ref, table_ref, smat_ref):
     downs = []
-    for c in range(turned_ref.shape[0]):
+    for c in range(smat_ref.shape[0]):
         tiles = [table_ref[top_ref[c, k] >> 1] for k in range(TOPK)]
         downs.append(dot_tt(jnp.concatenate(tiles, axis=1), smat_ref[c]).astype(jnp.bfloat16))
-    return [dot_nn(down, turned_ref[c]) for c, down in enumerate(downs)]
+    return downs
 
 
 def second_kernel(
-    place_ref, top_ref, table_ref, smat_ref, turned_ref, fold_ref, nugget_ref, field_ref, near_ref, edge_ref,
-    chunk_ref, image_ref, cells_ref, inner_ref, outer_ref,
+    place_ref, top_ref, table_ref, smat_ref, turned_ref, gram_ref, fold_ref, nugget_ref, field_ref, near_ref, edge_ref,
+    chunk_hbm, image_ref, inner_ref, outer_ref, chunk_ref, sem,
 ):
     clusters, _, span = fold_ref.shape
-    rhs = field_ref.shape[0]
-    parts = []
-    fars = far_parts(top_ref, table_ref, smat_ref, turned_ref)
-    for c, far in enumerate(fars):
-        at = slice(c * span, (c + 1) * span)
-        image = nugget_ref[:, at] * field_ref[:, at] + near_part(c, clusters, near_ref, edge_ref) + far
-        image_ref[:, at] = image
-        both = split(image)
-        cells_ref[:, at] = both
-        parts.append(halves_sum(dot_tt(both, fold_ref[c])))
-    put_chunk(chunk_ref, parts)
-    put_halo(place_ref[1], cells_ref, inner_ref, outer_ref)
+    spans = [slice(c * span, (c + 1) * span) for c in range(clusters)]
+    downs = down_parts(top_ref, table_ref, smat_ref)
+    bases, parts = [], []
+    for c, at in enumerate(spans):
+        bases.append(nugget_ref[:, at] * field_ref[:, at] + near_part(c, clusters, near_ref, edge_ref))
+        parts.append(halves_sum(dot_tt(split(bases[c]), fold_ref[c])))
+    parts = [part + dot_nn(down, gram_ref[c]) for c, (part, down) in enumerate(zip(parts, downs))]
+    sent = send_chunk(chunk_hbm, chunk_ref, sem, parts)
+    for c, at in enumerate(spans):
+        image_ref[:, at] = bases[c] + dot_nn(downs[c], turned_ref[c])
+    put_halo(place_ref[1], image_ref, inner_ref, outer_ref)
+    sent.wait()
 
 
 def third_kernel(
@@ -271,8 +277,9 @@
 ):
     clusters, _, span = turned_ref.shape
     rhs = field_ref.shape[0]
-    for c, far in enumerate(far_parts(top_ref, table_ref, smat_ref, turned_ref)):
+    for c, down in enumerate(down_parts(top_ref, table_ref, smat_ref)):
         at = slice(c * span, (c + 1) * span)
+        far = dot_nn(down, turned_ref[c])
         near = near_part(c, clusters, near_ref, edge_ref)
         twice_ref[:, at] = nugget_ref[:, at] * image_ref[:, at] + near + far
 
@@ -306,37 +313,31 @@
 
 def last_kernel(sums_ref, field_ref, image_ref, twice_ref, solution_ref, residual_ref):
     rhs = field_ref.shape[0]
-    sums = sums_ref[...].reshape(sums_ref.shape[0], sums_ref.shape[2])
+    sums = sums_ref[...].reshape(sums_ref.shape[0], sums_ref.shape[2]).T
 
     def part(at):
-        return sums[:, at * rhs : (at + 1) * rhs]
+        return sums[at * rhs : (at + 1) * rhs]
 
     def total(value):
-        return jnp.sum(value, axis=0, keepdims=True)
+        return jnp.sum(value, axis=1, keepdims=True)
 
     norm = total(part(0))
     curve = total(part(1))
+    size = part(2)
+    own = part(1) / jnp.where(size > 0, size, 1.0)
     alpha = norm / curve
-    size = part(2)
-    delta = part(1) / jnp.where(size > 0, size, 1.0) - alpha
+    delta = own - alpha
     norm_next = total(part(3) + delta * delta * size)
-    beta = norm_next / norm
     rest_bent = total(part(4) + delta * (part(5) + delta * part(6)))
     rest_image = total(delta * size)
+    beta = norm_next / norm
     curve_next = rest_bent + beta * (2.0 * rest_image + beta * curve)
     alpha_next = norm_next / curve_next
-    eye = lax.broadcasted_iota(jnp.int32, (rhs, rhs), 0) == lax.broadcasted_iota(jnp.int32, (rhs, rhs), 1)
-
-    def column(value):
-        return jnp.sum(jnp.where(eye, value, 0.0), axis=1, keepdims=True)
-
-    alpha, beta, alpha_next = column(alpha), column(beta), column(alpha_next)
+    outer = alpha + alpha_next * (1.0 + beta)
+    inner = alpha * alpha_next
     field, image = field_ref[...], image_ref[...]
-    residual = field - alpha * image
-    direction = residual + beta * field
-    solution_ref[...] = alpha * field + alpha_next * direction
-    image_next = image - alpha * twice_ref[...] + beta * image
-    residual_ref[...] = residual - alpha_next * image_next
+    solution_ref[...] = outer * field - inner * image
+    residual_ref[...] = field - outer * image + inner * twice_ref[...]
 
 
 def exchange(chunk):
@@ -362,29 +363,29 @@
     span = leaf * LEAF_CL
     devices = lax.axis_size("group") * lax.axis_size("dev")
     nugget = nugget[None]
-    chunk_shape = struct((devices, clusters // 2, rhs, 2 * rank), jnp.bfloat16)
+    chunk_shape = pltpu.HBM((devices, clusters // 2, rhs, 2 * rank), jnp.bfloat16)
+    chunk_scratch = [pltpu.VMEM(chunk_shape.shape, jnp.bfloat16), pltpu.SemaphoreType.DMA((1,))]
     end = HALO * leaf
     field_shape = pltpu.VMEM((rhs, width), jnp.float32)
-    cells_shape = pltpu.VMEM((2 * rhs, width), jnp.bfloat16)
     fold_shape = pltpu.VMEM((clusters, rank, span), jnp.bfloat16)
-    end_shape = pltpu.HBM((2 * rhs, end), jnp.bfloat16)
-
-    chunk, fold, cells, inner, outer, place, near_list, top_list = pl.pallas_call(
+    end_shape = pltpu.VMEM((2 * rhs, end), jnp.bfloat16)
+
+    chunk, field, fold, inner, outer, place, near_list, top_list = pl.pallas_call(
         first_kernel,
         in_specs=[HBM] * 5,
-        out_specs=[VMEM] * 5 + [SMEM] * 3,
+        out_specs=[HBM] + [VMEM] * 4 + [SMEM] * 3,
         out_shape=[
             chunk_shape,
+            field_shape,
             fold_shape,
-            cells_shape,
             end_shape,
             end_shape,
             pltpu.SMEM((2,), jnp.int32),
             pltpu.SMEM(near_list.T.shape, near_list.dtype),
             pltpu.SMEM(top_list.shape, top_list.dtype),
         ],
-        scratch_shapes=[
-            pltpu.VMEM(right_side.shape, right_side.dtype),
+        scratch_shapes=chunk_scratch
+        + [
             pltpu.VMEM(basis.shape, basis.dtype),
             pltpu.VMEM(transfer.shape, transfer.dtype),
             pltpu.VMEM((leaves * rank // 2, 2 * rank), jnp.float32),
@@ -412,15 +413,16 @@
             name="edge",
         )(place, near_list, *swap_ends(inner, outer), ends)
 
-    near, ends, smat, turned = pl.pallas_call(
+    near, ends, smat, turned, gram = pl.pallas_call(
         prepare_kernel,
         in_specs=[SMEM] * 3 + [VMEM] * 2 + [HBM] * 2,
-        out_specs=[VMEM] * 4,
+        out_specs=[VMEM] * 5,
         out_shape=[
             field_shape,
             ends_shape,
             pltpu.VMEM((clusters, rank, TOPK * 2 * rank), jnp.bfloat16),
             fold_shape,
+            pltpu.VMEM((clusters, rank, rank), jnp.bfloat16),
         ],
         scratch_shapes=near_scratch
         + [
@@ -430,17 +432,18 @@
         ],
         compiler_params=PARAMS,
         name="prepare",
-    )(place, near_list, top_list, cells, fold, *in_hbm(coupling, near_blocks))
+    )(place, near_list, top_list, field, fold, *in_hbm(coupling, near_blocks))
     edge = edge_product(inner, outer, ends)
 
-    chunk, image, cells, inner, outer = pl.pallas_call(
+    chunk, image, inner, outer = pl.pallas_call(
         second_kernel,
-        in_specs=[SMEM] * 2 + [VMEM] * 8,
-        out_specs=[VMEM] * 5,
-        out_shape=[chunk_shape, field_shape, cells_shape, end_shape, end_shape],
+        in_specs=[SMEM] * 2 + [VMEM] * 9,
+        out_specs=[HBM] + [VMEM] * 3,
+        out_shape=[chunk_shape, field_shape, end_shape, end_shape],
+        scratch_shapes=chunk_scratch,
         compiler_params=PARAMS,
         name="second",
-    )(place, top_list, table, smat, turned, fold, nugget, right_side, near, edge)
+    )(place, top_list, table, smat, turned, gram, fold, nugget, field, near, edge)
     table = exchange(chunk).reshape(-1, rhs, 2 * rank)
     near, ends = pl.pallas_call(
         near_kernel,
@@ -450,7 +453,7 @@
         scratch_shapes=near_scratch + [pltpu.SemaphoreType.DMA((PARTS,))],
         compiler_params=PARAMS,
         name="near",
-    )(place, near_list, cells, *in_hbm(near_blocks))
+    )(place, near_list, image, *in_hbm(near_blocks))
     edge = edge_product(inner, outer, ends)
 
     twice, sums = pl.pallas_call(
@@ -460,7 +463,7 @@
         out_shape=[field_shape, struct((devices, 1, 8 * rhs), jnp.float32)],
         compiler_params=PARAMS,
         name="third",
-    )(top_list, table, smat, turned, nugget, right_side, image, near, edge)
+    )(top_list, table, smat, turned, nugget, field, image, near, edge)
     sums = exchange(sums)
 
     return pl.pallas_call(
@@ -470,7 +473,7 @@
         out_shape=[struct((rhs, width), jnp.float32)] * 2,
         compiler_params=PARAMS,
         name="last",
-    )(sums, right_side, image, twice)
+    )(sums, field, image, twice)
 
 
 def solution(mesh):

time: 47.2 us -> 47 us (level)
  no operation moved by 1% of the time
where the time goes in v6:
time: 47 us; the launch traced here: 46.6 us
  waiting for transfers between devices  12.4 us (26%)
  Pallas kernels  12.3 us (26%)
  starting transfers between devices  11.8 us (25%)
  blocking collectives  9.4 us (20%)
  between operations  0.75 us (2%)
    all_to_all x2, waiting for transfers between devices, exchange(): return lax.all_to_all(chunk, AXES, 0, 0)  12.4 us
    all_to_all x2, starting transfers between devices, exchange(): return lax.all_to_all(chunk, AXES, 0, 0)  9.9 us
    all_to_all x1, blocking collectives, exchange(): return lax.all_to_all(chunk, AXES, 0, 0)  9.4 us
    pallas_call x1, Pallas kernels, per_device(): pl.pallas_call(prepare_kernel, in_specs=[SMEM] * 3 + [VMEM] * 2 + [HBM] *...  2.96 us
    pallas_call x1, Pallas kernels, per_device(): pl.pallas_call(first_kernel, in_specs=[HBM] * 5, out_specs=[HBM] + [VMEM]...  2.75 us
    pallas_call x1, Pallas kernels, per_device(): pl.pallas_call(near_kernel, in_specs=[SMEM] * 2 + [VMEM, HBM], out_specs=...  2.64 us
    pallas_call x1, Pallas kernels, per_device(): pl.pallas_call(second_kernel, in_specs=[SMEM] * 2 + [VMEM] * 9, out_specs...  1.34 us
    ppermute x2, starting transfers between devices, swap_ends(): outer = lax.ppermute(outer, 'dev', pairs + [(b, a) for a, b in pairs])  1.3 us
  transfers between devices with their start and end apart: 6, of which 2 were waited for; matrix products, arithmetic and copies ran while one was open for 0% of the time, Pallas kernels for 14%

profile of v6, /device:TPU:0, one launch (start us, length us, event | category | flops | bytes accessed | tf_op | source)
XLA Modules:
  0.0 46.6 jit_solution(9958263118441025175)
XLA Ops:
  0.6 0.0 copy-start
  0.6 2.8 %first.1 = (bf16[32,2,16,128]{3,2,1,0:T(8,128)(2,1)}, f32[16,4096]{1,0:T(8,128)S(1)}, bf16[4,64,1024]{2,1,0:T(8,128)(2,1)S(1)}, bf16[32,512]{1,0:T(8,128)(2,1)S(...) custom-call(f32[16,4096]{1,0:T(8,128)} %field_hbm.1, ...), custom_call_target="tpu_custom_call" | custom-call | tf_op jit(solution)/shard_map/first/pallas_call | solution.py:373
  3.4 7.3 %all-to-all-start = ((bf16[32,2,16,128]{3,2,1,0:T(8,128)(2,1)}), bf16[32,2,16,128]{3,2,1,0:T(8,128)(2,1)S(1)}, u32[]{:S(2)}, u32[]{:S(2)}) async-start(bf16[32,2,16,128]{3,2,1,0:T(8,128)(2,1)} %get-tuple-element.25), calls=%async_computation | async-start | bytes 524288 | tf_op jit(solution)/shard_map/all_to_all | solution.py:344
  10.7 0.3 collective-permute-start
  11.0 0.7 %collective-permute-start.1 = (bf16[32,512]{1,0:T(8,128)(2,1)S(1)}, bf16[32,512]{1,0:T(8,128)(2,1)S(1)}, u32[]{:S(2)}, u32[]{:S(2)}) collective-permute-start(bf16[32,512]{1,0:T(8,128)(2,1)S(1)} %get-tuple-element.34), channel_id=1, source_target_pairs={{1,2},{3,4},{5,6},{2,1},{4,3},{6,5},{9,10},{11,12},{13,14},{10,9},... | collective-permute-start | bytes 98312 | tf_op jit(solution)/shard_map/ppermute | solution.py:355
  11.7 3.0 %prepare.1 = (f32[16,4096]{1,0:T(8,128)S(1)}, bf16[8,4,128,128]{3,2,1,0:T(8,128)(2,1)S(1)}, bf16[4,64,2048]{2,1,0:T(8,128)(2,1)S(1)}, bf16[4,64,1024]{2,1,0:T(8,128)(2,1)S(1)}, bf16[4,64,64]{2,1,0:T(8,128)(2,1)S(1)}) custom-call(s32[2]{0:T(128)S(4)} %get-tuple-element.24.place_ref, s32[4,32]{1,0:T(4,128)S(4)} %get-tuple-element.26.list_ref, ...), custom_call_target="tpu_custom_call" | custom-call | tf_op jit(solution)/shard_map/prepare/pallas_call | solution.py:416
  14.7 0.0 collective-permute-done.inner_ref
  14.7 0.0 collective-permute-done.1.outer_ref
  14.7 0.4 edge.2.edge_ref
  15.1 6.0 %all-to-all-done = bf16[32,2,16,128]{3,2,1,0:T(8,128)(2,1)S(1)} async-done(((bf16[32,2,16,128]{3,2,1,0:T(8,128)(2,1)}), bf16[32,2,16,128]{3,2,1,0:T(8,128)(2,1)S(1)}, u32[]{:S(2)}, u32[]{:S(2)}) %all-to-all-start) | async-done | bytes 262176 | tf_op jit(solution)/shard_map/all_to_all | solution.py:344
  21.1 0.0 copy-done
  21.1 1.3 %second.1 = (bf16[32,2,16,128]{3,2,1,0:T(8,128)(2,1)}, f32[16,4096]{1,0:T(8,128)S(1)}, bf16[32,512]{1,0:T(8,128)(2,1)S(1)}, bf16[32,512]{1,0:T(8,128)(2,1)S(1)}) custom-call(s32[2]{0:T(128)S(4)} %get-tuple-element.24.place_ref, s32[4,16]{1,0:T(4,128)S(4)} %get-tuple-element.23.top_ref, bf16[64,16,128]{2,1,0:T(8,128)(2,1)S(1)} %bitcast.4, ...), custom_call_target="tpu_custom_call" | custom-call | tf_op jit(solution)/shard_map/second/pallas_call | solution.py:438
  22.4 2.6 %all-to-all-start.1 = ((bf16[32,2,16,128]{3,2,1,0:T(8,128)(2,1)}), bf16[32,2,16,128]{3,2,1,0:T(8,128)(2,1)S(1)}, u32[]{:S(2)}, u32[]{:S(2)}) async-start(bf16[32,2,16,128]{3,2,1,0:T(8,128)(2,1)} %get-tuple-element.36), calls=%async_computation.1 | async-start | bytes 524288 | tf_op jit(solution)/shard_map/all_to_all | solution.py:344
  25.1 0.2 collective-permute-start.2
  25.3 0.7 %collective-permute-start.3 = (bf16[32,512]{1,0:T(8,128)(2,1)S(1)}, bf16[32,512]{1,0:T(8,128)(2,1)S(1)}, u32[]{:S(2)}, u32[]{:S(2)}) collective-permute-start(bf16[32,512]{1,0:T(8,128)(2,1)S(1)} %get-tuple-element.40), channel_id=1, source_target_pairs={{1,2},{3,4},{5,6},{2,1},{4,3},{6,5},{9,10},{11,12},{13,14},{10,9},... | collective-permute-start | bytes 98312 | tf_op jit(solution)/shard_map/ppermute | solution.py:355
  26.0 2.6 %near.1 = (f32[16,4096]{1,0:T(8,128)S(1)}, bf16[8,4,128,128]{3,2,1,0:T(8,128)(2,1)S(1)}) custom-call(s32[2]{0:T(128)S(4)} %get-tuple-element.24.place_ref, s32[4,32]{1,0:T(4,128)S(4)} %get-tuple-element.26.list_ref, f32[16,4096]{1,0:T(8,128)S(1)} %get-tuple-element.37.field_ref.image_ref, bf16[32,4,128,128]{3,2,1,0:T(8,128)(2,1)} %blocks_hbm.3), custom_call_target="tpu_custom_call" | custom-call | tf_op jit(solution)/shard_map/near/pallas_call | solution.py:448
  28.6 0.0 collective-permute-done.2.inner_ref
  28.6 0.0 collective-permute-done.3.outer_ref
  28.6 0.4 edge.3.edge_ref
  29.0 6.4 %all-to-all-done.1 = bf16[32,2,16,128]{3,2,1,0:T(8,128)(2,1)S(1)} async-done(((bf16[32,2,16,128]{3,2,1,0:T(8,128)(2,1)}), bf16[32,2,16,128]{3,2,1,0:T(8,128)(2,1)S(1)}, u32[]{:S(2)}, u32[]{:S(2)}) %all-to-all-start.1) | async-done | bytes 262176 | tf_op jit(solution)/shard_map/all_to_all | solution.py:344
  35.4 0.7 %third.1 = (f32[16,4096]{1,0:T(8,128)S(1)}, f32[32,1,128]{2,1,0:T(1,128)S(1)}) custom-call(s32[4,16]{1,0:T(4,128)S(4)} %get-tuple-element.23.top_ref, bf16[64,16,128]{2,1,0:T(8,128)(2,1)S(1)} %bitcast.5, bf16[4,64,2048]{2,1,0:T(8,128)(2,1)S(1)} %get-tuple-element.29.smat_ref, bf16[4,64,1024]{2,1,0:T(8,128)(2,1)S(1)} %get-tuple-element.30.turned_ref, ...), custom_call_target="tpu_custom_call" | custom-call | tf_op jit(solution)/shard_map/third/pallas_call | solution.py:459
  36.1 9.4 %all_to_all.15.sums_ref = f32[32,1,128]{2,1,0:T(1,128)S(1)} all-to-all(f32[32,1,128]{2,1,0:T(1,128)S(1)} %get-tuple-element.42), channel_id=1, replica_groups=mesh['group'=4,'dev'=8] {'group','dev'}, dimensions={0} | all-to-all | bytes 32768 | tf_op jit(solution)/shard_map/all_to_all | solution.py:344
  45.5 1.1 %last.1 = (f32[16,4096]{1,0:T(8,128)}, f32[16,4096]{1,0:T(8,128)}) custom-call(f32[32,1,128]{2,1,0:T(1,128)S(1)} %all_to_all.15.sums_ref, f32[16,4096]{1,0:T(8,128)S(1)} %get-tuple-element.27.field_ref, f32[16,4096]{1,0:T(8,128)S(1)} %get-tuple-element.37.field_ref.image_ref, f32[16,4096]{1,0:T(8,128)S(1)} %get-tuple-element.43.twice_ref), custom_call_target="tpu_custom_call" | custom-call | tf_op jit(solution)/shard_map/last/pallas_call | solution.py:469
Async XLA Ops:
  0.6 20.5 %copy-start = (f32[4096]{0:T(1024)S(1)}, f32[4096]{0:T(1024)}, u32[]{:S(2)}) copy-start(f32[4096]{0:T(1024)} %param.9) | copy-start | bytes 49156
  3.4 17.7 %all-to-all-start = ((bf16[32,2,16,128]{3,2,1,0:T(8,128)(2,1)}), bf16[32,2,16,128]{3,2,1,0:T(8,128)(2,1)S(1)}, u32[]{:S(2)}, u32[]{:S(2)}) async-start(bf16[32,2,16,128]{3,2,1,0:T(8,128)(2,1)} %get-tuple-element.25), calls=%async_computation | async-start | bytes 524288 | tf_op jit(solution)/shard_map/all_to_all | solution.py:344
  10.7 3.9 %collective-permute-start = (bf16[32,512]{1,0:T(8,128)(2,1)S(1)}, bf16[32,512]{1,0:T(8,128)(2,1)S(1)}, u32[]{:S(2)}, u32[]{:S(2)}) collective-permute-start(bf16[32,512]{1,0:T(8,128)(2,1)S(1)} %get-tuple-element.33), channel_id=1, source_target_pairs={{0,1},{1,0},{2,3},{3,2},{4,5},{5,4},{6,7},{7,6},{8,9},{9,8},{10,11... | collective-permute-start | bytes 98312 | tf_op jit(solution)/shard_map/ppermute | solution.py:348
  11.0 3.6 %collective-permute-start.1 = (bf16[32,512]{1,0:T(8,128)(2,1)S(1)}, bf16[32,512]{1,0:T(8,128)(2,1)S(1)}, u32[]{:S(2)}, u32[]{:S(2)}) collective-permute-start(bf16[32,512]{1,0:T(8,128)(2,1)S(1)} %get-tuple-element.34), channel_id=1, source_target_pairs={{1,2},{3,4},{5,6},{2,1},{4,3},{6,5},{9,10},{11,12},{13,14},{10,9},... | collective-permute-start | bytes 98312 | tf_op jit(solution)/shard_map/ppermute | solution.py:355
  22.4 13.0 %all-to-all-start.1 = ((bf16[32,2,16,128]{3,2,1,0:T(8,128)(2,1)}), bf16[32,2,16,128]{3,2,1,0:T(8,128)(2,1)S(1)}, u32[]{:S(2)}, u32[]{:S(2)}) async-start(bf16[32,2,16,128]{3,2,1,0:T(8,128)(2,1)} %get-tuple-element.36), calls=%async_computation.1 | async-start | bytes 524288 | tf_op jit(solution)/shard_map/all_to_all | solution.py:344
  25.1 3.5 %collective-permute-start.2 = (bf16[32,512]{1,0:T(8,128)(2,1)S(1)}, bf16[32,512]{1,0:T(8,128)(2,1)S(1)}, u32[]{:S(2)}, u32[]{:S(2)}) collective-permute-start(bf16[32,512]{1,0:T(8,128)(2,1)S(1)} %get-tuple-element.39), channel_id=1, source_target_pairs={{0,1},{1,0},{2,3},{3,2},{4,5},{5,4},{6,7},{7,6},{8,9},{9,8},{10,11... | collective-permute-start | bytes 98312 | tf_op jit(solution)/shard_map/ppermute | solution.py:348
  25.3 3.3 %collective-permute-start.3 = (bf16[32,512]{1,0:T(8,128)(2,1)S(1)}, bf16[32,512]{1,0:T(8,128)(2,1)S(1)}, u32[]{:S(2)}, u32[]{:S(2)}) collective-permute-start(bf16[32,512]{1,0:T(8,128)(2,1)S(1)} %get-tuple-element.40), channel_id=1, source_target_pairs={{1,2},{3,4},{5,6},{2,1},{4,3},{6,5},{9,10},{11,12},{13,14},{10,9},... | collective-permute-start | bytes 98312 | tf_op jit(solution)/shard_map/ppermute | solution.py:355

commit v7 on v6

--- a/solution.py
+++ b/solution.py
@@ -129,7 +129,7 @@
 
 
 def prepare_kernel(
-    place_ref, list_ref, top_ref, field_ref, fold_ref, coupling_hbm, blocks_hbm,
+    place_ref, list_ref, field_ref, fold_ref, coupling_hbm, blocks_hbm,
     near_ref, ends_ref, smat_ref, turned_ref, gram_ref, table, blocks_ref, coupling_ref, rows_ref, sem
 ):
     pairs, each = part_copies(blocks_hbm, blocks_ref)
@@ -148,15 +148,12 @@
     for c in range(clusters):
         for j in range(half):
             rows_ref[j * TOPK : (j + 1) * TOPK] = coupling_ref[c, :, j * 2 * rank : (j + 1) * 2 * rank].astype(jnp.float32)
-        for k in range(TOPK):
-            rows = rows_ref[pl.ds(k, half, stride=TOPK), :]
-            upper = jnp.broadcast_to(top_ref[c, k] % 2, lower.shape) == 1
-            here = lower != upper
-            turned = pltpu.roll(rows, rank, 1)
-            even = jnp.where(here, jnp.where(upper, turned, rows), 0.0)
-            odd = jnp.where(here, jnp.where(upper, rows, turned), 0.0)
-            at = slice(k * 2 * rank, (k + 1) * 2 * rank)
-            smat_ref[c, :, at] = jnp.concatenate([even, odd], axis=0).astype(jnp.bfloat16)
+        for k in range(0, TOPK, 2):
+            one = rows_ref[pl.ds(k, half, stride=TOPK), :]
+            two = rows_ref[pl.ds(k + 1, half, stride=TOPK), :]
+            even = jnp.where(lower, one, pltpu.roll(two, rank, 1))
+            odd = jnp.where(lower, pltpu.roll(one, rank, 1), two)
+            smat_ref[c, :, k * rank : (k + 2) * rank] = jnp.concatenate([even, odd], axis=0).astype(jnp.bfloat16)
     ready = wait_parts(copies[1:], each)
     near_sum(place_ref, list_ref, field_ref, blocks_ref, near_ref, ends_ref, table, ready)
 
@@ -245,9 +242,19 @@
 
 
 def down_parts(top_ref, table_ref, smat_ref):
+    shape = table_ref.shape[1:]
+    rank = shape[1] // 2
+    lower = lax.broadcasted_iota(jnp.int32, shape, 1) < rank
+
+    def pick(c, k):
+        top = top_ref[c, k]
+        tile = table_ref[top >> 1]
+        turned = jnp.concatenate([tile[:, rank:], tile[:, :rank]], axis=1)
+        return jnp.where(jnp.broadcast_to(top & 1, shape) == k % 2, tile, turned)
+
     downs = []
     for c in range(smat_ref.shape[0]):
-        tiles = [table_ref[top_ref[c, k] >> 1] for k in range(TOPK)]
+        tiles = [jnp.where(lower, pick(c, k), pick(c, k + 1)) for k in range(0, TOPK, 2)]
         downs.append(dot_tt(jnp.concatenate(tiles, axis=1), smat_ref[c]).astype(jnp.bfloat16))
     return downs
 
@@ -415,12 +422,12 @@
 
     near, ends, smat, turned, gram = pl.pallas_call(
         prepare_kernel,
-        in_specs=[SMEM] * 3 + [VMEM] * 2 + [HBM] * 2,
+        in_specs=[SMEM] * 2 + [VMEM] * 2 + [HBM] * 2,
         out_specs=[VMEM] * 5,
         out_shape=[
             field_shape,
             ends_shape,
-            pltpu.VMEM((clusters, rank, TOPK * 2 * rank), jnp.bfloat16),
+            pltpu.VMEM((clusters, rank, TOPK * rank), jnp.bfloat16),
             fold_shape,
             pltpu.VMEM((clusters, rank, rank), jnp.bfloat16),
         ],
@@ -432,7 +439,7 @@
         ],
         compiler_params=PARAMS,
         name="prepare",
-    )(place, near_list, top_list, field, fold, *in_hbm(coupling, near_blocks))
+    )(place, near_list, field, fold, *in_hbm(coupling, near_blocks))
     edge = edge_product(inner, outer, ends)
 
     chunk, image, inner, outer = pl.pallas_call(

time: 47 us -> 46.9 us (level)
  no operation moved by 1% of the time
where the time goes in v7:
time: 46.9 us; the launch traced here: 46.5 us
  waiting for transfers between devices  12.5 us (27%)
  Pallas kernels  12.2 us (26%)
  starting transfers between devices  11.8 us (25%)
  blocking collectives  9.4 us (20%)
  between operations  0.75 us (2%)
    all_to_all x2, waiting for transfers between devices, exchange(): return lax.all_to_all(chunk, AXES, 0, 0)  12.4 us
    all_to_all x2, starting transfers between devices, exchange(): return lax.all_to_all(chunk, AXES, 0, 0)  9.9 us
    all_to_all x1, blocking collectives, exchange(): return lax.all_to_all(chunk, AXES, 0, 0)  9.4 us
    pallas_call x1, Pallas kernels, per_device(): pl.pallas_call(prepare_kernel, in_specs=[SMEM] * 2 + [VMEM] * 2 + [HBM] *...  2.89 us
    pallas_call x1, Pallas kernels, per_device(): pl.pallas_call(first_kernel, in_specs=[HBM] * 5, out_specs=[HBM] + [VMEM]...  2.75 us
    pallas_call x1, Pallas kernels, per_device(): pl.pallas_call(near_kernel, in_specs=[SMEM] * 2 + [VMEM, HBM], out_specs=...  2.64 us
    pallas_call x1, Pallas kernels, per_device(): pl.pallas_call(second_kernel, in_specs=[SMEM] * 2 + [VMEM] * 9, out_specs...  1.31 us
    ppermute x2, starting transfers between devices, swap_ends(): outer = lax.ppermute(outer, 'dev', pairs + [(b, a) for a, b in pairs])  1.3 us
  transfers between devices with their start and end apart: 6, of which 2 were waited for; matrix products, arithmetic and copies ran while one was open for 0% of the time, Pallas kernels for 14%

profile of v7, /device:TPU:0, one launch (start us, length us, event | category | flops | bytes accessed | tf_op | source)
XLA Modules:
  0.0 46.5 jit_solution(11167707135382341912)
XLA Ops:
  0.6 0.0 copy-start
  0.6 2.8 %first.1 = (bf16[32,2,16,128]{3,2,1,0:T(8,128)(2,1)}, f32[16,4096]{1,0:T(8,128)S(1)}, bf16[4,64,1024]{2,1,0:T(8,128)(2,1)S(1)}, bf16[32,512]{1,0:T(8,128)(2,1)S(...) custom-call(f32[16,4096]{1,0:T(8,128)} %field_hbm.1, ...), custom_call_target="tpu_custom_call" | custom-call | tf_op jit(solution)/shard_map/first/pallas_call | solution.py:380
  3.4 7.3 %all-to-all-start = ((bf16[32,2,16,128]{3,2,1,0:T(8,128)(2,1)}), bf16[32,2,16,128]{3,2,1,0:T(8,128)(2,1)S(1)}, u32[]{:S(2)}, u32[]{:S(2)}) async-start(bf16[32,2,16,128]{3,2,1,0:T(8,128)(2,1)} %get-tuple-element.25), calls=%async_computation | async-start | bytes 524288 | tf_op jit(solution)/shard_map/all_to_all | solution.py:351
  10.7 0.3 collective-permute-start
  11.0 0.7 %collective-permute-start.1 = (bf16[32,512]{1,0:T(8,128)(2,1)S(1)}, bf16[32,512]{1,0:T(8,128)(2,1)S(1)}, u32[]{:S(2)}, u32[]{:S(2)}) collective-permute-start(bf16[32,512]{1,0:T(8,128)(2,1)S(1)} %get-tuple-element.34), channel_id=1, source_target_pairs={{1,2},{3,4},{5,6},{2,1},{4,3},{6,5},{9,10},{11,12},{13,14},{10,9},... | collective-permute-start | bytes 98312 | tf_op jit(solution)/shard_map/ppermute | solution.py:362
  11.7 2.9 %prepare.1 = (f32[16,4096]{1,0:T(8,128)S(1)}, bf16[8,4,128,128]{3,2,1,0:T(8,128)(2,1)S(1)}, bf16[4,64,1024]{2,1,0:T(8,128)(2,1)S(1)}, bf16[4,64,1024]{2,1,0:T(8,128)(2,1)S(1)}, bf16[4,64,64]{2,1,0:T(8,128)(2,1)S(1)}) custom-call(s32[2]{0:T(128)S(4)} %get-tuple-element.24.place_ref, s32[4,32]{1,0:T(4,128)S(4)} %get-tuple-element.26.list_ref, ...), custom_call_target="tpu_custom_call" | custom-call | tf_op jit(solution)/shard_map/prepare/pallas_call | solution.py:423
  14.6 0.0 collective-permute-done.inner_ref
  14.6 0.0 collective-permute-done.1.outer_ref
  14.6 0.4 edge.2.edge_ref
  15.0 6.1 %all-to-all-done = bf16[32,2,16,128]{3,2,1,0:T(8,128)(2,1)S(1)} async-done(((bf16[32,2,16,128]{3,2,1,0:T(8,128)(2,1)}), bf16[32,2,16,128]{3,2,1,0:T(8,128)(2,1)S(1)}, u32[]{:S(2)}, u32[]{:S(2)}) %all-to-all-start) | async-done | bytes 262176 | tf_op jit(solution)/shard_map/all_to_all | solution.py:351
  21.1 0.0 copy-done
  21.1 1.3 %second.1 = (bf16[32,2,16,128]{3,2,1,0:T(8,128)(2,1)}, f32[16,4096]{1,0:T(8,128)S(1)}, bf16[32,512]{1,0:T(8,128)(2,1)S(1)}, bf16[32,512]{1,0:T(8,128)(2,1)S(1)}) custom-call(s32[2]{0:T(128)S(4)} %get-tuple-element.24.place_ref, s32[4,16]{1,0:T(4,128)S(4)} %get-tuple-element.23.top_ref, bf16[64,16,128]{2,1,0:T(8,128)(2,1)S(1)} %bitcast.4, ...), custom_call_target="tpu_custom_call" | custom-call | tf_op jit(solution)/shard_map/second/pallas_call | solution.py:445
  22.4 2.6 %all-to-all-start.1 = ((bf16[32,2,16,128]{3,2,1,0:T(8,128)(2,1)}), bf16[32,2,16,128]{3,2,1,0:T(8,128)(2,1)S(1)}, u32[]{:S(2)}, u32[]{:S(2)}) async-start(bf16[32,2,16,128]{3,2,1,0:T(8,128)(2,1)} %get-tuple-element.36), calls=%async_computation.1 | async-start | bytes 524288 | tf_op jit(solution)/shard_map/all_to_all | solution.py:351
  25.0 0.2 collective-permute-start.2
  25.3 0.7 %collective-permute-start.3 = (bf16[32,512]{1,0:T(8,128)(2,1)S(1)}, bf16[32,512]{1,0:T(8,128)(2,1)S(1)}, u32[]{:S(2)}, u32[]{:S(2)}) collective-permute-start(bf16[32,512]{1,0:T(8,128)(2,1)S(1)} %get-tuple-element.40), channel_id=1, source_target_pairs={{1,2},{3,4},{5,6},{2,1},{4,3},{6,5},{9,10},{11,12},{13,14},{10,9},... | collective-permute-start | bytes 98312 | tf_op jit(solution)/shard_map/ppermute | solution.py:362
  25.9 2.6 %near.1 = (f32[16,4096]{1,0:T(8,128)S(1)}, bf16[8,4,128,128]{3,2,1,0:T(8,128)(2,1)S(1)}) custom-call(s32[2]{0:T(128)S(4)} %get-tuple-element.24.place_ref, s32[4,32]{1,0:T(4,128)S(4)} %get-tuple-element.26.list_ref, f32[16,4096]{1,0:T(8,128)S(1)} %get-tuple-element.37.field_ref.image_ref, bf16[32,4,128,128]{3,2,1,0:T(8,128)(2,1)} %blocks_hbm.3), custom_call_target="tpu_custom_call" | custom-call | tf_op jit(solution)/shard_map/near/pallas_call | solution.py:455
  28.6 0.0 collective-permute-done.2.inner_ref
  28.6 0.0 collective-permute-done.3.outer_ref
  28.6 0.4 edge.3.edge_ref
  29.0 6.4 %all-to-all-done.1 = bf16[32,2,16,128]{3,2,1,0:T(8,128)(2,1)S(1)} async-done(((bf16[32,2,16,128]{3,2,1,0:T(8,128)(2,1)}), bf16[32,2,16,128]{3,2,1,0:T(8,128)(2,1)S(1)}, u32[]{:S(2)}, u32[]{:S(2)}) %all-to-all-start.1) | async-done | bytes 262176 | tf_op jit(solution)/shard_map/all_to_all | solution.py:351
  35.4 0.6 %third.1 = (f32[16,4096]{1,0:T(8,128)S(1)}, f32[32,1,128]{2,1,0:T(1,128)S(1)}) custom-call(s32[4,16]{1,0:T(4,128)S(4)} %get-tuple-element.23.top_ref, bf16[64,16,128]{2,1,0:T(8,128)(2,1)S(1)} %bitcast.5, bf16[4,64,1024]{2,1,0:T(8,128)(2,1)S(1)} %get-tuple-element.29.smat_ref, bf16[4,64,1024]{2,1,0:T(8,128)(2,1)S(1)} %get-tuple-element.30.turned_ref, ...), custom_call_target="tpu_custom_call" | custom-call | tf_op jit(solution)/shard_map/third/pallas_call | solution.py:466
  36.0 9.4 %all_to_all.15.sums_ref = f32[32,1,128]{2,1,0:T(1,128)S(1)} all-to-all(f32[32,1,128]{2,1,0:T(1,128)S(1)} %get-tuple-element.42), channel_id=1, replica_groups=mesh['group'=4,'dev'=8] {'group','dev'}, dimensions={0} | all-to-all | bytes 32768 | tf_op jit(solution)/shard_map/all_to_all | solution.py:351
  45.4 1.1 %last.1 = (f32[16,4096]{1,0:T(8,128)}, f32[16,4096]{1,0:T(8,128)}) custom-call(f32[32,1,128]{2,1,0:T(1,128)S(1)} %all_to_all.15.sums_ref, f32[16,4096]{1,0:T(8,128)S(1)} %get-tuple-element.27.field_ref, f32[16,4096]{1,0:T(8,128)S(1)} %get-tuple-element.37.field_ref.image_ref, f32[16,4096]{1,0:T(8,128)S(1)} %get-tuple-element.43.twice_ref), custom_call_target="tpu_custom_call" | custom-call | tf_op jit(solution)/shard_map/last/pallas_call | solution.py:476
Async XLA Ops:
  0.6 20.5 %copy-start = (f32[4096]{0:T(1024)S(1)}, f32[4096]{0:T(1024)}, u32[]{:S(2)}) copy-start(f32[4096]{0:T(1024)} %param.9) | copy-start | bytes 49156
  3.4 17.7 %all-to-all-start = ((bf16[32,2,16,128]{3,2,1,0:T(8,128)(2,1)}), bf16[32,2,16,128]{3,2,1,0:T(8,128)(2,1)S(1)}, u32[]{:S(2)}, u32[]{:S(2)}) async-start(bf16[32,2,16,128]{3,2,1,0:T(8,128)(2,1)} %get-tuple-element.25), calls=%async_computation | async-start | bytes 524288 | tf_op jit(solution)/shard_map/all_to_all | solution.py:351
  10.7 3.9 %collective-permute-start = (bf16[32,512]{1,0:T(8,128)(2,1)S(1)}, bf16[32,512]{1,0:T(8,128)(2,1)S(1)}, u32[]{:S(2)}, u32[]{:S(2)}) collective-permute-start(bf16[32,512]{1,0:T(8,128)(2,1)S(1)} %get-tuple-element.33), channel_id=1, source_target_pairs={{0,1},{1,0},{2,3},{3,2},{4,5},{5,4},{6,7},{7,6},{8,9},{9,8},{10,11... | collective-permute-start | bytes 98312 | tf_op jit(solution)/shard_map/ppermute | solution.py:355
  11.0 3.6 %collective-permute-start.1 = (bf16[32,512]{1,0:T(8,128)(2,1)S(1)}, bf16[32,512]{1,0:T(8,128)(2,1)S(1)}, u32[]{:S(2)}, u32[]{:S(2)}) collective-permute-start(bf16[32,512]{1,0:T(8,128)(2,1)S(1)} %get-tuple-element.34), channel_id=1, source_target_pairs={{1,2},{3,4},{5,6},{2,1},{4,3},{6,5},{9,10},{11,12},{13,14},{10,9},... | collective-permute-start | bytes 98312 | tf_op jit(solution)/shard_map/ppermute | solution.py:362
  22.4 13.0 %all-to-all-start.1 = ((bf16[32,2,16,128]{3,2,1,0:T(8,128)(2,1)}), bf16[32,2,16,128]{3,2,1,0:T(8,128)(2,1)S(1)}, u32[]{:S(2)}, u32[]{:S(2)}) async-start(bf16[32,2,16,128]{3,2,1,0:T(8,128)(2,1)} %get-tuple-element.36), calls=%async_computation.1 | async-start | bytes 524288 | tf_op jit(solution)/shard_map/all_to_all | solution.py:351
  25.0 3.6 %collective-permute-start.2 = (bf16[32,512]{1,0:T(8,128)(2,1)S(1)}, bf16[32,512]{1,0:T(8,128)(2,1)S(1)}, u32[]{:S(2)}, u32[]{:S(2)}) collective-permute-start(bf16[32,512]{1,0:T(8,128)(2,1)S(1)} %get-tuple-element.39), channel_id=1, source_target_pairs={{0,1},{1,0},{2,3},{3,2},{4,5},{5,4},{6,7},{7,6},{8,9},{9,8},{10,11... | collective-permute-start | bytes 98312 | tf_op jit(solution)/shard_map/ppermute | solution.py:355
  25.3 3.3 %collective-permute-start.3 = (bf16[32,512]{1,0:T(8,128)(2,1)S(1)}, bf16[32,512]{1,0:T(8,128)(2,1)S(1)}, u32[]{:S(2)}, u32[]{:S(2)}) collective-permute-start(bf16[32,512]{1,0:T(8,128)(2,1)S(1)} %get-tuple-element.40), channel_id=1, source_target_pairs={{1,2},{3,4},{5,6},{2,1},{4,3},{6,5},{9,10},{11,12},{13,14},{10,9},... | collective-permute-start | bytes 98312 | tf_op jit(solution)/shard_map/ppermute | solution.py:362

commit v8 on v7

--- a/solution.py
+++ b/solution.py
@@ -10,7 +10,7 @@
 LEAF_CL = 8
 TOPK = 16
 NEAR = 4
-PARTS = 4
+PARTS = 2
 HALO = 4
 AXES = ("group", "dev")
 VMEM = pl.BlockSpec(memory_space=pltpu.VMEM)

time: 46.9 us -> 46.9 us (level)
  no operation moved by 1% of the time
where the time goes in v8:
time: 46.9 us; the launch traced here: 46.5 us
  Pallas kernels  12.5 us (27%)
  waiting for transfers between devices  12.2 us (26%)
  starting transfers between devices  11.8 us (25%)
  blocking collectives  9.4 us (20%)
  between operations  0.75 us (2%)
    all_to_all x2, waiting for transfers between devices, exchange(): return lax.all_to_all(chunk, AXES, 0, 0)  12.1 us
    all_to_all x2, starting transfers between devices, exchange(): return lax.all_to_all(chunk, AXES, 0, 0)  9.9 us
    all_to_all x1, blocking collectives, exchange(): return lax.all_to_all(chunk, AXES, 0, 0)  9.4 us
    pallas_call x1, Pallas kernels, per_device(): pl.pallas_call(prepare_kernel, in_specs=[SMEM] * 2 + [VMEM] * 2 + [HBM] *...  3.01 us
    pallas_call x1, Pallas kernels, per_device(): pl.pallas_call(near_kernel, in_specs=[SMEM] * 2 + [VMEM, HBM], out_specs=...  2.82 us
    pallas_call x1, Pallas kernels, per_device(): pl.pallas_call(first_kernel, in_specs=[HBM] * 5, out_specs=[HBM] + [VMEM]...  2.75 us
    pallas_call x1, Pallas kernels, per_device(): pl.pallas_call(second_kernel, in_specs=[SMEM] * 2 + [VMEM] * 9, out_specs...  1.3 us
    ppermute x2, starting transfers between devices, swap_ends(): outer = lax.ppermute(outer, 'dev', pairs + [(b, a) for a, b in pairs])  1.3 us
  transfers between devices with their start and end apart: 6, of which 2 were waited for; matrix products, arithmetic and copies ran while one was open for 0% of the time, Pallas kernels for 14%

profile of v8, /device:TPU:0, one launch (start us, length us, event | category | flops | bytes accessed | tf_op | source)
XLA Modules:
  0.0 46.5 jit_solution(10628557000282031758)
XLA Ops:
  0.6 0.0 copy-start
  0.6 2.8 %first.1 = (bf16[32,2,16,128]{3,2,1,0:T(8,128)(2,1)}, f32[16,4096]{1,0:T(8,128)S(1)}, bf16[4,64,1024]{2,1,0:T(8,128)(2,1)S(1)}, bf16[32,512]{1,0:T(8,128)(2,1)S(...) custom-call(f32[16,4096]{1,0:T(8,128)} %field_hbm.1, ...), custom_call_target="tpu_custom_call" | custom-call | tf_op jit(solution)/shard_map/first/pallas_call | solution.py:380
  3.4 7.3 %all-to-all-start = ((bf16[32,2,16,128]{3,2,1,0:T(8,128)(2,1)}), bf16[32,2,16,128]{3,2,1,0:T(8,128)(2,1)S(1)}, u32[]{:S(2)}, u32[]{:S(2)}) async-start(bf16[32,2,16,128]{3,2,1,0:T(8,128)(2,1)} %get-tuple-element.25), calls=%async_computation | async-start | bytes 524288 | tf_op jit(solution)/shard_map/all_to_all | solution.py:351
  10.7 0.3 collective-permute-start
  11.0 0.7 %collective-permute-start.1 = (bf16[32,512]{1,0:T(8,128)(2,1)S(1)}, bf16[32,512]{1,0:T(8,128)(2,1)S(1)}, u32[]{:S(2)}, u32[]{:S(2)}) collective-permute-start(bf16[32,512]{1,0:T(8,128)(2,1)S(1)} %get-tuple-element.34), channel_id=1, source_target_pairs={{1,2},{3,4},{5,6},{2,1},{4,3},{6,5},{9,10},{11,12},{13,14},{10,9},... | collective-permute-start | bytes 98312 | tf_op jit(solution)/shard_map/ppermute | solution.py:362
  11.7 3.0 %prepare.1 = (f32[16,4096]{1,0:T(8,128)S(1)}, bf16[8,4,128,128]{3,2,1,0:T(8,128)(2,1)S(1)}, bf16[4,64,1024]{2,1,0:T(8,128)(2,1)S(1)}, bf16[4,64,1024]{2,1,0:T(8,128)(2,1)S(1)}, bf16[4,64,64]{2,1,0:T(8,128)(2,1)S(1)}) custom-call(s32[2]{0:T(128)S(4)} %get-tuple-element.24.place_ref, s32[4,32]{1,0:T(4,128)S(4)} %get-tuple-element.26.list_ref, ...), custom_call_target="tpu_custom_call" | custom-call | tf_op jit(solution)/shard_map/prepare/pallas_call | solution.py:423
  14.7 0.0 collective-permute-done.inner_ref
  14.7 0.0 collective-permute-done.1.outer_ref
  14.7 0.4 edge.2.edge_ref
  15.2 5.9 %all-to-all-done = bf16[32,2,16,128]{3,2,1,0:T(8,128)(2,1)S(1)} async-done(((bf16[32,2,16,128]{3,2,1,0:T(8,128)(2,1)}), bf16[32,2,16,128]{3,2,1,0:T(8,128)(2,1)S(1)}, u32[]{:S(2)}, u32[]{:S(2)}) %all-to-all-start) | async-done | bytes 262176 | tf_op jit(solution)/shard_map/all_to_all | solution.py:351
  21.1 0.0 copy-done
  21.1 1.3 %second.1 = (bf16[32,2,16,128]{3,2,1,0:T(8,128)(2,1)}, f32[16,4096]{1,0:T(8,128)S(1)}, bf16[32,512]{1,0:T(8,128)(2,1)S(1)}, bf16[32,512]{1,0:T(8,128)(2,1)S(1)}) custom-call(s32[2]{0:T(128)S(4)} %get-tuple-element.24.place_ref, s32[4,16]{1,0:T(4,128)S(4)} %get-tuple-element.23.top_ref, bf16[64,16,128]{2,1,0:T(8,128)(2,1)S(1)} %bitcast.4, ...), custom_call_target="tpu_custom_call" | custom-call | tf_op jit(solution)/shard_map/second/pallas_call | solution.py:445
  22.4 2.6 %all-to-all-start.1 = ((bf16[32,2,16,128]{3,2,1,0:T(8,128)(2,1)}), bf16[32,2,16,128]{3,2,1,0:T(8,128)(2,1)S(1)}, u32[]{:S(2)}, u32[]{:S(2)}) async-start(bf16[32,2,16,128]{3,2,1,0:T(8,128)(2,1)} %get-tuple-element.36), calls=%async_computation.1 | async-start | bytes 524288 | tf_op jit(solution)/shard_map/all_to_all | solution.py:351
  25.0 0.2 collective-permute-start.2
  25.3 0.7 %collective-permute-start.3 = (bf16[32,512]{1,0:T(8,128)(2,1)S(1)}, bf16[32,512]{1,0:T(8,128)(2,1)S(1)}, u32[]{:S(2)}, u32[]{:S(2)}) collective-permute-start(bf16[32,512]{1,0:T(8,128)(2,1)S(1)} %get-tuple-element.40), channel_id=1, source_target_pairs={{1,2},{3,4},{5,6},{2,1},{4,3},{6,5},{9,10},{11,12},{13,14},{10,9},... | collective-permute-start | bytes 98312 | tf_op jit(solution)/shard_map/ppermute | solution.py:362
  25.9 2.8 %near.1 = (f32[16,4096]{1,0:T(8,128)S(1)}, bf16[8,4,128,128]{3,2,1,0:T(8,128)(2,1)S(1)}) custom-call(s32[2]{0:T(128)S(4)} %get-tuple-element.24.place_ref, s32[4,32]{1,0:T(4,128)S(4)} %get-tuple-element.26.list_ref, f32[16,4096]{1,0:T(8,128)S(1)} %get-tuple-element.37.field_ref.image_ref, bf16[32,4,128,128]{3,2,1,0:T(8,128)(2,1)} %blocks_hbm.3), custom_call_target="tpu_custom_call" | custom-call | tf_op jit(solution)/shard_map/near/pallas_call | solution.py:455
  28.8 0.0 collective-permute-done.2.inner_ref
  28.8 0.0 collective-permute-done.3.outer_ref
  28.8 0.4 edge.3.edge_ref
  29.2 6.2 %all-to-all-done.1 = bf16[32,2,16,128]{3,2,1,0:T(8,128)(2,1)S(1)} async-done(((bf16[32,2,16,128]{3,2,1,0:T(8,128)(2,1)}), bf16[32,2,16,128]{3,2,1,0:T(8,128)(2,1)S(1)}, u32[]{:S(2)}, u32[]{:S(2)}) %all-to-all-start.1) | async-done | bytes 262176 | tf_op jit(solution)/shard_map/all_to_all | solution.py:351
  35.4 0.6 %third.1 = (f32[16,4096]{1,0:T(8,128)S(1)}, f32[32,1,128]{2,1,0:T(1,128)S(1)}) custom-call(s32[4,16]{1,0:T(4,128)S(4)} %get-tuple-element.23.top_ref, bf16[64,16,128]{2,1,0:T(8,128)(2,1)S(1)} %bitcast.5, bf16[4,64,1024]{2,1,0:T(8,128)(2,1)S(1)} %get-tuple-element.29.smat_ref, bf16[4,64,1024]{2,1,0:T(8,128)(2,1)S(1)} %get-tuple-element.30.turned_ref, ...), custom_call_target="tpu_custom_call" | custom-call | tf_op jit(solution)/shard_map/third/pallas_call | solution.py:466
  36.0 9.4 %all_to_all.15.sums_ref = f32[32,1,128]{2,1,0:T(1,128)S(1)} all-to-all(f32[32,1,128]{2,1,0:T(1,128)S(1)} %get-tuple-element.42), channel_id=1, replica_groups=mesh['group'=4,'dev'=8] {'group','dev'}, dimensions={0} | all-to-all | bytes 32768 | tf_op jit(solution)/shard_map/all_to_all | solution.py:351
  45.4 1.1 %last.1 = (f32[16,4096]{1,0:T(8,128)}, f32[16,4096]{1,0:T(8,128)}) custom-call(f32[32,1,128]{2,1,0:T(1,128)S(1)} %all_to_all.15.sums_ref, f32[16,4096]{1,0:T(8,128)S(1)} %get-tuple-element.27.field_ref, f32[16,4096]{1,0:T(8,128)S(1)} %get-tuple-element.37.field_ref.image_ref, f32[16,4096]{1,0:T(8,128)S(1)} %get-tuple-element.43.twice_ref), custom_call_target="tpu_custom_call" | custom-call | tf_op jit(solution)/shard_map/last/pallas_call | solution.py:476
Async XLA Ops:
  0.6 20.5 %copy-start = (f32[4096]{0:T(1024)S(1)}, f32[4096]{0:T(1024)}, u32[]{:S(2)}) copy-start(f32[4096]{0:T(1024)} %param.9) | copy-start | bytes 49156
  3.4 17.7 %all-to-all-start = ((bf16[32,2,16,128]{3,2,1,0:T(8,128)(2,1)}), bf16[32,2,16,128]{3,2,1,0:T(8,128)(2,1)S(1)}, u32[]{:S(2)}, u32[]{:S(2)}) async-start(bf16[32,2,16,128]{3,2,1,0:T(8,128)(2,1)} %get-tuple-element.25), calls=%async_computation | async-start | bytes 524288 | tf_op jit(solution)/shard_map/all_to_all | solution.py:351
  10.7 4.0 %collective-permute-start = (bf16[32,512]{1,0:T(8,128)(2,1)S(1)}, bf16[32,512]{1,0:T(8,128)(2,1)S(1)}, u32[]{:S(2)}, u32[]{:S(2)}) collective-permute-start(bf16[32,512]{1,0:T(8,128)(2,1)S(1)} %get-tuple-element.33), channel_id=1, source_target_pairs={{0,1},{1,0},{2,3},{3,2},{4,5},{5,4},{6,7},{7,6},{8,9},{9,8},{10,11... | collective-permute-start | bytes 98312 | tf_op jit(solution)/shard_map/ppermute | solution.py:355
  11.0 3.7 %collective-permute-start.1 = (bf16[32,512]{1,0:T(8,128)(2,1)S(1)}, bf16[32,512]{1,0:T(8,128)(2,1)S(1)}, u32[]{:S(2)}, u32[]{:S(2)}) collective-permute-start(bf16[32,512]{1,0:T(8,128)(2,1)S(1)} %get-tuple-element.34), channel_id=1, source_target_pairs={{1,2},{3,4},{5,6},{2,1},{4,3},{6,5},{9,10},{11,12},{13,14},{10,9},... | collective-permute-start | bytes 98312 | tf_op jit(solution)/shard_map/ppermute | solution.py:362
  22.4 13.0 %all-to-all-start.1 = ((bf16[32,2,16,128]{3,2,1,0:T(8,128)(2,1)}), bf16[32,2,16,128]{3,2,1,0:T(8,128)(2,1)S(1)}, u32[]{:S(2)}, u32[]{:S(2)}) async-start(bf16[32,2,16,128]{3,2,1,0:T(8,128)(2,1)} %get-tuple-element.36), calls=%async_computation.1 | async-start | bytes 524288 | tf_op jit(solution)/shard_map/all_to_all | solution.py:351
  25.0 3.7 %collective-permute-start.2 = (bf16[32,512]{1,0:T(8,128)(2,1)S(1)}, bf16[32,512]{1,0:T(8,128)(2,1)S(1)}, u32[]{:S(2)}, u32[]{:S(2)}) collective-permute-start(bf16[32,512]{1,0:T(8,128)(2,1)S(1)} %get-tuple-element.39), channel_id=1, source_target_pairs={{0,1},{1,0},{2,3},{3,2},{4,5},{5,4},{6,7},{7,6},{8,9},{9,8},{10,11... | collective-permute-start | bytes 98312 | tf_op jit(solution)/shard_map/ppermute | solution.py:355
  25.3 3.5 %collective-permute-start.3 = (bf16[32,512]{1,0:T(8,128)(2,1)S(1)}, bf16[32,512]{1,0:T(8,128)(2,1)S(1)}, u32[]{:S(2)}, u32[]{:S(2)}) collective-permute-start(bf16[32,512]{1,0:T(8,128)(2,1)S(1)} %get-tuple-element.40), channel_id=1, source_target_pairs={{1,2},{3,4},{5,6},{2,1},{4,3},{6,5},{9,10},{11,12},{13,14},{10,9},... | collective-permute-start | bytes 98312 | tf_op jit(solution)/shard_map/ppermute | solution.py:362

commit v9 on v8

--- a/solution.py
+++ b/solution.py
@@ -201,11 +201,15 @@
 
 
 def near_kernel(
-    place_ref, list_ref, field_ref, blocks_hbm, near_ref, ends_ref, table, blocks_ref, sem
+    place_ref, list_ref, field_ref, start_ref, blocks_hbm, near_ref, ends_ref, rest_ref, table, blocks_ref, sem
 ):
     pairs, each = part_copies(blocks_hbm, blocks_ref)
     ready = wait_parts(load_all(pairs, sem), each)
     near_sum(place_ref, list_ref, field_ref, blocks_ref, near_ref, ends_ref, table, ready)
+    start, field = start_ref[...], field_ref[...]
+    size = jnp.sum(field * field, axis=1, keepdims=True)
+    cross = jnp.sum(start * field, axis=1, keepdims=True)
+    rest_ref[...] = start - cross / jnp.where(size > 0, size, 1.0) * field
 
 
 def edge_kernel(leaves, place_ref, list_ref, inner_ref, outer_ref, ends_ref, edge_ref, table):
@@ -279,7 +283,7 @@
 
 
 def third_kernel(
-    top_ref, table_ref, smat_ref, turned_ref, nugget_ref, field_ref, image_ref, near_ref, edge_ref,
+    top_ref, table_ref, smat_ref, turned_ref, nugget_ref, field_ref, image_ref, rest_ref, near_ref, edge_ref,
     twice_ref, sums_ref,
 ):
     clusters, _, span = turned_ref.shape
@@ -294,19 +298,19 @@
         return jnp.sum(left * right, axis=1, keepdims=True)
 
     field, image, twice = field_ref[...], image_ref[...], twice_ref[...]
+    rest = rest_ref[...]
     size = dot(image, image)
     cross = dot(field, image)
+    rest_twice, image_twice = dot(rest, twice), dot(image, twice)
     own = cross / jnp.where(size > 0, size, 1.0)
-    rest = field - own * image
-    bent = image - own * twice
     sums = [
         dot(field, field),
         cross,
         size,
         dot(rest, rest),
-        dot(rest, bent),
-        dot(image, bent) + dot(rest, twice),
-        dot(image, twice),
+        dot(rest, image) - own * rest_twice,
+        size - own * image_twice + rest_twice,
+        image_twice,
     ]
     width = sums_ref.shape[2]
     lane = lax.broadcasted_iota(jnp.int32, (rhs, width), 1)
@@ -452,25 +456,25 @@
         name="second",
     )(place, top_list, table, smat, turned, gram, fold, nugget, field, near, edge)
     table = exchange(chunk).reshape(-1, rhs, 2 * rank)
-    near, ends = pl.pallas_call(
+    near, ends, rest = pl.pallas_call(
         near_kernel,
-        in_specs=[SMEM] * 2 + [VMEM, HBM],
-        out_specs=[VMEM] * 2,
-        out_shape=[field_shape, ends_shape],
+        in_specs=[SMEM] * 2 + [VMEM] * 2 + [HBM],
+        out_specs=[VMEM] * 3,
+        out_shape=[field_shape, ends_shape, field_shape],
         scratch_shapes=near_scratch + [pltpu.SemaphoreType.DMA((PARTS,))],
         compiler_params=PARAMS,
         name="near",
-    )(place, near_list, image, *in_hbm(near_blocks))
+    )(place, near_list, image, field, *in_hbm(near_blocks))
     edge = edge_product(inner, outer, ends)
 
     twice, sums = pl.pallas_call(
         third_kernel,
-        in_specs=[SMEM] + [VMEM] * 8,
+        in_specs=[SMEM] + [VMEM] * 9,
         out_specs=[VMEM] * 2,
         out_shape=[field_shape, struct((devices, 1, 8 * rhs), jnp.float32)],
         compiler_params=PARAMS,
         name="third",
-    )(top_list, table, smat, turned, nugget, field, image, near, edge)
+    )(top_list, table, smat, turned, nugget, field, image, rest, near, edge)
     sums = exchange(sums)
 
     return pl.pallas_call(

time: 46.9 us -> 46.9 us (level)
  no operation moved by 1% of the time
where the time goes in v9:
time: 46.9 us; the launch traced here: 46.6 us
  Pallas kernels  12.5 us (27%)
  waiting for transfers between devices  12.1 us (26%)
  starting transfers between devices  11.8 us (25%)
  blocking collectives  9.41 us (20%)
  between operations  0.75 us (2%)
    all_to_all x2, waiting for transfers between devices, exchange(): return lax.all_to_all(chunk, AXES, 0, 0)  12.1 us
    all_to_all x2, starting transfers between devices, exchange(): return lax.all_to_all(chunk, AXES, 0, 0)  9.9 us
    all_to_all x1, blocking collectives, exchange(): return lax.all_to_all(chunk, AXES, 0, 0)  9.41 us
    pallas_call x1, Pallas kernels, per_device(): pl.pallas_call(prepare_kernel, in_specs=[SMEM] * 2 + [VMEM] * 2 + [HBM] *...  3.01 us
    pallas_call x1, Pallas kernels, per_device(): pl.pallas_call(near_kernel, in_specs=[SMEM] * 2 + [VMEM] * 2 + [HBM], out...  2.86 us
    pallas_call x1, Pallas kernels, per_device(): pl.pallas_call(first_kernel, in_specs=[HBM] * 5, out_specs=[HBM] + [VMEM]...  2.75 us
    pallas_call x1, Pallas kernels, per_device(): pl.pallas_call(second_kernel, in_specs=[SMEM] * 2 + [VMEM] * 9, out_specs...  1.3 us
    ppermute x2, starting transfers between devices, swap_ends(): outer = lax.ppermute(outer, 'dev', pairs + [(b, a) for a, b in pairs])  1.3 us
  transfers between devices with their start and end apart: 6, of which 2 were waited for; matrix products, arithmetic and copies ran while one was open for 0% of the time, Pallas kernels for 14%

profile of v9, /device:TPU:0, one launch (start us, length us, event | category | flops | bytes accessed | tf_op | source)
XLA Modules:
  0.0 46.6 jit_solution(5430669856849167710)
XLA Ops:
  0.6 0.0 copy-start
  0.6 2.8 %first.1 = (bf16[32,2,16,128]{3,2,1,0:T(8,128)(2,1)}, f32[16,4096]{1,0:T(8,128)S(1)}, bf16[4,64,1024]{2,1,0:T(8,128)(2,1)S(1)}, bf16[32,512]{1,0:T(8,128)(2,1)S(...) custom-call(f32[16,4096]{1,0:T(8,128)} %field_hbm.1, ...), custom_call_target="tpu_custom_call" | custom-call | tf_op jit(solution)/shard_map/first/pallas_call | solution.py:384
  3.4 7.3 %all-to-all-start = ((bf16[32,2,16,128]{3,2,1,0:T(8,128)(2,1)}), bf16[32,2,16,128]{3,2,1,0:T(8,128)(2,1)S(1)}, u32[]{:S(2)}, u32[]{:S(2)}) async-start(bf16[32,2,16,128]{3,2,1,0:T(8,128)(2,1)} %get-tuple-element.26), calls=%async_computation | async-start | bytes 524288 | tf_op jit(solution)/shard_map/all_to_all | solution.py:355
  10.7 0.3 collective-permute-start
  11.0 0.7 %collective-permute-start.1 = (bf16[32,512]{1,0:T(8,128)(2,1)S(1)}, bf16[32,512]{1,0:T(8,128)(2,1)S(1)}, u32[]{:S(2)}, u32[]{:S(2)}) collective-permute-start(bf16[32,512]{1,0:T(8,128)(2,1)S(1)} %get-tuple-element.35), channel_id=1, source_target_pairs={{1,2},{3,4},{5,6},{2,1},{4,3},{6,5},{9,10},{11,12},{13,14},{10,9},... | collective-permute-start | bytes 98312 | tf_op jit(solution)/shard_map/ppermute | solution.py:366
  11.7 3.0 %prepare.1 = (f32[16,4096]{1,0:T(8,128)S(1)}, bf16[8,4,128,128]{3,2,1,0:T(8,128)(2,1)S(1)}, bf16[4,64,1024]{2,1,0:T(8,128)(2,1)S(1)}, bf16[4,64,1024]{2,1,0:T(8,128)(2,1)S(1)}, bf16[4,64,64]{2,1,0:T(8,128)(2,1)S(1)}) custom-call(s32[2]{0:T(128)S(4)} %get-tuple-element.25.place_ref, s32[4,32]{1,0:T(4,128)S(4)} %get-tuple-element.27.list_ref, ...), custom_call_target="tpu_custom_call" | custom-call | tf_op jit(solution)/shard_map/prepare/pallas_call | solution.py:427
  14.7 0.0 collective-permute-done.inner_ref
  14.7 0.0 collective-permute-done.1.outer_ref
  14.7 0.4 edge.2.edge_ref
  15.2 5.9 %all-to-all-done = bf16[32,2,16,128]{3,2,1,0:T(8,128)(2,1)S(1)} async-done(((bf16[32,2,16,128]{3,2,1,0:T(8,128)(2,1)}), bf16[32,2,16,128]{3,2,1,0:T(8,128)(2,1)S(1)}, u32[]{:S(2)}, u32[]{:S(2)}) %all-to-all-start) | async-done | bytes 262176 | tf_op jit(solution)/shard_map/all_to_all | solution.py:355
  21.1 0.0 copy-done
  21.1 1.3 %second.1 = (bf16[32,2,16,128]{3,2,1,0:T(8,128)(2,1)}, f32[16,4096]{1,0:T(8,128)S(1)}, bf16[32,512]{1,0:T(8,128)(2,1)S(1)}, bf16[32,512]{1,0:T(8,128)(2,1)S(1)}) custom-call(s32[2]{0:T(128)S(4)} %get-tuple-element.25.place_ref, s32[4,16]{1,0:T(4,128)S(4)} %get-tuple-element.24.top_ref, bf16[64,16,128]{2,1,0:T(8,128)(2,1)S(1)} %bitcast.4, ...), custom_call_target="tpu_custom_call" | custom-call | tf_op jit(solution)/shard_map/second/pallas_call | solution.py:449
  22.4 2.6 %all-to-all-start.1 = ((bf16[32,2,16,128]{3,2,1,0:T(8,128)(2,1)}), bf16[32,2,16,128]{3,2,1,0:T(8,128)(2,1)S(1)}, u32[]{:S(2)}, u32[]{:S(2)}) async-start(bf16[32,2,16,128]{3,2,1,0:T(8,128)(2,1)} %get-tuple-element.37), calls=%async_computation.1 | async-start | bytes 524288 | tf_op jit(solution)/shard_map/all_to_all | solution.py:355
  25.0 0.2 collective-permute-start.2
  25.3 0.7 %collective-permute-start.3 = (bf16[32,512]{1,0:T(8,128)(2,1)S(1)}, bf16[32,512]{1,0:T(8,128)(2,1)S(1)}, u32[]{:S(2)}, u32[]{:S(2)}) collective-permute-start(bf16[32,512]{1,0:T(8,128)(2,1)S(1)} %get-tuple-element.42), channel_id=1, source_target_pairs={{1,2},{3,4},{5,6},{2,1},{4,3},{6,5},{9,10},{11,12},{13,14},{10,9},... | collective-permute-start | bytes 98312 | tf_op jit(solution)/shard_map/ppermute | solution.py:366
  25.9 2.9 %near.1 = (f32[16,4096]{1,0:T(8,128)S(1)}, bf16[8,4,128,128]{3,2,1,0:T(8,128)(2,1)S(1)}, f32[16,4096]{1,0:T(8,128)S(1)}) custom-call(s32[2]{0:T(128)S(4)} %get-tuple-element.25.place_ref, s32[4,32]{1,0:T(4,128)S(4)} %get-tuple-element.27.list_ref, f32[16,4096]{1,0:T(8,128)S(1)} %get-tuple-element.38.field_ref.image_ref, ...), custom_call_target="tpu_custom_call" | custom-call | tf_op jit(solution)/shard_map/near/pallas_call | solution.py:459
  28.8 0.0 collective-permute-done.2.inner_ref
  28.8 0.0 collective-permute-done.3.outer_ref
  28.8 0.4 edge.3.edge_ref
  29.2 6.2 %all-to-all-done.1 = bf16[32,2,16,128]{3,2,1,0:T(8,128)(2,1)S(1)} async-done(((bf16[32,2,16,128]{3,2,1,0:T(8,128)(2,1)}), bf16[32,2,16,128]{3,2,1,0:T(8,128)(2,1)S(1)}, u32[]{:S(2)}, u32[]{:S(2)}) %all-to-all-start.1) | async-done | bytes 262176 | tf_op jit(solution)/shard_map/all_to_all | solution.py:355
  35.4 0.6 %third.1 = (f32[16,4096]{1,0:T(8,128)S(1)}, f32[32,1,128]{2,1,0:T(1,128)S(1)}) custom-call(s32[4,16]{1,0:T(4,128)S(4)} %get-tuple-element.24.top_ref, bf16[64,16,128]{2,1,0:T(8,128)(2,1)S(1)} %bitcast.5, bf16[4,64,1024]{2,1,0:T(8,128)(2,1)S(1)} %get-tuple-element.30.smat_ref, bf16[4,64,1024]{2,1,0:T(8,128)(2,1)S(1)} %get-tuple-element.31.turned_ref, ...), custom_call_target="tpu_custom_call" | custom-call | tf_op jit(solution)/shard_map/third/pallas_call | solution.py:470
  36.0 9.4 %all_to_all.15.sums_ref = f32[32,1,128]{2,1,0:T(1,128)S(1)} all-to-all(f32[32,1,128]{2,1,0:T(1,128)S(1)} %get-tuple-element.44), channel_id=1, replica_groups=mesh['group'=4,'dev'=8] {'group','dev'}, dimensions={0} | all-to-all | bytes 32768 | tf_op jit(solution)/shard_map/all_to_all | solution.py:355
  45.4 1.1 %last.1 = (f32[16,4096]{1,0:T(8,128)}, f32[16,4096]{1,0:T(8,128)}) custom-call(f32[32,1,128]{2,1,0:T(1,128)S(1)} %all_to_all.15.sums_ref, f32[16,4096]{1,0:T(8,128)S(1)} %get-tuple-element.28.field_ref.start_ref, f32[16,4096]{1,0:T(8,128)S(1)} %get-tuple-element.38.field_ref.image_ref, f32[16,4096]{1,0:T(8,128)S(1)} %get-tuple-element.45.twice_ref), custom_call_target="tpu_custom_call" | custom-call | tf_op jit(solution)/shard_map/last/pallas_call | solution.py:480
Async XLA Ops:
  0.6 20.5 %copy-start = (f32[4096]{0:T(1024)S(1)}, f32[4096]{0:T(1024)}, u32[]{:S(2)}) copy-start(f32[4096]{0:T(1024)} %param.9) | copy-start | bytes 49156
  3.4 17.7 %all-to-all-start = ((bf16[32,2,16,128]{3,2,1,0:T(8,128)(2,1)}), bf16[32,2,16,128]{3,2,1,0:T(8,128)(2,1)S(1)}, u32[]{:S(2)}, u32[]{:S(2)}) async-start(bf16[32,2,16,128]{3,2,1,0:T(8,128)(2,1)} %get-tuple-element.26), calls=%async_computation | async-start | bytes 524288 | tf_op jit(solution)/shard_map/all_to_all | solution.py:355
  10.7 4.0 %collective-permute-start = (bf16[32,512]{1,0:T(8,128)(2,1)S(1)}, bf16[32,512]{1,0:T(8,128)(2,1)S(1)}, u32[]{:S(2)}, u32[]{:S(2)}) collective-permute-start(bf16[32,512]{1,0:T(8,128)(2,1)S(1)} %get-tuple-element.34), channel_id=1, source_target_pairs={{0,1},{1,0},{2,3},{3,2},{4,5},{5,4},{6,7},{7,6},{8,9},{9,8},{10,11... | collective-permute-start | bytes 98312 | tf_op jit(solution)/shard_map/ppermute | solution.py:359
  11.0 3.7 %collective-permute-start.1 = (bf16[32,512]{1,0:T(8,128)(2,1)S(1)}, bf16[32,512]{1,0:T(8,128)(2,1)S(1)}, u32[]{:S(2)}, u32[]{:S(2)}) collective-permute-start(bf16[32,512]{1,0:T(8,128)(2,1)S(1)} %get-tuple-element.35), channel_id=1, source_target_pairs={{1,2},{3,4},{5,6},{2,1},{4,3},{6,5},{9,10},{11,12},{13,14},{10,9},... | collective-permute-start | bytes 98312 | tf_op jit(solution)/shard_map/ppermute | solution.py:366
  22.4 13.0 %all-to-all-start.1 = ((bf16[32,2,16,128]{3,2,1,0:T(8,128)(2,1)}), bf16[32,2,16,128]{3,2,1,0:T(8,128)(2,1)S(1)}, u32[]{:S(2)}, u32[]{:S(2)}) async-start(bf16[32,2,16,128]{3,2,1,0:T(8,128)(2,1)} %get-tuple-element.37), calls=%async_computation.1 | async-start | bytes 524288 | tf_op jit(solution)/shard_map/all_to_all | solution.py:355
  25.0 3.8 %collective-permute-start.2 = (bf16[32,512]{1,0:T(8,128)(2,1)S(1)}, bf16[32,512]{1,0:T(8,128)(2,1)S(1)}, u32[]{:S(2)}, u32[]{:S(2)}) collective-permute-start(bf16[32,512]{1,0:T(8,128)(2,1)S(1)} %get-tuple-element.41), channel_id=1, source_target_pairs={{0,1},{1,0},{2,3},{3,2},{4,5},{5,4},{6,7},{7,6},{8,9},{9,8},{10,11... | collective-permute-start | bytes 98312 | tf_op jit(solution)/shard_map/ppermute | solution.py:359
  25.3 3.5 %collective-permute-start.3 = (bf16[32,512]{1,0:T(8,128)(2,1)S(1)}, bf16[32,512]{1,0:T(8,128)(2,1)S(1)}, u32[]{:S(2)}, u32[]{:S(2)}) collective-permute-start(bf16[32,512]{1,0:T(8,128)(2,1)S(1)} %get-tuple-element.42), channel_id=1, source_target_pairs={{1,2},{3,4},{5,6},{2,1},{4,3},{6,5},{9,10},{11,12},{13,14},{10,9},... | collective-permute-start | bytes 98312 | tf_op jit(solution)/shard_map/ppermute | solution.py:366
